TPU v7x, 128 devices: a whole 4x4x4 slice. The times are simulated.
128 devices in a mesh: view: 32 (over y, x, core), band: 4 (over z).
Axes of the slice: x: 4, y: 4, z: 4, core: 2. Of those that a mesh axis runs over, the one named last changes fastest.
Arguments:
- gaussians: float32 [2048, 62, 256], P(('view', 'band')), may hold values from -8 to 128, as said below
- first_moment: float32 [2048, 62, 256], P(('view', 'band')), may hold values from -0.6 to 0.6
- second_moment: float32 [2048, 62, 256], P(('view', 'band')), may hold values from 0.0001 to 0.1
- camera: float32 [32, 9], P('view'), may hold values from -352 to 352, as said below
- target: float32 [32, 3, 64, 128], P('view', None, 'band'), may hold values from 0 to 1
- block_list: int32 [32, 4, 16], P('view', 'band'), may hold values from -1 to 2047, as said below
- block_count: int32 [32, 4], P('view', 'band'), may hold values from 12 to 16, as said below
- tile_start: int32 [32, 4, 8], P('view', 'band'), may hold values from 0 to 15, as said below
- tile_end: int32 [32, 4, 8], P('view', 'band'), may hold values from 1 to 16, as said below
Outputs:
- new_gaussians: float32 [2048, 62, 256], P(('view', 'band'))
- new_first_moment: float32 [2048, 62, 256], P(('view', 'band'))
- new_second_moment: float32 [2048, 62, 256], P(('view', 'band'))
- mean_loss: float32 [], replicated
- grads: float32 [2048, 62, 256], P(('view', 'band'))
Inputs may be any that keep to these rules, and one draw needn't show every extreme that they name: Block k is held by device k // 16, devices counted with view slowest. Entry i of block_list[v, b] is a block for i < block_count[v, b] and -1 after; the live entries of one band are distinct, at most 1 of them are held by one device, and in every band some device holds exactly 1 of them. `block_count`: some band has exactly 16. tile_start < tile_end <= block_count of the band; tile_end - tile_start is at most 2, and exactly 2 for some tile of every band; the tiles of a band together cover every live position. `tile_end`: see tile_start. `gaussians`: component 9 of every Gaussian lies in [1, 2]; components 6 to 8 lie in [0, 2]. `camera`: A0 x A1 has a third entry of 0.6 or more.
All inputs are finite; a program needn't handle non-finite values.
Results may differ from a plain program's by a relative error of at most 0.0003.
Values sent between devices are 32-bit elements; how exact they have to be, the bound alone decides.
No kernel may reach another device: no remote copies, remote signals or barrier semaphores. Data moves between devices by JAX's collectives and lax.ppermute only.
A program may use at most 128 MiB of HBM per device.

v0:
```python
import math

import jax
import jax.numpy as jnp
import numpy as np
from jax import lax
from jax.experimental import pallas as pl
from jax.experimental.pallas import tpu as pltpu
from jax.sharding import PartitionSpec as P

TILE = 16
ROWS = 16
COLS = 128
TILES = 8
LIST = 16
BLOCK = 256
BLK_DEV = 16
DEVICES = 128
BANDS = 4
COMPS = 62
TILE_MOST = 2
GAUSS = TILE_MOST * BLOCK
HALO = 10
EXT = 40
RECORD = 9 * BLOCK
SLOT = RECORD + 128
ASK = 128
IMG_ROWS = BANDS * ROWS
AXES = ("view", "band")

HIGHEST_MODE = lax.Precision.HIGHEST
SSIM_WEIGHT = 0.2
ABS_WEIGHT = 0.8
STAB_MEAN = 0.0001
STAB_VAR = 0.0009
BIAS_FIRST = 1.0 - math.exp(100.0 * math.log(0.9))
BIAS_SECOND = 1.0 - math.exp(100.0 * math.log(0.999))
SH_ZERO = 0.28209479177387814
SH_ONE = 0.4886025119029199
SH_TWO = [
    1.0925484305920792,
    -1.0925484305920792,
    0.31539156525252005,
    -1.0925484305920792,
    0.5462742152960396,
]
SH_THREE = [
    -0.5900435899266435,
    2.890611442640554,
    -0.4570457994644658,
    0.3731763325901154,
    -0.4570457994644658,
    1.445305721320277,
    -0.5900435899266435,
]

W_ID = 0
W_CAM = 1
W_SH = 10
W_CA = 26
W_CB = 32
W_CC = 38

SMEM = pltpu.SMEM
VMEM = pltpu.VMEM


def spec(space):
    return pl.BlockSpec(memory_space=space)


def params(mib):
    return pltpu.CompilerParams(vmem_limit_bytes=mib * 1024 * 1024)


def kernel_taps():
    raw_taps = [math.exp(-(offset * offset) / 4.5) for offset in range(-5, 6)]
    tap_total = sum(raw_taps)
    return [raw_tap / tap_total for raw_tap in raw_taps]


def tap_matrices():
    taps = kernel_taps()
    first = np.zeros((32, EXT), np.float32)
    for r in range(ROWS + 10):
        for o in range(11):
            first[r, r + o] = taps[o]
    second = np.zeros((ROWS, 32), np.float32)
    for r in range(ROWS):
        for o in range(11):
            second[r, r + o] = taps[o]
    across = np.zeros((COLS, COLS), np.float32)
    for c in range(COLS):
        for o in range(11):
            if 0 <= c + o - 5 < COLS:
                across[c + o - 5, c] = taps[o]
    return first, second, across


def learning_rates():
    return np.concatenate(
        [
            np.full(6, 0.016),
            np.full(3, 0.005),
            np.full(4, 0.001),
            np.full(1, 0.05),
            np.full(3, 0.0025),
            np.full(45, 0.000125),
        ]
    ).astype(np.float32)


def harmonics(dir_x, dir_y, dir_z):
    sq_x, sq_y, sq_z = (dir_x * dir_x, dir_y * dir_y, dir_z * dir_z)
    return [
        SH_ZERO + 0.0 * dir_x,
        -SH_ONE * dir_y,
        SH_ONE * dir_z,
        -SH_ONE * dir_x,
        SH_TWO[0] * dir_x * dir_y,
        SH_TWO[1] * dir_y * dir_z,
        SH_TWO[2] * (2.0 * sq_z - sq_x - sq_y),
        SH_TWO[3] * dir_x * dir_z,
        SH_TWO[4] * (sq_x - sq_y),
        SH_THREE[0] * dir_y * (3.0 * sq_x - sq_y),
        SH_THREE[1] * dir_x * dir_y * dir_z,
        SH_THREE[2] * dir_y * (4.0 * sq_z - sq_x - sq_y),
        SH_THREE[3] * dir_z * (2.0 * sq_z - 3.0 * sq_x - 3.0 * sq_y),
        SH_THREE[4] * dir_x * (4.0 * sq_z - sq_x - sq_y),
        SH_THREE[5] * dir_z * (sq_x - sq_y),
        SH_THREE[6] * dir_x * (sq_x - 3.0 * sq_y),
    ]


def request_kernel(list_ref, count_ref, cam_ref, out_ref):
    cam = [jnp.full((1, ASK), cam_ref[0, i], jnp.float32) for i in range(9)]
    a, b = cam[0:3], cam[3:6]
    normal = [
        a[1] * b[2] - a[2] * b[1],
        a[2] * b[0] - a[0] * b[2],
        a[0] * b[1] - a[1] * b[0],
    ]
    size = jnp.sqrt(normal[0] * normal[0] + normal[1] * normal[1] + normal[2] * normal[2])
    basis = harmonics(normal[0] / size, normal[1] / size, normal[2] / size)
    pairs = [(0, 0), (0, 1), (0, 2), (1, 1), (1, 2), (2, 2)]

    def product(p, q):
        return [p[i] * q[i] if i == j else p[i] * q[j] + p[j] * q[i] for i, j in pairs]

    words = [jnp.full((1, ASK), -1.0, jnp.float32)] + cam + basis
    words = words + product(a, a) + product(a, b) + product(b, b)
    lane = lax.broadcasted_iota(jnp.int32, (1, ASK), 1)
    row = jnp.zeros((1, ASK), jnp.float32)
    for i, word in enumerate(words):
        row = jnp.where(lane == i, word, row)

    def fill(s, carry):
        out_ref[s] = row
        return carry

    lax.fori_loop(0, DEVICES, fill, 0, unroll=8)
    for i in range(LIST):

        @pl.when(i < count_ref[0, 0])
        def _(i=i):
            block = list_ref[0, 0, i]
            local = jnp.full((1, ASK), block % BLK_DEV, jnp.int32).astype(jnp.float32)
            out_ref[block // BLK_DEV] = jnp.where(lane == 0, local, row)


def shape_terms(g_ref):
    squares = [jnp.exp(2.0 * g_ref[:, 6 + c, :]) for c in range(3)]
    quat = [g_ref[:, 9 + c, :] for c in range(4)]
    size = jnp.sqrt(quat[0] * quat[0] + quat[1] * quat[1] + quat[2] * quat[2] + quat[3] * quat[3])
    r, x, y, z = [q / size for q in quat]
    rotation = [
        [1.0 - 2.0 * (y * y + z * z), 2.0 * (x * y - r * z), 2.0 * (x * z + r * y)],
        [2.0 * (x * y + r * z), 1.0 - 2.0 * (x * x + z * z), 2.0 * (y * z - r * x)],
        [2.0 * (x * z - r * y), 2.0 * (y * z + r * x), 1.0 - 2.0 * (x * x + y * y)],
    ]
    return squares, rotation, (r, x, y, z), size


def records_kernel(ask_ref, g_ref, out_ref, shape_ref):
    squares, rot, unused, unused_size = shape_terms(g_ref)
    at = 0
    for i in range(3):
        for j in range(i, 3):
            shape_ref[at] = (
                rot[i][0] * rot[j][0] * squares[0]
                + rot[i][1] * rot[j][1] * squares[1]
                + rot[i][2] * rot[j][2] * squares[2]
            )
            at += 1
    shape_ref[6] = 1.0 / (1.0 + jnp.exp(-g_ref[:, 13, :]))

    def slot(s, carry):
        local = ask_ref[s, 0, W_ID]

        @pl.when(local >= 0.0)
        def _():
            k = local.astype(jnp.int32)

            def word(i):
                return ask_ref[s, 0, i]

            def comp(i):
                return g_ref[k, pl.ds(i, 1), :]

            def put(p, value):
                out_ref[s, :, pl.ds(p * BLOCK, BLOCK)] = value

            time = word(W_CAM + 8)
            centre = [comp(c) + time * comp(3 + c) for c in range(3)]
            for p in range(2):
                put(
                    p,
                    word(W_CAM + 3 * p) * centre[0]
                    + word(W_CAM + 3 * p + 1) * centre[1]
                    + word(W_CAM + 3 * p + 2) * centre[2]
                    + word(W_CAM + 6 + p),
                )
            shapes = [shape_ref[i, pl.ds(k, 1), :] for i in range(6)]
            for p, (at, extra) in enumerate(((W_CA, 0.3), (W_CB, 0.0), (W_CC, 0.3))):
                total = word(at) * shapes[0]
                for i in range(1, 6):
                    total = total + word(at + i) * shapes[i]
                put(2 + p, total + extra)
            put(5, shape_ref[6, pl.ds(k, 1), :])
            colour = word(W_SH) * g_ref[k, pl.ds(14, 3), :]
            for q in range(1, 16):
                colour = colour + word(W_SH + q) * g_ref[k, pl.ds(14 + 3 * q, 3), :]
            colour = colour + 0.5
            for ch in range(3):
                put(6 + ch, colour[ch : ch + 1])

        return carry

    lax.fori_loop(0, DEVICES, slot, 0)


def pixel_rows(row_base):
    px = lax.broadcasted_iota(jnp.int32, (ROWS, COLS), 1).astype(jnp.float32) + 0.5
    py = lax.broadcasted_iota(jnp.int32, (ROWS, COLS), 0).astype(jnp.float32) + 0.5
    return px, py + row_base.astype(jnp.float32)


def row_of(ref, p, i):
    return jnp.broadcast_to(ref[p, pl.ds(i, 1), :], (ROWS, COLS))


def alpha_of(table, i, px, py):
    dx = px - row_of(table, 0, i)
    dy = py - row_of(table, 1, i)
    power = row_of(table, 2, i) * dx * dx + dy * (
        row_of(table, 3, i) * dx + row_of(table, 4, i) * dy
    )
    return row_of(table, 5, i) * jnp.exp(power)


def render_kernel(
    list_ref, start_ref, end_ref, base_ref, got_ref, pred_ref, compact_ref, table_ref
):
    for t in range(TILES):
        first = start_ref[0, 0, t]
        last = end_ref[0, 0, t]
        for j in range(TILE_MOST):
            live = first + j < last
            place = jnp.where(live, first + j, first)
            owner = list_ref[0, 0, place] // BLK_DEV
            there = jnp.where(live, 1.0, 0.0)
            for p in range(9):
                row = got_ref[owner, :, pl.ds(p * BLOCK, BLOCK)]
                if p == 5:
                    row = row * there
                compact_ref[p, pl.ds(t, 1), pl.ds(j * BLOCK, BLOCK)] = row
    ca, cb, cc = compact_ref[2], compact_ref[3], compact_ref[4]
    det = ca * cc - cb * cb
    forms = [
        compact_ref[0],
        compact_ref[1],
        -0.5 * cc / det,
        cb / det,
        -0.5 * ca / det,
        compact_ref[5],
        compact_ref[6],
        compact_ref[7],
        compact_ref[8],
    ]
    for p, form in enumerate(forms):
        wide = jnp.broadcast_to(form[:, None, :], (TILES, TILE, GAUSS)).reshape(COLS, GAUSS)
        table_ref[p] = wide.T
    px, py = pixel_rows(base_ref[0])

    def blend(i, carry):
        trans, red, green, blue = carry
        weight = alpha_of(table_ref, i, px, py) * trans
        return (
            trans - weight,
            red + weight * row_of(table_ref, 6, i),
            green + weight * row_of(table_ref, 7, i),
            blue + weight * row_of(table_ref, 8, i),
        )

    zero = jnp.zeros((ROWS, COLS), jnp.float32)
    done = lax.fori_loop(0, GAUSS, blend, (zero + 1.0, zero, zero, zero), unroll=8)
    for ch in range(3):
        pred_ref[ch] = done[1 + ch]


def ssim_value(mean_x, mean_y, square_x, square_y, cross_xy):
    var_x = square_x - mean_x * mean_x
    var_y = square_y - mean_y * mean_y
    covar = cross_xy - mean_x * mean_y
    upper = (2.0 * mean_x * mean_y + STAB_MEAN) * (2.0 * covar + STAB_VAR)
    lower = (mean_x * mean_x + mean_y * mean_y + STAB_MEAN) * (var_x + var_y + STAB_VAR)
    return upper / lower


def exact_dot(a, b):
    return jnp.dot(a, b, precision=HIGHEST_MODE, preferred_element_type=jnp.float32)


def loss_gradient(
    base, pred_ref, target_ref, before_ref, after_ref, first_ref, second_ref, across_ref, ext_ref
):
    ext_ref[...] = jnp.zeros(ext_ref.shape, jnp.float32)
    for part, mine in enumerate((pred_ref, target_ref)):
        for ch in range(3):
            ext_ref[part, ch, pl.ds(0, HALO), :] = before_ref[part, ch]
            ext_ref[part, ch, pl.ds(HALO, ROWS), :] = mine[ch]
            ext_ref[part, ch, pl.ds(HALO + ROWS, HALO), :] = after_ref[part, ch]
    first, second, across = first_ref[...], second_ref[...], across_ref[...]
    row = lax.broadcasted_iota(jnp.int32, (32, COLS), 0)
    image_row = row + base - 5
    inside = (image_row >= 0) & (image_row < IMG_ROWS) & (row < ROWS + 10)
    total = jnp.zeros((ROWS, COLS), jnp.float32)
    slopes = []
    for ch in range(3):
        x, y = ext_ref[0, ch], ext_ref[1, ch]
        maps = jnp.concatenate([x, y, x * x, y * y, x * y], axis=0)
        maps = exact_dot(maps, across)
        smooth = [exact_dot(first, maps[EXT * m : EXT * (m + 1)]) for m in range(5)]
        value, pullback = jax.vjp(ssim_value, *smooth)
        parts = pullback(jnp.full_like(value, -SSIM_WEIGHT / 3.0))
        adjoint = [jnp.where(inside, parts[m], 0.0) for m in (0, 2, 4)]
        back = [exact_dot(second, part) for part in adjoint]
        back = exact_dot(jnp.concatenate(back, axis=0), across)
        pred, target = pred_ref[ch], target_ref[ch]
        error = pred - target
        sign = jnp.where(error > 0.0, 1.0, jnp.where(error < 0.0, -1.0, 0.0))
        slopes.append(
            ABS_WEIGHT / 3.0 * sign
            + back[0:ROWS]
            + 2.0 * pred * back[ROWS : 2 * ROWS]
            + target * back[2 * ROWS : 3 * ROWS]
        )
        total = total + (
            ABS_WEIGHT / 3.0 * jnp.abs(error)
            + SSIM_WEIGHT / 3.0 * (1.0 - value[5 : 5 + ROWS])
        )
    total = jnp.sum(jnp.sum(total, axis=1, keepdims=True), axis=0, keepdims=True)
    return total, slopes


def backward_kernel(
    list_ref,
    start_ref,
    end_ref,
    base_ref,
    pred_ref,
    target_ref,
    before_ref,
    after_ref,
    first_ref,
    second_ref,
    across_ref,
    seg_ref,
    compact_ref,
    table_ref,
    out_ref,
    ext_ref,
    alpha_ref,
    trans_ref,
    part_ref,
    moment_ref,
    grad_ref,
):
    total, slopes = loss_gradient(
        base_ref[0],
        pred_ref,
        target_ref,
        before_ref,
        after_ref,
        first_ref,
        second_ref,
        across_ref,
        ext_ref,
    )
    loss_row = jnp.broadcast_to(total, (1, 128))
    empty = jnp.zeros((1, RECORD), jnp.float32)

    def clear(s, carry):
        out_ref[s, :, pl.ds(RECORD, 128)] = loss_row
        out_ref[s, :, pl.ds(0, RECORD)] = empty
        return carry

    lax.fori_loop(0, DEVICES, clear, 0, unroll=4)
    px, py = pixel_rows(base_ref[0])

    def forward(i, trans):
        alpha = alpha_of(table_ref, i, px, py)
        alpha_ref[i] = alpha
        trans_ref[i] = trans
        return trans - alpha * trans

    one = jnp.ones((ROWS, COLS), jnp.float32)
    lax.fori_loop(0, GAUSS, forward, one, unroll=8)
    py_top, py_low = py[0:8], py[8:16]

    def fold(value):
        return value[0:8] + value[8:16]

    def reverse(step, behind):
        chunk = GAUSS // 8 - 1 - step
        for r in range(7, -1, -1):
            i = chunk * 8 + r
            alpha = alpha_ref[i]
            trans = trans_ref[i]
            weight = alpha * trans
            seen = (
                row_of(table_ref, 6, i) * slopes[0]
                + row_of(table_ref, 7, i) * slopes[1]
                + row_of(table_ref, 8, i) * slopes[2]
            )
            ahead = seen - behind
            behind = behind + alpha * ahead
            d_power = weight * ahead
            dy = py - row_of(table_ref, 1, i)
            d_row = d_power * dy
            part_ref[0, pl.ds(8 * r, 8), :] = fold(d_power)
            part_ref[1, pl.ds(8 * r, 8), :] = fold(d_row)
            part_ref[2, pl.ds(8 * r, 8), :] = fold(d_row * dy)
            for ch in range(3):
                part_ref[3 + ch, pl.ds(8 * r, 8), :] = fold(weight * slopes[ch])
        sums = []
        for p in range(6):
            piece = part_ref[p, pl.ds(0, 8, stride=8), :]
            for s in range(1, 8):
                piece = piece + part_ref[p, pl.ds(s, 8, stride=8), :]
            sums.append(piece)
        here = pl.ds(pl.multiple_of(chunk * 8, 8), 8)
        dx = px[0:8] - table_ref[0, here, :]
        first_x = sums[0] * dx
        moment_ref[0, here, :] = sums[0]
        moment_ref[1, here, :] = first_x
        moment_ref[2, here, :] = first_x * dx
        moment_ref[3, here, :] = sums[1]
        moment_ref[4, here, :] = sums[1] * dx
        moment_ref[5, here, :] = sums[2]
        for ch in range(3):
            moment_ref[6 + ch, here, :] = sums[3 + ch]
        return behind

    lax.fori_loop(0, GAUSS // 8, reverse, jnp.zeros((ROWS, COLS), jnp.float32))
    seg = seg_ref[...]
    m = [
        lax.dot_general(
            seg,
            moment_ref[p],
            (((1,), (1,)), ((), ())),
            precision=HIGHEST_MODE,
            preferred_element_type=jnp.float32,
        )
        for p in range(9)
    ]
    ca, cb, cc = compact_ref[2], compact_ref[3], compact_ref[4]
    inverse = 1.0 / (ca * cc - cb * cb)
    d_inverse = -0.5 * cc * m[2] + cb * m[4] - 0.5 * ca * m[5]
    d_det = -inverse * inverse * d_inverse
    grad_ref[0] = (cc * m[1] - cb * m[3]) * inverse
    grad_ref[1] = (ca * m[3] - cb * m[1]) * inverse
    grad_ref[2] = -0.5 * inverse * m[5] + cc * d_det
    grad_ref[3] = inverse * m[4] - 2.0 * cb * d_det
    grad_ref[4] = -0.5 * inverse * m[2] + ca * d_det
    grad_ref[5] = m[0]
    for ch in range(3):
        grad_ref[6 + ch] = m[6 + ch]
    for t in range(TILES):
        first = start_ref[0, 0, t]
        for j in range(TILE_MOST):

            @pl.when(first + j < end_ref[0, 0, t])
            def _(t=t, j=j, first=first):
                owner = list_ref[0, 0, first + j] // BLK_DEV
                for p in range(9):
                    lanes = pl.ds(p * BLOCK, BLOCK)
                    out_ref[owner, :, lanes] = (
                        out_ref[owner, :, lanes]
                        + grad_ref[p, pl.ds(t, 1), pl.ds(j * BLOCK, BLOCK)]
                    )


def pullback_kernel(ask_ref, g_ref, got_ref, grad_ref, loss_ref, shape_ref):
    losses = got_ref[:, :, pl.ds(RECORD, 128)]
    loss_ref[...] = jnp.sum(losses, axis=0) * (1.0 / (DEVICES * ROWS * COLS))
    grad_ref[...] = jnp.zeros(grad_ref.shape, jnp.float32)
    shape_ref[...] = jnp.zeros(shape_ref.shape, jnp.float32)

    def slot(s, carry):
        local = ask_ref[s, 0, W_ID]

        @pl.when(local >= 0.0)
        def _():
            k = local.astype(jnp.int32)

            def word(i):
                return ask_ref[s, 0, i]

            d = [got_ref[s, :, pl.ds(p * BLOCK, BLOCK)] for p in range(9)]
            time = word(W_CAM + 8)
            for c in range(3):
                d_centre = word(W_CAM + c) * d[0] + word(W_CAM + 3 + c) * d[1]
                grad_ref[k, pl.ds(c, 1), :] = grad_ref[k, pl.ds(c, 1), :] + d_centre
                grad_ref[k, pl.ds(3 + c, 1), :] = grad_ref[k, pl.ds(3 + c, 1), :] + time * d_centre
            here = pl.ds(k, 1)
            for i in range(6):
                shape_ref[i, here, :] = shape_ref[i, here, :] + (
                    word(W_CA + i) * d[2] + word(W_CB + i) * d[3] + word(W_CC + i) * d[4]
                )
            shape_ref[6, here, :] = shape_ref[6, here, :] + d[5]
            colour = jnp.concatenate(d[6:9], axis=0)
            for q in range(16):
                at = pl.ds(14 + 3 * q, 3)
                grad_ref[k, at, :] = grad_ref[k, at, :] + word(W_SH + q) * colour

        return carry

    lax.fori_loop(0, DEVICES, slot, 0)
    squares, rot, quat, size = shape_terms(g_ref)
    s00, s01, s02, s11, s12, s22 = [shape_ref[i] for i in range(6)]
    twice = [[2.0 * s00, s01, s02], [s01, 2.0 * s11, s12], [s02, s12, 2.0 * s22]]
    d_rot = [[None] * 3 for _ in range(3)]
    for c in range(3):
        pulled = [
            twice[i][0] * rot[0][c] + twice[i][1] * rot[1][c] + twice[i][2] * rot[2][c]
            for i in range(3)
        ]
        along = rot[0][c] * pulled[0] + rot[1][c] * pulled[1] + rot[2][c] * pulled[2]
        grad_ref[:, 6 + c, :] = squares[c] * along
        for i in range(3):
            d_rot[i][c] = pulled[i] * squares[c]
    r, x, y, z = quat
    n = d_rot
    d_r = 2.0 * (
        -z * n[0][1] + y * n[0][2] + z * n[1][0] - x * n[1][2] - y * n[2][0] + x * n[2][1]
    )
    d_x = 2.0 * (
        y * n[0][1] + z * n[0][2] + y * n[1][0] - 2.0 * x * n[1][1] - r * n[1][2]
        + z * n[2][0] + r * n[2][1] - 2.0 * x * n[2][2]
    )
    d_y = 2.0 * (
        -2.0 * y * n[0][0] + x * n[0][1] + r * n[0][2] + x * n[1][0] + z * n[1][2]
        - r * n[2][0] + z * n[2][1] - 2.0 * y * n[2][2]
    )
    d_z = 2.0 * (
        -2.0 * z * n[0][0] - r * n[0][1] + x * n[0][2] + r * n[1][0] - 2.0 * z * n[1][1]
        + y * n[1][2] + x * n[2][0] + y * n[2][1]
    )
    d_quat = [d_r, d_x, d_y, d_z]
    along = r * d_r + x * d_x + y * d_y + z * d_z
    for c in range(4):
        grad_ref[:, 9 + c, :] = (d_quat[c] - quat[c] * along) / size
    opacity = 1.0 / (1.0 + jnp.exp(-g_ref[:, 13, :]))
    grad_ref[:, 13, :] = shape_ref[6] * (1.0 - opacity)


def adam_update(gaussians, moment_one, moment_two, gradient):
    learn_rates = jnp.asarray(learning_rates())[None, :, None]
    new_one = 0.9 * moment_one + 0.1 * gradient
    new_two = 0.999 * moment_two + 0.001 * gradient * gradient
    change = learn_rates * (new_one / BIAS_FIRST) / (jnp.sqrt(new_two / BIAS_SECOND) + 1e-08)
    return (gaussians - change, new_one, new_two)


def shaped(*shape):
    return jax.ShapeDtypeStruct(shape, jnp.float32)


def exchanged(slots):
    return lax.all_to_all(slots, AXES, split_axis=0, concat_axis=0, tiled=True)


def halo(array):
    up = [(i, i + 1) for i in range(BANDS - 1)]
    down = [(i + 1, i) for i in range(BANDS - 1)]
    before = lax.ppermute(array[:, ROWS - HALO :], "band", up)
    after = lax.ppermute(array[:, :HALO], "band", down)
    return before, after


def per_device(
    gaussians,
    first_moment,
    second_moment,
    camera,
    target,
    block_list,
    block_count,
    tile_start,
    tile_end,
):
    base = (lax.axis_index("band") * ROWS).astype(jnp.int32).reshape(1)
    request = pl.pallas_call(
        request_kernel,
        in_specs=[spec(SMEM)] * 3,
        out_specs=spec(VMEM),
        out_shape=shaped(DEVICES, 1, ASK),
        name="request",
    )(block_list, block_count, camera)
    asked = exchanged(request)
    target_band = target[0]
    target_before, target_after = halo(target_band)
    records = pl.pallas_call(
        records_kernel,
        in_specs=[spec(SMEM), spec(VMEM)],
        out_specs=spec(VMEM),
        out_shape=shaped(DEVICES, 1, RECORD),
        scratch_shapes=[VMEM((7, BLK_DEV, BLOCK), jnp.float32)],
        compiler_params=params(32),
        name="records",
    )(asked, gaussians)
    received = exchanged(records)
    pred, compact, table = pl.pallas_call(
        render_kernel,
        in_specs=[spec(SMEM)] * 4 + [spec(VMEM)],
        out_specs=[spec(VMEM)] * 3,
        out_shape=[
            shaped(3, ROWS, COLS),
            shaped(9, TILES, GAUSS),
            shaped(9, GAUSS, COLS),
        ],
        compiler_params=params(32),
        name="render",
    )(block_list, tile_start, tile_end, base, received)
    pred_before, pred_after = halo(pred)
    first, second, across = tap_matrices()
    seg = (np.arange(COLS)[None, :] // TILE == np.arange(TILES)[:, None]).astype(np.float32)
    outgoing = pl.pallas_call(
        backward_kernel,
        in_specs=[spec(SMEM)] * 4 + [spec(VMEM)] * 10,
        out_specs=spec(VMEM),
        out_shape=shaped(DEVICES, 1, SLOT),
        scratch_shapes=[
            VMEM((2, 3, EXT, COLS), jnp.float32),
            VMEM((GAUSS, ROWS, COLS), jnp.float32),
            VMEM((GAUSS, ROWS, COLS), jnp.float32),
            VMEM((6, 64, COLS), jnp.float32),
            VMEM((9, GAUSS, COLS), jnp.float32),
            VMEM((9, TILES, GAUSS), jnp.float32),
        ],
        compiler_params=params(48),
        name="backward",
    )(
        block_list,
        tile_start,
        tile_end,
        base,
        pred,
        target_band,
        jnp.stack([pred_before, target_before]),
        jnp.stack([pred_after, target_after]),
        first,
        second,
        across,
        seg,
        compact,
        table,
    )
    incoming = exchanged(outgoing)
    gradient, loss = pl.pallas_call(
        pullback_kernel,
        in_specs=[spec(SMEM)] + [spec(VMEM)] * 2,
        out_specs=[spec(VMEM)] * 2,
        out_shape=[shaped(BLK_DEV, COMPS, BLOCK), shaped(1, 128)],
        scratch_shapes=[VMEM((7, BLK_DEV, BLOCK), jnp.float32)],
        compiler_params=params(32),
        name="pullback",
    )(asked, gaussians, incoming)
    new_params, new_one, new_two = adam_update(gaussians, first_moment, second_moment, gradient)
    return (new_params, new_one, new_two, loss[0, 0], gradient)


def solution(mesh):
    return jax.shard_map(
        per_device,
        mesh=mesh,
        in_specs=(
            P(AXES, None, None),
            P(AXES, None, None),
            P(AXES, None, None),
            P("view", None),
            P("view", None, "band", None),
            P("view", "band", None),
            P("view", "band"),
            P("view", "band", None),
            P("view", "band", None),
        ),
        out_specs=(
            P(AXES, None, None),
            P(AXES, None, None),
            P(AXES, None, None),
            P(),
            P(AXES, None, None),
        ),
        check_vma=False,
    )
```

profile of v0, /device:TPU:1, one launch (start us, length us, event | category | flops | bytes accessed | tf_op | source)
XLA Modules:
  0.0 121.8 jit_solution(1129706356434014780)
XLA Ops:
  1.3 1.7 %request.1 = f32[128,1,128]{2,1,0:T(1,128)} custom-call(s32[1,1,16]{2,1,0:T(1,128)} %list_ref.5, s32[1,1]{1,0:T(1,128)S(6)} %copy.37.count_ref, f32[1,9]{1,0:T(1,128)} %cam_ref.1), custom_call_target="tpu_custom_call" | custom-call | tf_op jit(solution)/shard_map/request/pallas_call | solution.py:614
  3.0 11.5 %all-to-all-start = ((f32[128,1,128]{2,1,0:T(1,128)}), f32[128,1,128]{2,1,0:T(1,128)S(1)}, u32[]{:S(2)}, u32[]{:S(2)}) async-start(f32[128,1,128]{2,1,0:T(1,128)} %request.1), calls=%async_computation | async-start | bytes 131072 | tf_op jit(solution)/shard_map/all_to_all | solution.py:591
  14.4 1.8 %copy.23.g_ref = f32[16,62,256]{2,1,0:T(8,128)S(1)} copy(f32[16,62,256]{2,0,1:T(8,128)} %param.14) | data formatting | bytes 2031616 | tf_op args[0]
  16.3 7.8 %all-to-all-done.ask_ref = f32[128,1,128]{2,1,0:T(1,128)S(1)} async-done(((f32[128,1,128]{2,1,0:T(1,128)}), f32[128,1,128]{2,1,0:T(1,128)S(1)}, u32[]{:S(2)}, u32[]{:S(2)}) %all-to-all-start) | async-done | bytes 65568 | tf_op jit(solution)/shard_map/all_to_all | solution.py:591
  24.0 5.6 %records.1 = f32[128,1,2304]{2,1,0:T(1,128)} custom-call(f32[128,1,128]{2,1,0:T(1,128)S(1)} %all-to-all-done.ask_ref, f32[16,62,256]{2,1,0:T(8,128)S(1)} %copy.23.g_ref), custom_call_target="tpu_custom_call" | custom-call | tf_op jit(solution)/shard_map/records/pallas_call | solution.py:624
  29.6 0.0 copy-start
  29.6 0.0 copy-start.4
  29.6 0.0 copy-start.6
  29.6 0.0 copy-start.7
  29.6 4.4 %all-to-all-start.1 = ((f32[128,1,2304]{2,1,0:T(1,128)}), f32[128,1,2304]{2,1,0:T(1,128)S(1)}, u32[]{:S(2)}, u32[]{:S(2)}) async-start(f32[128,1,2304]{2,1,0:T(1,128)} %records.1), calls=%async_computation.1 | async-start | bytes 2359296 | tf_op jit(solution)/shard_map/all_to_all | solution.py:591
  34.0 0.0 copy-start.1
  34.0 0.0 copy-start.2
  34.0 0.0 copy-start.3
  34.0 0.0 copy-start.5
  34.1 0.0 copy-done
  34.1 1.3 %collective-permute-start.3 = (f32[3,10,128]{2,1,0:T(8,128)S(1)}, f32[3,10,128]{2,1,0:T(8,128)S(1)}, u32[]{:S(2)}, u32[]{:S(2)}) collective-permute-start(f32[3,10,128]{2,1,0:T(8,128)S(1)} %get-tuple-element.25), channel_id=1, source_target_pairs={{1,0},{2,1},{3,2},{5,4},{6,5},{7,6},{9,8},{10,9},{11,10},{13,12},{... | collective-permute-start | bytes 46088 | tf_op jit(solution)/shard_map/ppermute | solution.py:598
  35.4 19.4 %all-to-all-done.1.got_ref = f32[128,1,2304]{2,1,0:T(1,128)S(1)} async-done(((f32[128,1,2304]{2,1,0:T(1,128)}), f32[128,1,2304]{2,1,0:T(1,128)S(1)}, u32[]{:S(2)}, u32[]{:S(2)}) %all-to-all-start.1) | async-done | bytes 1179680 | tf_op jit(solution)/shard_map/all_to_all | solution.py:591
  54.8 0.0 copy-done.4
  54.8 0.0 copy-done.6
  54.8 0.0 copy-done.7
  54.8 4.4 %render.1 = (f32[3,16,128]{2,1,0:T(8,128)S(1)}, f32[9,8,512]{2,1,0:T(8,128)S(1)}, f32[9,512,128]{2,1,0:T(8,128)S(1)}) custom-call(s32[1,1,16]{2,1,0:T(1,128)S(1)} %copy-done.4, s32[1,1,8]{2,1,0:T(1,128)S(1)} %copy-done.6, s32[1,1,8]{2,1,0:T(1,128)S(1)} %copy-done.7, s32[1]{0:T(128)} %bitcast.base_ref, f32[128,1,2304]{2,1,0:T(1,128)S(1)} %all-to-all-done.1.got_ref), custom_call_target="tpu_custom_call" | custom-call | tf_op jit(solution)/shard_map/render/pallas_call | solution.py:634
  59.2 1.3 %collective-permute-start.2 = (f32[3,10,128]{2,1,0:T(8,128)S(1)}, f32[3,10,128]{2,1,0:T(8,128)S(1)}, u32[]{:S(2)}, u32[]{:S(2)}) collective-permute-start(f32[3,10,128]{2,1,0:T(8,128)S(1)} %get-tuple-element.23), channel_id=1, source_target_pairs={{1,0},{2,1},{3,2},{5,4},{6,5},{7,6},{9,8},{10,9},{11,10},{13,12},{... | collective-permute-start | bytes 46088 | tf_op jit(solution)/shard_map/ppermute | solution.py:598
  60.5 4.0 %collective-permute-start.1 = (f32[3,10,128]{2,1,0:T(8,128)S(1)}, f32[3,10,128]{2,1,0:T(8,128)S(1)}, u32[]{:S(2)}, u32[]{:S(2)}) collective-permute-start(f32[3,10,128]{2,1,0:T(8,128)S(1)} %get-tuple-element.26), channel_id=1, source_target_pairs={{0,1},{1,2},{2,3},{4,5},{5,6},{6,7},{8,9},{9,10},{10,11},{12,13},{... | collective-permute-start | bytes 46088 | tf_op jit(solution)/shard_map/ppermute | solution.py:597
  64.5 2.5 %collective-permute-start = (f32[3,10,128]{2,1,0:T(8,128)S(1)}, f32[3,10,128]{2,1,0:T(8,128)S(1)}, u32[]{:S(2)}, u32[]{:S(2)}) collective-permute-start(f32[3,10,128]{2,1,0:T(8,128)S(1)} %get-tuple-element.24), channel_id=1, source_target_pairs={{0,1},{1,2},{2,3},{4,5},{5,6},{6,7},{8,9},{9,10},{10,11},{12,13},{... | collective-permute-start | bytes 46088 | tf_op jit(solution)/shard_map/ppermute | solution.py:597
  67.0 0.0 collective-permute-done.3
  67.0 0.0 collective-permute-done.2
  67.0 0.0 collective-permute-done.1
  67.0 0.9 collective-permute-done
  67.9 0.0 copy-done.1
  67.9 0.0 copy-done.2
  68.0 0.0 copy-done.3
  68.0 0.0 copy-done.5
  68.0 12.6 %backward.1 = f32[128,1,2432]{2,1,0:T(1,128)S(1)} custom-call(s32[1,1,16]{2,1,0:T(1,128)S(1)} %copy-done.4, s32[1,1,8]{2,1,0:T(1,128)S(1)} %copy-done.6, s32[1,1,8]{2,1,0:T(1,128)S(1)} %copy-done.7, s32[1]{0:T(128)} %bitcast.base_ref, f32[3,16,128]{2,1,0:T(8,128)S(1)} %get-tuple-element.10.pred_ref, f32[3,16,128]{2,1,0:T(8,128)S(1)} %bitcast.9, ...), custom_call_target="tpu_custom_call" | custom-call | tf_op jit(solution)/shard_map/backward/pallas_call | solution.py:649
  80.6 28.2 %all_to_all.15.got_ref = f32[128,1,2432]{2,1,0:T(1,128)S(1)} all-to-all(f32[128,1,2432]{2,1,0:T(1,128)S(1)} %backward.1), channel_id=1, replica_groups=mesh['view'=32,'band'=4] {'view','band'}, dimensions={0} | all-to-all | bytes 2490368 | tf_op jit(solution)/shard_map/all_to_all | solution.py:591
  108.8 0.0 copy-start.10
  108.8 4.7 %pullback.1 = (f32[16,62,256]{2,1,0:T(8,128)S(1)}, f32[1,128]{1,0:T(1,128)}) custom-call(f32[128,1,128]{2,1,0:T(1,128)S(1)} %all-to-all-done.ask_ref, f32[16,62,256]{2,1,0:T(8,128)S(1)} %copy.23.g_ref, f32[128,1,2432]{2,1,0:T(1,128)S(1)} %all_to_all.15.got_ref), custom_call_target="tpu_custom_call" | custom-call | tf_op jit(solution)/shard_map/pullback/pallas_call | solution.py:681
  113.5 0.0 copy-start.8
  113.5 0.0 copy-start.9
  113.5 0.0 copy-start.11
  113.5 1.5 %copy.27 = f32[16,62,256]{2,0,1:T(8,128)} copy(f32[16,62,256]{2,1,0:T(8,128)S(1)} %get-tuple-element.19) | data formatting | bytes 2031616
  115.0 0.0 copy-done.10
  115.0 0.0 copy-done.8
  115.0 0.0 copy-done.9
  115.0 0.0 copy-done.11
  115.0 2.1 %divide_subtract_fusion = (f32[16,62,256]{2,1,0:T(8,128)S(1)}, f32[16,62,256]{2,1,0:T(8,128)S(1)}, f32[16,62,256]{2,1,0:T(8,128)S(1)}) fusion(f32[62]{0:T(128)S(1)} %copy-done.11, f32[16,62,256]{2,0,1:T(8,128)S(1)} %copy-done.8, f32[16,62,256]{2,1,0:T(8,128)S(1)} %get-tuple-element.19, f32[16,62,256]{2,0,1:T(8,128)S(1)} %copy-done.9, ...), kind=kLoop, calls=%fused_computation.5 | loop fusion | flops 3047424 | bytes 7110904 | tf_op jit(solution)/shard_map/sub | solution.py:583
  117.1 1.5 %copy.24 = f32[16,62,256]{2,0,1:T(8,128)} copy(f32[16,62,256]{2,1,0:T(8,128)S(1)} %get-tuple-element.20) | data formatting | bytes 2031616
  118.7 1.5 %copy.25 = f32[16,62,256]{2,0,1:T(8,128)} copy(f32[16,62,256]{2,1,0:T(8,128)S(1)} %get-tuple-element.21) | data formatting | bytes 2031616
  120.2 1.5 %copy.26 = f32[16,62,256]{2,0,1:T(8,128)} copy(f32[16,62,256]{2,1,0:T(8,128)S(1)} %get-tuple-element.22) | data formatting | bytes 2031616
  (4 shorter events, 0.0 us)
Async XLA Ops:
  3.0 21.1 %all-to-all-start = ((f32[128,1,128]{2,1,0:T(1,128)}), f32[128,1,128]{2,1,0:T(1,128)S(1)}, u32[]{:S(2)}, u32[]{:S(2)}) async-start(f32[128,1,128]{2,1,0:T(1,128)} %request.1), calls=%async_computation | async-start | bytes 131072 | tf_op jit(solution)/shard_map/all_to_all | solution.py:591
  29.6 4.4 %copy-start = (f32[1,3,16,128]{3,2,1,0:T(8,128)S(1)}, f32[1,3,16,128]{3,2,1,0:T(8,128)}, u32[]{:S(2)}) copy-start(f32[1,3,16,128]{3,2,1,0:T(8,128)} %param.18) | copy-start | bytes 73732
  29.6 25.2 %copy-start.4 = (s32[1,1,16]{2,1,0:T(1,128)S(1)}, s32[1,1,16]{2,1,0:T(1,128)}, u32[]{:S(2)}) copy-start(s32[1,1,16]{2,1,0:T(1,128)} %list_ref.5) | copy-start | bytes 196
  29.6 25.2 %copy-start.6 = (s32[1,1,8]{2,1,0:T(1,128)S(1)}, s32[1,1,8]{2,1,0:T(1,128)}, u32[]{:S(2)}) copy-start(s32[1,1,8]{2,1,0:T(1,128)} %start_ref.3) | copy-start | bytes 100
  29.6 25.2 %copy-start.7 = (s32[1,1,8]{2,1,0:T(1,128)S(1)}, s32[1,1,8]{2,1,0:T(1,128)}, u32[]{:S(2)}) copy-start(s32[1,1,8]{2,1,0:T(1,128)} %end_ref.3) | copy-start | bytes 100
  29.6 25.2 %all-to-all-start.1 = ((f32[128,1,2304]{2,1,0:T(1,128)}), f32[128,1,2304]{2,1,0:T(1,128)S(1)}, u32[]{:S(2)}, u32[]{:S(2)}) async-start(f32[128,1,2304]{2,1,0:T(1,128)} %records.1), calls=%async_computation.1 | async-start | bytes 2359296 | tf_op jit(solution)/shard_map/all_to_all | solution.py:591
  34.0 33.9 %copy-start.1 = (f32[128,128]{1,0:T(8,128)S(1)}, f32[128,128]{1,0:T(8,128)}, u32[]{:S(2)}) copy-start(f32[128,128]{1,0:T(8,128)} %constant.34.clone.across_ref) | copy-start | bytes 196612
  34.0 33.9 %copy-start.2 = (f32[32,40]{1,0:T(8,128)S(1)}, f32[32,40]{1,0:T(8,128)}, u32[]{:S(2)}) copy-start(f32[32,40]{1,0:T(8,128)} %constant.32.clone.first_ref) | copy-start | bytes 15364
  34.0 33.9 %copy-start.3 = (f32[16,32]{1,0:T(8,128)S(1)}, f32[16,32]{1,0:T(8,128)}, u32[]{:S(2)}) copy-start(f32[16,32]{1,0:T(8,128)} %constant.33.clone.second_ref) | copy-start | bytes 6148
  34.0 33.9 %copy-start.5 = (f32[8,128]{1,0:T(8,128)S(1)}, f32[8,128]{1,0:T(8,128)}, u32[]{:S(2)}) copy-start(f32[8,128]{1,0:T(8,128)} %constant.35.clone.seg_ref) | copy-start | bytes 12292
  34.1 32.9 %collective-permute-start.3 = (f32[3,10,128]{2,1,0:T(8,128)S(1)}, f32[3,10,128]{2,1,0:T(8,128)S(1)}, u32[]{:S(2)}, u32[]{:S(2)}) collective-permute-start(f32[3,10,128]{2,1,0:T(8,128)S(1)} %get-tuple-element.25), channel_id=1, source_target_pairs={{1,0},{2,1},{3,2},{5,4},{6,5},{7,6},{9,8},{10,9},{11,10},{13,12},{... | collective-permute-start | bytes 46088 | tf_op jit(solution)/shard_map/ppermute | solution.py:598
  59.2 7.8 %collective-permute-start.2 = (f32[3,10,128]{2,1,0:T(8,128)S(1)}, f32[3,10,128]{2,1,0:T(8,128)S(1)}, u32[]{:S(2)}, u32[]{:S(2)}) collective-permute-start(f32[3,10,128]{2,1,0:T(8,128)S(1)} %get-tuple-element.23), channel_id=1, source_target_pairs={{1,0},{2,1},{3,2},{5,4},{6,5},{7,6},{9,8},{10,9},{11,10},{13,12},{... | collective-permute-start | bytes 46088 | tf_op jit(solution)/shard_map/ppermute | solution.py:598
  60.5 6.5 %collective-permute-start.1 = (f32[3,10,128]{2,1,0:T(8,128)S(1)}, f32[3,10,128]{2,1,0:T(8,128)S(1)}, u32[]{:S(2)}, u32[]{:S(2)}) collective-permute-start(f32[3,10,128]{2,1,0:T(8,128)S(1)} %get-tuple-element.26), channel_id=1, source_target_pairs={{0,1},{1,2},{2,3},{4,5},{5,6},{6,7},{8,9},{9,10},{10,11},{12,13},{... | collective-permute-start | bytes 46088 | tf_op jit(solution)/shard_map/ppermute | solution.py:597
  64.5 3.4 %collective-permute-start = (f32[3,10,128]{2,1,0:T(8,128)S(1)}, f32[3,10,128]{2,1,0:T(8,128)S(1)}, u32[]{:S(2)}, u32[]{:S(2)}) collective-permute-start(f32[3,10,128]{2,1,0:T(8,128)S(1)} %get-tuple-element.24), channel_id=1, source_target_pairs={{0,1},{1,2},{2,3},{4,5},{5,6},{6,7},{8,9},{9,10},{10,11},{12,13},{... | collective-permute-start | bytes 46088 | tf_op jit(solution)/shard_map/ppermute | solution.py:597
  108.8 6.3 %copy-start.10 = (f32[16,62,256]{2,0,1:T(8,128)S(1)}, f32[16,62,256]{2,0,1:T(8,128)}, u32[]{:S(2)}) copy-start(f32[16,62,256]{2,0,1:T(8,128)} %param.16) | copy-start | bytes 3047428
  113.5 1.6 %copy-start.8 = (f32[16,62,256]{2,0,1:T(8,128)S(1)}, f32[16,62,256]{2,0,1:T(8,128)}, u32[]{:S(2)}) copy-start(f32[16,62,256]{2,0,1:T(8,128)} %param.14) | copy-start | bytes 3047428
  113.5 1.6 %copy-start.9 = (f32[16,62,256]{2,0,1:T(8,128)S(1)}, f32[16,62,256]{2,0,1:T(8,128)}, u32[]{:S(2)}) copy-start(f32[16,62,256]{2,0,1:T(8,128)} %param.15) | copy-start | bytes 3047428
  113.5 1.6 %copy-start.11 = (f32[62]{0:T(128)S(1)}, f32[62]{0:T(128)}, u32[]{:S(2)}) copy-start(f32[62]{0:T(128)} %constant.46) | copy-start | bytes 748
where the time goes:
time: 122 us
  Pallas kernels  29 us (24%)
  blocking collectives  28.2 us (23%)
  waiting for transfers between devices  28.1 us (23%)
  starting transfers between devices  24.9 us (20%)
  local copies, waits for them, and re-layouts  8.06 us (7%)
  other arithmetic  2.13 us (2%)
  between operations  1.49 us (1%)
    all_to_all x1, blocking collectives, exchanged(): return lax.all_to_all(slots, AXES, split_axis=0, concat_axis=0, tiled=True)  28.2 us
    all_to_all x2, waiting for transfers between devices, exchanged(): return lax.all_to_all(slots, AXES, split_axis=0, concat_axis=0, tiled=True)  27.2 us
    all_to_all x2, starting transfers between devices, exchanged(): return lax.all_to_all(slots, AXES, split_axis=0, concat_axis=0, tiled=True)  15.8 us
    pallas_call x1, Pallas kernels, per_device(): pl.pallas_call(backward_kernel, in_specs=[spec(SMEM)] * 4 + [spec(VMEM)]...  12.6 us
    unnamed x29, local copies, waits for them, and re-layouts  8.05 us
    ppermute x2, starting transfers between devices, halo(): before = lax.ppermute(array[:, ROWS - HALO:], 'band', up)  6.45 us
    pallas_call x1, Pallas kernels, per_device(): pl.pallas_call(records_kernel, in_specs=[spec(SMEM), spec(VMEM)], out_spe...  5.61 us
    pallas_call x1, Pallas kernels, per_device(): pl.pallas_call(pullback_kernel, in_specs=[spec(SMEM)] + [spec(VMEM)] * 2,...  4.7 us
  transfers between devices with their start and end apart: 6, of which 3 were waited for; matrix products, arithmetic and copies ran while one was open for 2% of the time, Pallas kernels for 4%

commit v1 on v0

--- a/solution.py
+++ b/solution.py
@@ -25,6 +25,8 @@
 RECORD = 9 * BLOCK
 SLOT = RECORD + 128
 ASK = 128
+UNROLL = 4
+KEPT = 18
 IMG_ROWS = BANDS * ROWS
 AXES = ("view", "band")
 
@@ -168,9 +170,13 @@
             out_ref[block // BLK_DEV] = jnp.where(lane == 0, local, row)
 
 
+def component(ref, c):
+    return ref[c]
+
+
 def shape_terms(g_ref):
-    squares = [jnp.exp(2.0 * g_ref[:, 6 + c, :]) for c in range(3)]
-    quat = [g_ref[:, 9 + c, :] for c in range(4)]
+    squares = [jnp.exp(2.0 * component(g_ref, 6 + c)) for c in range(3)]
+    quat = [component(g_ref, 9 + c) for c in range(4)]
     size = jnp.sqrt(quat[0] * quat[0] + quat[1] * quat[1] + quat[2] * quat[2] + quat[3] * quat[3])
     r, x, y, z = [q / size for q in quat]
     rotation = [
@@ -181,8 +187,16 @@
     return squares, rotation, (r, x, y, z), size
 
 
-def records_kernel(ask_ref, g_ref, out_ref, shape_ref):
-    squares, rot, unused, unused_size = shape_terms(g_ref)
+def opacity_of(g_ref):
+    return 1.0 / (1.0 + jnp.exp(-component(g_ref, 13)))
+
+
+def shapes_kernel(g_ref, shape_ref, kept_ref):
+    squares, rot, quat, size = shape_terms(g_ref)
+    opacity = opacity_of(g_ref)
+    kept = squares + rot[0] + rot[1] + rot[2] + list(quat) + [1.0 / size, 1.0 - opacity]
+    for i, value in enumerate(kept):
+        kept_ref[i] = value
     at = 0
     for i in range(3):
         for j in range(i, 3):
@@ -192,51 +206,60 @@
                 + rot[i][2] * rot[j][2] * squares[2]
             )
             at += 1
-    shape_ref[6] = 1.0 / (1.0 + jnp.exp(-g_ref[:, 13, :]))
-
-    def slot(s, carry):
-        local = ask_ref[s, 0, W_ID]
-
-        @pl.when(local >= 0.0)
-        def _():
-            k = local.astype(jnp.int32)
-
-            def word(i):
-                return ask_ref[s, 0, i]
-
-            def comp(i):
-                return g_ref[k, pl.ds(i, 1), :]
-
-            def put(p, value):
-                out_ref[s, :, pl.ds(p * BLOCK, BLOCK)] = value
-
-            time = word(W_CAM + 8)
-            centre = [comp(c) + time * comp(3 + c) for c in range(3)]
-            for p in range(2):
-                put(
-                    p,
-                    word(W_CAM + 3 * p) * centre[0]
-                    + word(W_CAM + 3 * p + 1) * centre[1]
-                    + word(W_CAM + 3 * p + 2) * centre[2]
-                    + word(W_CAM + 6 + p),
-                )
-            shapes = [shape_ref[i, pl.ds(k, 1), :] for i in range(6)]
-            for p, (at, extra) in enumerate(((W_CA, 0.3), (W_CB, 0.0), (W_CC, 0.3))):
-                total = word(at) * shapes[0]
-                for i in range(1, 6):
-                    total = total + word(at + i) * shapes[i]
-                put(2 + p, total + extra)
-            put(5, shape_ref[6, pl.ds(k, 1), :])
-            colour = word(W_SH) * g_ref[k, pl.ds(14, 3), :]
+    shape_ref[6] = opacity
+
+
+def listed_slots(ask_ref, order_ref):
+    def look(s, found):
+        order_ref[found] = s
+        return found + jnp.where(ask_ref[s, 0, W_ID] >= 0.0, 1, 0)
+
+    return lax.fori_loop(0, DEVICES, look, 0, unroll=8)
+
+
+def records_kernel(ask_ref, g_ref, shape_ref, out_ref, order_ref, count_ref):
+    count = listed_slots(ask_ref, order_ref)
+    count_ref[0] = count
+
+    def slot(n, carry):
+        s = order_ref[n]
+        k = ask_ref[s, 0, W_ID].astype(jnp.int32)
+
+        def word(i):
+            return ask_ref[s, 0, i]
+
+        def comp(i):
+            return g_ref[i, pl.ds(k, 1), :]
+
+        def put(p, value):
+            out_ref[s, :, pl.ds(p * BLOCK, BLOCK)] = value
+
+        time = word(W_CAM + 8)
+        centre = [comp(c) + time * comp(3 + c) for c in range(3)]
+        for p in range(2):
+            put(
+                p,
+                word(W_CAM + 3 * p) * centre[0]
+                + word(W_CAM + 3 * p + 1) * centre[1]
+                + word(W_CAM + 3 * p + 2) * centre[2]
+                + word(W_CAM + 6 + p),
+            )
+        shapes = [shape_ref[i, pl.ds(k, 1), :] for i in range(6)]
+        for p, (at, extra) in enumerate(((W_CA, 0.3), (W_CB, 0.0), (W_CC, 0.3))):
+            total = word(at) * shapes[0]
+            for i in range(1, 6):
+                total = total + word(at + i) * shapes[i]
+            put(2 + p, total + extra)
+        put(5, shape_ref[6, pl.ds(k, 1), :])
+        basis = [word(W_SH + q) for q in range(16)]
+        for ch in range(3):
+            colour = basis[0] * comp(14 + ch)
             for q in range(1, 16):
-                colour = colour + word(W_SH + q) * g_ref[k, pl.ds(14 + 3 * q, 3), :]
-            colour = colour + 0.5
-            for ch in range(3):
-                put(6 + ch, colour[ch : ch + 1])
-
+                colour = colour + basis[q] * comp(14 + 3 * q + ch)
+            put(6 + ch, colour + 0.5)
         return carry
 
-    lax.fori_loop(0, DEVICES, slot, 0)
+    lax.fori_loop(0, count, slot, 0)
 
 
 def pixel_rows(row_base):
@@ -259,7 +282,16 @@
 
 
 def render_kernel(
-    list_ref, start_ref, end_ref, base_ref, got_ref, pred_ref, compact_ref, table_ref
+    list_ref,
+    start_ref,
+    end_ref,
+    base_ref,
+    got_ref,
+    pred_ref,
+    compact_ref,
+    table_ref,
+    alpha_ref,
+    weight_ref,
 ):
     for t in range(TILES):
         first = start_ref[0, 0, t]
@@ -294,7 +326,10 @@
 
     def blend(i, carry):
         trans, red, green, blue = carry
-        weight = alpha_of(table_ref, i, px, py) * trans
+        alpha = alpha_of(table_ref, i, px, py)
+        weight = alpha * trans
+        alpha_ref[i] = alpha
+        weight_ref[i] = weight
         return (
             trans - weight,
             red + weight * row_of(table_ref, 6, i),
@@ -303,7 +338,7 @@
         )
 
     zero = jnp.zeros((ROWS, COLS), jnp.float32)
-    done = lax.fori_loop(0, GAUSS, blend, (zero + 1.0, zero, zero, zero), unroll=8)
+    done = lax.fori_loop(0, GAUSS, blend, (zero + 1.0, zero, zero, zero), unroll=16)
     for ch in range(3):
         pred_ref[ch] = done[1 + ch]
 
@@ -321,15 +356,27 @@
     return jnp.dot(a, b, precision=HIGHEST_MODE, preferred_element_type=jnp.float32)
 
 
+def extended(mine, before, after):
+    rest = jnp.zeros((EXT - ROWS - 2 * HALO, COLS), jnp.float32)
+    return jnp.concatenate([before, mine, after, rest], axis=0)
+
+
+def smoothed(maps, first, across):
+    wide = exact_dot(jnp.concatenate(maps, axis=0), across)
+    return [exact_dot(first, wide[EXT * m : EXT * (m + 1)]) for m in range(len(maps))]
+
+
+def target_kernel(target_ref, before_ref, after_ref, first_ref, across_ref, ext_ref, maps_ref):
+    first, across = first_ref[...], across_ref[...]
+    for ch in range(3):
+        y = extended(target_ref[ch], before_ref[ch], after_ref[ch])
+        ext_ref[ch] = y
+        maps_ref[ch, 0], maps_ref[ch, 1] = smoothed([y, y * y], first, across)
+
+
 def loss_gradient(
-    base, pred_ref, target_ref, before_ref, after_ref, first_ref, second_ref, across_ref, ext_ref
+    base, pred_ref, before_ref, after_ref, target_ref, maps_ref, first_ref, second_ref, across_ref
 ):
-    ext_ref[...] = jnp.zeros(ext_ref.shape, jnp.float32)
-    for part, mine in enumerate((pred_ref, target_ref)):
-        for ch in range(3):
-            ext_ref[part, ch, pl.ds(0, HALO), :] = before_ref[part, ch]
-            ext_ref[part, ch, pl.ds(HALO, ROWS), :] = mine[ch]
-            ext_ref[part, ch, pl.ds(HALO + ROWS, HALO), :] = after_ref[part, ch]
     first, second, across = first_ref[...], second_ref[...], across_ref[...]
     row = lax.broadcasted_iota(jnp.int32, (32, COLS), 0)
     image_row = row + base - 5
@@ -337,16 +384,16 @@
     total = jnp.zeros((ROWS, COLS), jnp.float32)
     slopes = []
     for ch in range(3):
-        x, y = ext_ref[0, ch], ext_ref[1, ch]
-        maps = jnp.concatenate([x, y, x * x, y * y, x * y], axis=0)
-        maps = exact_dot(maps, across)
-        smooth = [exact_dot(first, maps[EXT * m : EXT * (m + 1)]) for m in range(5)]
+        pred = pred_ref[ch]
+        x, y = extended(pred, before_ref[ch], after_ref[ch]), target_ref[ch]
+        mean, square, cross = smoothed([x, x * x, x * y], first, across)
+        smooth = [mean, maps_ref[ch, 0], square, maps_ref[ch, 1], cross]
         value, pullback = jax.vjp(ssim_value, *smooth)
         parts = pullback(jnp.full_like(value, -SSIM_WEIGHT / 3.0))
         adjoint = [jnp.where(inside, parts[m], 0.0) for m in (0, 2, 4)]
         back = [exact_dot(second, part) for part in adjoint]
         back = exact_dot(jnp.concatenate(back, axis=0), across)
-        pred, target = pred_ref[ch], target_ref[ch]
+        target = y[HALO : HALO + ROWS]
         error = pred - target
         sign = jnp.where(error > 0.0, 1.0, jnp.where(error < 0.0, -1.0, 0.0))
         slopes.append(
@@ -365,23 +412,24 @@
 
 def backward_kernel(
     list_ref,
+    count_ref,
     start_ref,
     end_ref,
     base_ref,
     pred_ref,
-    target_ref,
     before_ref,
     after_ref,
+    target_ref,
+    maps_ref,
     first_ref,
     second_ref,
     across_ref,
     seg_ref,
     compact_ref,
     table_ref,
+    alpha_ref,
+    weight_ref,
     out_ref,
-    ext_ref,
-    alpha_ref,
-    trans_ref,
     part_ref,
     moment_ref,
     grad_ref,
@@ -389,91 +437,88 @@
     total, slopes = loss_gradient(
         base_ref[0],
         pred_ref,
-        target_ref,
         before_ref,
         after_ref,
+        target_ref,
+        maps_ref,
         first_ref,
         second_ref,
         across_ref,
-        ext_ref,
     )
     loss_row = jnp.broadcast_to(total, (1, 128))
     empty = jnp.zeros((1, RECORD), jnp.float32)
 
-    def clear(s, carry):
+    def tell(s, carry):
         out_ref[s, :, pl.ds(RECORD, 128)] = loss_row
-        out_ref[s, :, pl.ds(0, RECORD)] = empty
         return carry
 
-    lax.fori_loop(0, DEVICES, clear, 0, unroll=4)
+    lax.fori_loop(0, DEVICES, tell, 0, unroll=8)
+
+    def clear(i, carry):
+        out_ref[list_ref[0, 0, i] // BLK_DEV, :, pl.ds(0, RECORD)] = empty
+        return carry
+
+    lax.fori_loop(0, count_ref[0, 0], clear, 0)
     px, py = pixel_rows(base_ref[0])
-
-    def forward(i, trans):
-        alpha = alpha_of(table_ref, i, px, py)
-        alpha_ref[i] = alpha
-        trans_ref[i] = trans
-        return trans - alpha * trans
-
-    one = jnp.ones((ROWS, COLS), jnp.float32)
-    lax.fori_loop(0, GAUSS, forward, one, unroll=8)
-    py_top, py_low = py[0:8], py[8:16]
 
     def fold(value):
         return value[0:8] + value[8:16]
 
     def reverse(step, behind):
-        chunk = GAUSS // 8 - 1 - step
-        for r in range(7, -1, -1):
-            i = chunk * 8 + r
-            alpha = alpha_ref[i]
-            trans = trans_ref[i]
-            weight = alpha * trans
-            seen = (
-                row_of(table_ref, 6, i) * slopes[0]
-                + row_of(table_ref, 7, i) * slopes[1]
-                + row_of(table_ref, 8, i) * slopes[2]
-            )
-            ahead = seen - behind
-            behind = behind + alpha * ahead
-            d_power = weight * ahead
-            dy = py - row_of(table_ref, 1, i)
-            d_row = d_power * dy
-            part_ref[0, pl.ds(8 * r, 8), :] = fold(d_power)
-            part_ref[1, pl.ds(8 * r, 8), :] = fold(d_row)
-            part_ref[2, pl.ds(8 * r, 8), :] = fold(d_row * dy)
+        for half in range(UNROLL - 1, -1, -1):
+            chunk = GAUSS // 8 - UNROLL * (step + 1) + half
+            for r in range(7, -1, -1):
+                i = chunk * 8 + r
+                alpha = alpha_ref[i]
+                weight = weight_ref[i]
+                seen = (
+                    row_of(table_ref, 6, i) * slopes[0]
+                    + row_of(table_ref, 7, i) * slopes[1]
+                    + row_of(table_ref, 8, i) * slopes[2]
+                )
+                ahead = seen - behind
+                behind = behind + alpha * ahead
+                d_power = weight * ahead
+                dy = py - row_of(table_ref, 1, i)
+                d_row = d_power * dy
+                part_ref[half, 0, pl.ds(8 * r, 8), :] = fold(d_power)
+                part_ref[half, 1, pl.ds(8 * r, 8), :] = fold(d_row)
+                part_ref[half, 2, pl.ds(8 * r, 8), :] = fold(d_row * dy)
+                for ch in range(3):
+                    part_ref[half, 3 + ch, pl.ds(8 * r, 8), :] = fold(weight * slopes[ch])
+            sums = []
+            for p in range(6):
+                piece = part_ref[half, p, pl.ds(0, 8, stride=8), :]
+                for s in range(1, 8):
+                    piece = piece + part_ref[half, p, pl.ds(s, 8, stride=8), :]
+                sums.append(piece)
+            here = pl.ds(pl.multiple_of(chunk * 8, 8), 8)
+            dx = px[0:8] - table_ref[0, here, :]
+            first_x = sums[0] * dx
+            moment_ref[0, here, :] = sums[0]
+            moment_ref[1, here, :] = first_x
+            moment_ref[2, here, :] = first_x * dx
+            moment_ref[3, here, :] = sums[1]
+            moment_ref[4, here, :] = sums[1] * dx
+            moment_ref[5, here, :] = sums[2]
             for ch in range(3):
-                part_ref[3 + ch, pl.ds(8 * r, 8), :] = fold(weight * slopes[ch])
-        sums = []
-        for p in range(6):
-            piece = part_ref[p, pl.ds(0, 8, stride=8), :]
-            for s in range(1, 8):
-                piece = piece + part_ref[p, pl.ds(s, 8, stride=8), :]
-            sums.append(piece)
-        here = pl.ds(pl.multiple_of(chunk * 8, 8), 8)
-        dx = px[0:8] - table_ref[0, here, :]
-        first_x = sums[0] * dx
-        moment_ref[0, here, :] = sums[0]
-        moment_ref[1, here, :] = first_x
-        moment_ref[2, here, :] = first_x * dx
-        moment_ref[3, here, :] = sums[1]
-        moment_ref[4, here, :] = sums[1] * dx
-        moment_ref[5, here, :] = sums[2]
-        for ch in range(3):
-            moment_ref[6 + ch, here, :] = sums[3 + ch]
+                moment_ref[6 + ch, here, :] = sums[3 + ch]
         return behind
 
-    lax.fori_loop(0, GAUSS // 8, reverse, jnp.zeros((ROWS, COLS), jnp.float32))
-    seg = seg_ref[...]
-    m = [
-        lax.dot_general(
-            seg,
-            moment_ref[p],
-            (((1,), (1,)), ((), ())),
-            precision=HIGHEST_MODE,
-            preferred_element_type=jnp.float32,
+    lax.fori_loop(0, GAUSS // 8 // UNROLL, reverse, jnp.zeros((ROWS, COLS), jnp.float32))
+    seg = seg_ref[...].astype(jnp.bfloat16)
+
+    def over_tile(value):
+        return lax.dot_general(
+            seg, value, (((1,), (1,)), ((), ())), preferred_element_type=jnp.float32
         )
-        for p in range(9)
-    ]
+
+    m = []
+    for p in range(9):
+        value = moment_ref[p]
+        large = value.astype(jnp.bfloat16)
+        small = (value - large.astype(jnp.float32)).astype(jnp.bfloat16)
+        m.append(over_tile(large) + over_tile(small))
     ca, cb, cc = compact_ref[2], compact_ref[3], compact_ref[4]
     inverse = 1.0 / (ca * cc - cb * cb)
     d_inverse = -0.5 * cc * m[2] + cb * m[4] - 0.5 * ca * m[5]
@@ -501,53 +546,105 @@
                     )
 
 
-def pullback_kernel(ask_ref, g_ref, got_ref, grad_ref, loss_ref, shape_ref):
+def update_kernel(
+    order_ref,
+    count_ref,
+    ask_ref,
+    kept_ref,
+    g_ref,
+    one_ref,
+    two_ref,
+    got_ref,
+    loss_ref,
+    new_out,
+    one_out,
+    two_out,
+    grad_out,
+    new_ref,
+    new_one_ref,
+    new_two_ref,
+    grad_ref,
+    shape_ref,
+    done_sem,
+):
+    rates = [float(rate) / BIAS_FIRST for rate in learning_rates()]
+    copies = []
+
+    def finish(low, high):
+        for c in range(low, high):
+            gradient = grad_ref[c]
+            new_one = 0.9 * one_ref[c] + 0.1 * gradient
+            new_two = 0.999 * two_ref[c] + 0.001 * gradient * gradient
+            root = jnp.sqrt(new_two * (1.0 / BIAS_SECOND)) + 1e-08
+            new_ref[c] = g_ref[c] - rates[c] * new_one / root
+            new_one_ref[c] = new_one
+            new_two_ref[c] = new_two
+        here = pl.ds(low, high - low)
+        for held, out in (
+            (new_ref, new_out),
+            (new_one_ref, one_out),
+            (new_two_ref, two_out),
+            (grad_ref, grad_out),
+        ):
+            copy = pltpu.make_async_copy(held.at[here], out.at[here], done_sem.at[len(copies)])
+            copy.start()
+            copies.append(copy)
+
     losses = got_ref[:, :, pl.ds(RECORD, 128)]
     loss_ref[...] = jnp.sum(losses, axis=0) * (1.0 / (DEVICES * ROWS * COLS))
     grad_ref[...] = jnp.zeros(grad_ref.shape, jnp.float32)
     shape_ref[...] = jnp.zeros(shape_ref.shape, jnp.float32)
-
-    def slot(s, carry):
-        local = ask_ref[s, 0, W_ID]
-
-        @pl.when(local >= 0.0)
-        def _():
-            k = local.astype(jnp.int32)
-
-            def word(i):
-                return ask_ref[s, 0, i]
-
-            d = [got_ref[s, :, pl.ds(p * BLOCK, BLOCK)] for p in range(9)]
-            time = word(W_CAM + 8)
-            for c in range(3):
-                d_centre = word(W_CAM + c) * d[0] + word(W_CAM + 3 + c) * d[1]
-                grad_ref[k, pl.ds(c, 1), :] = grad_ref[k, pl.ds(c, 1), :] + d_centre
-                grad_ref[k, pl.ds(3 + c, 1), :] = grad_ref[k, pl.ds(3 + c, 1), :] + time * d_centre
-            here = pl.ds(k, 1)
-            for i in range(6):
-                shape_ref[i, here, :] = shape_ref[i, here, :] + (
-                    word(W_CA + i) * d[2] + word(W_CB + i) * d[3] + word(W_CC + i) * d[4]
-                )
-            shape_ref[6, here, :] = shape_ref[6, here, :] + d[5]
-            colour = jnp.concatenate(d[6:9], axis=0)
-            for q in range(16):
-                at = pl.ds(14 + 3 * q, 3)
-                grad_ref[k, at, :] = grad_ref[k, at, :] + word(W_SH + q) * colour
-
+    count = count_ref[0]
+
+    def slot(n, carry):
+        s = order_ref[n]
+        k = ask_ref[s, 0, W_ID].astype(jnp.int32)
+
+        def word(i):
+            return ask_ref[s, 0, i]
+
+        here = pl.ds(k, 1)
+
+        def add(c, value):
+            grad_ref[c, here, :] = grad_ref[c, here, :] + value
+
+        d = [got_ref[s, :, pl.ds(p * BLOCK, BLOCK)] for p in range(9)]
+        time = word(W_CAM + 8)
+        for c in range(3):
+            d_centre = word(W_CAM + c) * d[0] + word(W_CAM + 3 + c) * d[1]
+            add(c, d_centre)
+            add(3 + c, time * d_centre)
+        for i in range(6):
+            shape_ref[i, here, :] = shape_ref[i, here, :] + (
+                word(W_CA + i) * d[2] + word(W_CB + i) * d[3] + word(W_CC + i) * d[4]
+            )
+        shape_ref[6, here, :] = shape_ref[6, here, :] + d[5]
+        for q in range(16):
+            basis = word(W_SH + q)
+            for ch in range(3):
+                add(14 + 3 * q + ch, basis * d[6 + ch])
         return carry
 
-    lax.fori_loop(0, DEVICES, slot, 0)
-    squares, rot, quat, size = shape_terms(g_ref)
+    lax.fori_loop(0, count, slot, 0)
+    for low, high in ((14, 30), (30, 46), (46, COMPS)):
+        finish(low, high)
+    squares = [kept_ref[c] for c in range(3)]
+    rot = [[kept_ref[3 + 3 * i + c] for c in range(3)] for i in range(3)]
+    quat = [kept_ref[12 + c] for c in range(4)]
     s00, s01, s02, s11, s12, s22 = [shape_ref[i] for i in range(6)]
     twice = [[2.0 * s00, s01, s02], [s01, 2.0 * s11, s12], [s02, s12, 2.0 * s22]]
     d_rot = [[None] * 3 for _ in range(3)]
+
+    def put(c, value):
+        grad_ref[c] = value
+
     for c in range(3):
         pulled = [
             twice[i][0] * rot[0][c] + twice[i][1] * rot[1][c] + twice[i][2] * rot[2][c]
             for i in range(3)
         ]
         along = rot[0][c] * pulled[0] + rot[1][c] * pulled[1] + rot[2][c] * pulled[2]
-        grad_ref[:, 6 + c, :] = squares[c] * along
+        put(6 + c, squares[c] * along)
         for i in range(3):
             d_rot[i][c] = pulled[i] * squares[c]
     r, x, y, z = quat
@@ -570,17 +667,11 @@
     d_quat = [d_r, d_x, d_y, d_z]
     along = r * d_r + x * d_x + y * d_y + z * d_z
     for c in range(4):
-        grad_ref[:, 9 + c, :] = (d_quat[c] - quat[c] * along) / size
-    opacity = 1.0 / (1.0 + jnp.exp(-g_ref[:, 13, :]))
-    grad_ref[:, 13, :] = shape_ref[6] * (1.0 - opacity)
-
-
-def adam_update(gaussians, moment_one, moment_two, gradient):
-    learn_rates = jnp.asarray(learning_rates())[None, :, None]
-    new_one = 0.9 * moment_one + 0.1 * gradient
-    new_two = 0.999 * moment_two + 0.001 * gradient * gradient
-    change = learn_rates * (new_one / BIAS_FIRST) / (jnp.sqrt(new_two / BIAS_SECOND) + 1e-08)
-    return (gaussians - change, new_one, new_two)
+        put(9 + c, (d_quat[c] - quat[c] * along) * kept_ref[16])
+    put(13, shape_ref[6] * kept_ref[17])
+    finish(0, 14)
+    for copy in copies:
+        copy.wait()
 
 
 def shaped(*shape):
@@ -610,6 +701,11 @@
     tile_start,
     tile_end,
 ):
+    flat, flat_one, flat_two = [
+        jnp.transpose(a, (1, 0, 2))
+        for a in (gaussians, first_moment, second_moment)
+    ]
+    first, second, across = tap_matrices()
     base = (lax.axis_index("band") * ROWS).astype(jnp.int32).reshape(1)
     request = pl.pallas_call(
         request_kernel,
@@ -620,74 +716,100 @@
     )(block_list, block_count, camera)
     asked = exchanged(request)
     target_band = target[0]
-    target_before, target_after = halo(target_band)
-    records = pl.pallas_call(
+    shapes, kept = pl.pallas_call(
+        shapes_kernel,
+        in_specs=[spec(VMEM)],
+        out_specs=[spec(VMEM)] * 2,
+        out_shape=[shaped(7, BLK_DEV, BLOCK), shaped(KEPT, BLK_DEV, BLOCK)],
+        compiler_params=params(16),
+        name="shapes",
+    )(flat)
+    asked, shapes, kept = lax.optimization_barrier((asked, shapes, kept))
+    records, order, count = pl.pallas_call(
         records_kernel,
-        in_specs=[spec(SMEM), spec(VMEM)],
-        out_specs=spec(VMEM),
-        out_shape=shaped(DEVICES, 1, RECORD),
-        scratch_shapes=[VMEM((7, BLK_DEV, BLOCK), jnp.float32)],
-        compiler_params=params(32),
+        in_specs=[spec(SMEM), spec(VMEM), spec(VMEM)],
+        out_specs=[spec(VMEM), spec(SMEM), spec(SMEM)],
+        out_shape=[
+            shaped(DEVICES, 1, RECORD),
+            jax.ShapeDtypeStruct((DEVICES + 1,), jnp.int32),
+            jax.ShapeDtypeStruct((1,), jnp.int32),
+        ],
+        compiler_params=params(16),
         name="records",
-    )(asked, gaussians)
+    )(asked, flat, shapes)
+    records, target_band = lax.optimization_barrier((records, target_band))
     received = exchanged(records)
-    pred, compact, table = pl.pallas_call(
+    target_ext, target_maps = pl.pallas_call(
+        target_kernel,
+        in_specs=[spec(VMEM)] * 5,
+        out_specs=[spec(VMEM)] * 2,
+        out_shape=[shaped(3, EXT, COLS), shaped(3, 2, 32, COLS)],
+        compiler_params=params(16),
+        name="target",
+    )(target_band, *halo(target_band), first, across)
+    received, target_ext, target_maps = lax.optimization_barrier(
+        (received, target_ext, target_maps)
+    )
+    pred, compact, table, alpha, weight = pl.pallas_call(
         render_kernel,
         in_specs=[spec(SMEM)] * 4 + [spec(VMEM)],
-        out_specs=[spec(VMEM)] * 3,
+        out_specs=[spec(VMEM)] * 5,
         out_shape=[
             shaped(3, ROWS, COLS),
             shaped(9, TILES, GAUSS),
             shaped(9, GAUSS, COLS),
+            shaped(GAUSS, ROWS, COLS),
+            shaped(GAUSS, ROWS, COLS),
         ],
-        compiler_params=params(32),
+        compiler_params=params(16),
         name="render",
     )(block_list, tile_start, tile_end, base, received)
     pred_before, pred_after = halo(pred)
-    first, second, across = tap_matrices()
     seg = (np.arange(COLS)[None, :] // TILE == np.arange(TILES)[:, None]).astype(np.float32)
     outgoing = pl.pallas_call(
         backward_kernel,
-        in_specs=[spec(SMEM)] * 4 + [spec(VMEM)] * 10,
+        in_specs=[spec(SMEM)] * 5 + [spec(VMEM)] * 13,
         out_specs=spec(VMEM),
         out_shape=shaped(DEVICES, 1, SLOT),
         scratch_shapes=[
-            VMEM((2, 3, EXT, COLS), jnp.float32),
-            VMEM((GAUSS, ROWS, COLS), jnp.float32),
-            VMEM((GAUSS, ROWS, COLS), jnp.float32),
-            VMEM((6, 64, COLS), jnp.float32),
+            VMEM((UNROLL, 6, 64, COLS), jnp.float32),
             VMEM((9, GAUSS, COLS), jnp.float32),
             VMEM((9, TILES, GAUSS), jnp.float32),
         ],
-        compiler_params=params(48),
+        compiler_params=params(16),
         name="backward",
     )(
         block_list,
+        block_count,
         tile_start,
         tile_end,
         base,
         pred,
-        target_band,
-        jnp.stack([pred_before, target_before]),
-        jnp.stack([pred_after, target_after]),
+        pred_before,
+        pred_after,
+        target_ext,
+        target_maps,
         first,
         second,
         across,
         seg,
         compact,
         table,
+        alpha,
+        weight,
     )
     incoming = exchanged(outgoing)
-    gradient, loss = pl.pallas_call(
-        pullback_kernel,
-        in_specs=[spec(SMEM)] + [spec(VMEM)] * 2,
-        out_specs=[spec(VMEM)] * 2,
-        out_shape=[shaped(BLK_DEV, COMPS, BLOCK), shaped(1, 128)],
-        scratch_shapes=[VMEM((7, BLK_DEV, BLOCK), jnp.float32)],
-        compiler_params=params(32),
-        name="pullback",
-    )(asked, gaussians, incoming)
-    new_params, new_one, new_two = adam_update(gaussians, first_moment, second_moment, gradient)
+    loss, *flats = pl.pallas_call(
+        update_kernel,
+        in_specs=[spec(SMEM)] * 3 + [spec(VMEM)] * 5,
+        out_specs=[spec(VMEM)] + [spec(pl.ANY)] * 4,
+        out_shape=[shaped(1, 128)] + [shaped(COMPS, BLK_DEV, BLOCK)] * 4,
+        scratch_shapes=[VMEM((COMPS, BLK_DEV, BLOCK), jnp.float32)] * 4
+        + [VMEM((7, BLK_DEV, BLOCK), jnp.float32), pltpu.SemaphoreType.DMA((16,))],
+        compiler_params=params(16),
+        name="update",
+    )(order, count, asked, kept, flat, flat_one, flat_two, incoming)
+    new_params, new_one, new_two, gradient = [jnp.transpose(a, (1, 0, 2)) for a in flats]
     return (new_params, new_one, new_two, loss[0, 0], gradient)
 
 

time: 122 us -> 107 us (0.88)
  local copies, waits for them, and re-layouts: 8.06 us -> 1.29 us
  Pallas kernels: 29 us -> 24.3 us
  waiting for transfers between devices: 28.1 us -> 23.8 us
  other arithmetic: 2.13 us -> 0 us
  starting transfers between devices: 24.9 us -> 26.7 us
    all_to_all x2, waiting for transfers between devices: 27.2 us -> 19.5 us  [exchanged(): return lax.all_to_all(slots, AXES, split_axis=0, concat_axis=0, tiled=True)]
    unnamed x29 -> x24, local copies, waits for them, and re-layouts: 8.05 us -> 1.28 us
    pallas_call x3 -> x5, Pallas kernels: 22.9 us -> 18.5 us  [the longest x1 8.27 us: per_device(): pl.pallas_call(backward_kernel, in_specs=[spec(SMEM)] * 5 + [spec(VMEM)]...]
    ppermute x2, waiting for transfers between devices: 0.01 us -> 3.37 us  [halo(): after = lax.ppermute(array[:, :HALO], 'band', down)]
    sub x1 -> x0, other arithmetic: 2.12 us -> none  [adam_update(): return (gaussians - change, new_one, new_two)]
    ppermute x2, starting transfers between devices: 6.45 us -> 8.03 us  [halo(): before = lax.ppermute(array[:, ROWS - HALO:], 'band', up)]
  transfers between devices with their start and end apart: 6 -> 6, of which waited for: 3 -> 4; matrix products, arithmetic and copies ran while one was open for 2% -> 0% of each run, Pallas kernels for 4% -> 1%
where the time goes in v1:
time: 107 us; the launch traced here: 106 us
  blocking collectives  28.4 us (27%)
  starting transfers between devices  26.7 us (25%)
  Pallas kernels  24.3 us (23%)
  waiting for transfers between devices  23.8 us (22%)
  between operations  1.49 us (1%)
  local copies, waits for them, and re-layouts  1.29 us (1%)
    all_to_all x1, blocking collectives, exchanged(): return lax.all_to_all(slots, AXES, split_axis=0, concat_axis=0, tiled=True)  28.4 us
    all_to_all x2, waiting for transfers between devices, exchanged(): return lax.all_to_all(slots, AXES, split_axis=0, concat_axis=0, tiled=True)  19.5 us
    all_to_all x2, starting transfers between devices, exchanged(): return lax.all_to_all(slots, AXES, split_axis=0, concat_axis=0, tiled=True)  16.1 us
    pallas_call x1, Pallas kernels, per_device(): pl.pallas_call(backward_kernel, in_specs=[spec(SMEM)] * 5 + [spec(VMEM)]...  8.27 us
    ppermute x2, starting transfers between devices, halo(): before = lax.ppermute(array[:, ROWS - HALO:], 'band', up)  8.03 us
    pallas_call x1, Pallas kernels, per_device(): pl.pallas_call(update_kernel, in_specs=[spec(SMEM)] * 3 + [spec(VMEM)] *...  5.77 us
    pallas_call x1, Pallas kernels, per_device(): pl.pallas_call(render_kernel, in_specs=[spec(SMEM)] * 4 + [spec(VMEM)], o...  4.14 us
    pallas_call x1, Pallas kernels, per_device(): pl.pallas_call(records_kernel, in_specs=[spec(SMEM), spec(VMEM), spec(VME...  3.55 us
  transfers between devices with their start and end apart: 6, of which 4 were waited for; matrix products, arithmetic and copies ran while one was open for 0% of the time, Pallas kernels for 1%

profile of v1, /device:TPU:1, one launch (start us, length us, event | category | flops | bytes accessed | tf_op | source)
XLA Modules:
  0.0 105.9 jit_solution(4583364204409567735)
XLA Ops:
  1.3 1.7 %request.1 = f32[128,1,128]{2,1,0:T(1,128)} custom-call(s32[1,1,16]{2,1,0:T(1,128)} %list_ref.5, s32[1,1]{1,0:T(1,128)S(6)} %copy.18.count_ref, f32[1,9]{1,0:T(1,128)} %cam_ref.1), custom_call_target="tpu_custom_call" | custom-call | tf_op jit(solution)/shard_map/request/pallas_call | solution.py:710
  2.9 11.5 %all-to-all-start = ((f32[128,1,128]{2,1,0:T(1,128)}), f32[128,1,128]{2,1,0:T(1,128)S(1)}, u32[]{:S(2)}, u32[]{:S(2)}) async-start(f32[128,1,128]{2,1,0:T(1,128)} %request.1), calls=%async_computation | async-start | bytes 131072 | tf_op jit(solution)/shard_map/all_to_all | solution.py:682
  14.4 0.0 copy-start
  14.5 1.2 %copy-done = f32[16,62,256]{2,0,1:T(8,128)S(1)} copy-done((f32[16,62,256]{2,0,1:T(8,128)S(1)}, f32[16,62,256]{2,0,1:T(8,128)}, u32[]{:S(2)}) %copy-start) | copy-done | bytes 1015832
  15.7 0.0 copy-start.1
  15.7 0.1 shapes.1
  15.7 8.3 %all-to-all-done.ask_ref = f32[128,1,128]{2,1,0:T(1,128)S(1)} async-done(((f32[128,1,128]{2,1,0:T(1,128)}), f32[128,1,128]{2,1,0:T(1,128)S(1)}, u32[]{:S(2)}, u32[]{:S(2)}) %all-to-all-start) | async-done | bytes 65568 | tf_op jit(solution)/shard_map/all_to_all | solution.py:682
  24.0 0.0 copy-done.1
  24.0 3.6 %records.1 = (f32[128,1,2304]{2,1,0:T(1,128)}, s32[129]{0:T(256)S(1)}, s32[1]{0:T(128)}) custom-call(f32[128,1,128]{2,1,0:T(1,128)S(1)} %all-to-all-done.ask_ref, f32[62,16,256]{2,1,0:T(8,128)S(1)} %bitcast.12, f32[7,16,256]{2,1,0:T(8,128)S(1)} %get-tuple-element.33.shape_ref), custom_call_target="tpu_custom_call" | custom-call | tf_op jit(solution)/shard_map/records/pallas_call | solution.py:728
  27.6 0.0 copy-start.5
  27.6 0.0 copy-start.4
  27.6 0.0 copy-start.6
  27.6 0.0 copy-start.8
  27.6 0.0 copy-start.10
  27.6 0.0 copy-start.11
  27.6 4.6 %all-to-all-start.1 = ((f32[128,1,2304]{2,1,0:T(1,128)}), f32[128,1,2304]{2,1,0:T(1,128)S(1)}, u32[]{:S(2)}, u32[]{:S(2)}) async-start(f32[128,1,2304]{2,1,0:T(1,128)} %get-tuple-element.38), calls=%async_computation.1 | async-start | bytes 2359296 | tf_op jit(solution)/shard_map/all_to_all | solution.py:682
  32.2 0.0 copy-done.5
  32.2 0.0 copy-start.7
  32.3 0.0 copy-start.9
  32.3 1.3 %collective-permute-start.1 = (f32[3,10,128]{2,1,0:T(8,128)S(1)}, f32[3,10,128]{2,1,0:T(8,128)S(1)}, u32[]{:S(2)}, u32[]{:S(2)}) collective-permute-start(f32[3,10,128]{2,1,0:T(8,128)S(1)} %get-tuple-element.57), channel_id=1, source_target_pairs={{1,0},{2,1},{3,2},{5,4},{6,5},{7,6},{9,8},{10,9},{11,10},{13,12},{... | collective-permute-start | bytes 46088 | tf_op jit(solution)/shard_map/ppermute | solution.py:689
  33.6 4.0 %collective-permute-start = (f32[3,10,128]{2,1,0:T(8,128)S(1)}, f32[3,10,128]{2,1,0:T(8,128)S(1)}, u32[]{:S(2)}, u32[]{:S(2)}) collective-permute-start(f32[3,10,128]{2,1,0:T(8,128)S(1)} %get-tuple-element.58), channel_id=1, source_target_pairs={{0,1},{1,2},{2,3},{4,5},{5,6},{6,7},{8,9},{9,10},{10,11},{12,13},{... | collective-permute-start | bytes 46088 | tf_op jit(solution)/shard_map/ppermute | solution.py:688
  37.6 3.4 %collective-permute-done.1.after_ref = f32[3,10,128]{2,1,0:T(8,128)S(1)} collective-permute-done((f32[3,10,128]{2,1,0:T(8,128)S(1)}, f32[3,10,128]{2,1,0:T(8,128)S(1)}, u32[]{:S(2)}, u32[]{:S(2)}) %collective-permute-start.1) | collective-permute-done | bytes 15392 | tf_op jit(solution)/shard_map/ppermute | solution.py:689
  41.0 0.0 collective-permute-done.before_ref
  41.0 0.0 copy-done.4
  41.0 0.0 copy-done.6
  41.0 0.8 target.1
  41.8 11.2 %all-to-all-done.1.got_ref = f32[128,1,2304]{2,1,0:T(1,128)S(1)} async-done(((f32[128,1,2304]{2,1,0:T(1,128)}), f32[128,1,2304]{2,1,0:T(1,128)S(1)}, u32[]{:S(2)}, u32[]{:S(2)}) %all-to-all-start.1) | async-done | bytes 1179680 | tf_op jit(solution)/shard_map/all_to_all | solution.py:682
  53.0 0.0 copy-done.8
  53.0 0.0 copy-done.10
  53.0 0.0 copy-done.11
  53.0 4.1 %render.1 = (f32[3,16,128]{2,1,0:T(8,128)S(1)}, f32[9,8,512]{2,1,0:T(8,128)S(1)}, f32[9,512,128]{2,1,0:T(8,128)S(1)}, f32[512,16,128]{2,1,0:T(8,128)S(1)}, f32[512,16,128]{2,1,0:T(8,128)S(1)}) custom-call(s32[1,1,16]{2,1,0:T(1,128)S(1)} %copy-done.8, s32[1,1,8]{2,1,0:T(1,128)S(1)} %copy-done.10, s32[1,1,8]{2,1,0:T(1,128)S(1)} %copy-done.11, ...), custom_call_target="tpu_custom_call" | custom-call | tf_op jit(solution)/shard_map/render/pallas_call | solution.py:753
  57.2 1.3 %collective-permute-start.3 = (f32[3,10,128]{2,1,0:T(8,128)S(1)}, f32[3,10,128]{2,1,0:T(8,128)S(1)}, u32[]{:S(2)}, u32[]{:S(2)}) collective-permute-start(f32[3,10,128]{2,1,0:T(8,128)S(1)} %get-tuple-element.55), channel_id=1, source_target_pairs={{1,0},{2,1},{3,2},{5,4},{6,5},{7,6},{9,8},{10,9},{11,10},{13,12},{... | collective-permute-start | bytes 46088 | tf_op jit(solution)/shard_map/ppermute | solution.py:689
  58.5 4.0 %collective-permute-start.2 = (f32[3,10,128]{2,1,0:T(8,128)S(1)}, f32[3,10,128]{2,1,0:T(8,128)S(1)}, u32[]{:S(2)}, u32[]{:S(2)}) collective-permute-start(f32[3,10,128]{2,1,0:T(8,128)S(1)} %get-tuple-element.56), channel_id=1, source_target_pairs={{0,1},{1,2},{2,3},{4,5},{5,6},{6,7},{8,9},{9,10},{10,11},{12,13},{... | collective-permute-start | bytes 46088 | tf_op jit(solution)/shard_map/ppermute | solution.py:688
  62.5 0.0 collective-permute-done.3.after_ref
  62.5 0.9 collective-permute-done.2.before_ref
  63.4 0.0 copy-done.7
  63.4 0.0 copy-done.9
  63.4 8.3 %backward.1 = f32[128,1,2432]{2,1,0:T(1,128)S(1)} custom-call(s32[1,1,16]{2,1,0:T(1,128)S(1)} %copy-done.8, s32[1,1]{1,0:T(1,128)S(6)} %copy.18.count_ref, s32[1,1,8]{2,1,0:T(1,128)S(1)} %copy-done.10, s32[1,1,8]{2,1,0:T(1,128)S(1)} %copy-done.11, s32[1]{0:T(128)} %bitcast.3.base_ref, f32[3,16,128]{2,1,0:T(8,128)S(1)} %get-tuple-element.43.pred_ref, ...), custom_call_target="tpu_custom_call" | custom-call | tf_op jit(solution)/shard_map/backward/pallas_call | solution.py:769
  71.7 0.0 copy-start.2
  71.7 0.0 copy-start.3
  71.7 28.4 %all_to_all.15.got_ref = f32[128,1,2432]{2,1,0:T(1,128)S(1)} all-to-all(f32[128,1,2432]{2,1,0:T(1,128)S(1)} %backward.1), channel_id=1, replica_groups=mesh['view'=32,'band'=4] {'view','band'}, dimensions={0} | all-to-all | bytes 2490368 | tf_op jit(solution)/shard_map/all_to_all | solution.py:682
  100.2 0.0 copy-done.2
  100.2 0.0 copy-done.3
  100.2 5.8 %update.1 = (f32[1,128]{1,0:T(1,128)}, f32[62,16,256]{2,1,0:T(8,128)}, f32[62,16,256]{2,1,0:T(8,128)}, f32[62,16,256]{2,1,0:T(8,128)}, f32[62,16,256]{2,1,0:T(8,128)}) custom-call(s32[129]{0:T(256)S(1)} %get-tuple-element.34.order_ref, s32[1]{0:T(128)} %get-tuple-element.35.count_ref, f32[128,1,128]{2,1,0:T(1,128)S(1)} %all-to-all-done.ask_ref, ...), custom_call_target="tpu_custom_call" | custom-call | tf_op jit(solution)/shard_map/update/pallas_call | solution.py:802
  (2 shorter events, 0.0 us)
Async XLA Ops:
  2.9 21.1 %all-to-all-start = ((f32[128,1,128]{2,1,0:T(1,128)}), f32[128,1,128]{2,1,0:T(1,128)S(1)}, u32[]{:S(2)}, u32[]{:S(2)}) async-start(f32[128,1,128]{2,1,0:T(1,128)} %request.1), calls=%async_computation | async-start | bytes 131072 | tf_op jit(solution)/shard_map/all_to_all | solution.py:682
  14.4 1.2 %copy-start = (f32[16,62,256]{2,0,1:T(8,128)S(1)}, f32[16,62,256]{2,0,1:T(8,128)}, u32[]{:S(2)}) copy-start(f32[16,62,256]{2,0,1:T(8,128)} %param.13) | copy-start | bytes 3047428
  15.7 8.3 %copy-start.1 = (f32[16,62,256]{2,0,1:T(8,128)S(1)}, f32[16,62,256]{2,0,1:T(8,128)}, u32[]{:S(2)}) copy-start(f32[16,62,256]{2,0,1:T(8,128)} %param.13) | copy-start | bytes 3047428
  27.6 4.7 %copy-start.5 = (f32[1,3,16,128]{3,2,1,0:T(8,128)S(1)}, f32[1,3,16,128]{3,2,1,0:T(8,128)}, u32[]{:S(2)}) copy-start(f32[1,3,16,128]{3,2,1,0:T(8,128)} %param.17) | copy-start | bytes 73732
  27.6 13.4 %copy-start.4 = (f32[128,128]{1,0:T(8,128)S(1)}, f32[128,128]{1,0:T(8,128)}, u32[]{:S(2)}) copy-start(f32[128,128]{1,0:T(8,128)} %constant.15.clone.across_ref) | copy-start | bytes 196612
  27.6 13.4 %copy-start.6 = (f32[32,40]{1,0:T(8,128)S(1)}, f32[32,40]{1,0:T(8,128)}, u32[]{:S(2)}) copy-start(f32[32,40]{1,0:T(8,128)} %constant.14.clone.first_ref) | copy-start | bytes 15364
  27.6 25.4 %copy-start.8 = (s32[1,1,16]{2,1,0:T(1,128)S(1)}, s32[1,1,16]{2,1,0:T(1,128)}, u32[]{:S(2)}) copy-start(s32[1,1,16]{2,1,0:T(1,128)} %list_ref.5) | copy-start | bytes 196
  27.6 25.4 %copy-start.10 = (s32[1,1,8]{2,1,0:T(1,128)S(1)}, s32[1,1,8]{2,1,0:T(1,128)}, u32[]{:S(2)}) copy-start(s32[1,1,8]{2,1,0:T(1,128)} %start_ref.3) | copy-start | bytes 100
  27.6 25.4 %copy-start.11 = (s32[1,1,8]{2,1,0:T(1,128)S(1)}, s32[1,1,8]{2,1,0:T(1,128)}, u32[]{:S(2)}) copy-start(s32[1,1,8]{2,1,0:T(1,128)} %end_ref.3) | copy-start | bytes 100
  27.6 25.4 %all-to-all-start.1 = ((f32[128,1,2304]{2,1,0:T(1,128)}), f32[128,1,2304]{2,1,0:T(1,128)S(1)}, u32[]{:S(2)}, u32[]{:S(2)}) async-start(f32[128,1,2304]{2,1,0:T(1,128)} %get-tuple-element.38), calls=%async_computation.1 | async-start | bytes 2359296 | tf_op jit(solution)/shard_map/all_to_all | solution.py:682
  32.2 31.2 %copy-start.7 = (f32[16,32]{1,0:T(8,128)S(1)}, f32[16,32]{1,0:T(8,128)}, u32[]{:S(2)}) copy-start(f32[16,32]{1,0:T(8,128)} %constant.16.clone.second_ref) | copy-start | bytes 6148
  32.3 31.2 %copy-start.9 = (f32[8,128]{1,0:T(8,128)S(1)}, f32[8,128]{1,0:T(8,128)}, u32[]{:S(2)}) copy-start(f32[8,128]{1,0:T(8,128)} %constant.17.clone.seg_ref) | copy-start | bytes 12292
  32.3 8.7 %collective-permute-start.1 = (f32[3,10,128]{2,1,0:T(8,128)S(1)}, f32[3,10,128]{2,1,0:T(8,128)S(1)}, u32[]{:S(2)}, u32[]{:S(2)}) collective-permute-start(f32[3,10,128]{2,1,0:T(8,128)S(1)} %get-tuple-element.57), channel_id=1, source_target_pairs={{1,0},{2,1},{3,2},{5,4},{6,5},{7,6},{9,8},{10,9},{11,10},{13,12},{... | collective-permute-start | bytes 46088 | tf_op jit(solution)/shard_map/ppermute | solution.py:689
  33.6 7.4 %collective-permute-start = (f32[3,10,128]{2,1,0:T(8,128)S(1)}, f32[3,10,128]{2,1,0:T(8,128)S(1)}, u32[]{:S(2)}, u32[]{:S(2)}) collective-permute-start(f32[3,10,128]{2,1,0:T(8,128)S(1)} %get-tuple-element.58), channel_id=1, source_target_pairs={{0,1},{1,2},{2,3},{4,5},{5,6},{6,7},{8,9},{9,10},{10,11},{12,13},{... | collective-permute-start | bytes 46088 | tf_op jit(solution)/shard_map/ppermute | solution.py:688
  57.2 5.3 %collective-permute-start.3 = (f32[3,10,128]{2,1,0:T(8,128)S(1)}, f32[3,10,128]{2,1,0:T(8,128)S(1)}, u32[]{:S(2)}, u32[]{:S(2)}) collective-permute-start(f32[3,10,128]{2,1,0:T(8,128)S(1)} %get-tuple-element.55), channel_id=1, source_target_pairs={{1,0},{2,1},{3,2},{5,4},{6,5},{7,6},{9,8},{10,9},{11,10},{13,12},{... | collective-permute-start | bytes 46088 | tf_op jit(solution)/shard_map/ppermute | solution.py:689
  58.5 4.9 %collective-permute-start.2 = (f32[3,10,128]{2,1,0:T(8,128)S(1)}, f32[3,10,128]{2,1,0:T(8,128)S(1)}, u32[]{:S(2)}, u32[]{:S(2)}) collective-permute-start(f32[3,10,128]{2,1,0:T(8,128)S(1)} %get-tuple-element.56), channel_id=1, source_target_pairs={{0,1},{1,2},{2,3},{4,5},{5,6},{6,7},{8,9},{9,10},{10,11},{12,13},{... | collective-permute-start | bytes 46088 | tf_op jit(solution)/shard_map/ppermute | solution.py:688
  71.7 28.4 %copy-start.2 = (f32[16,62,256]{2,0,1:T(8,128)S(1)}, f32[16,62,256]{2,0,1:T(8,128)}, u32[]{:S(2)}) copy-start(f32[16,62,256]{2,0,1:T(8,128)} %param.14) | copy-start | bytes 3047428
  71.7 28.4 %copy-start.3 = (f32[16,62,256]{2,0,1:T(8,128)S(1)}, f32[16,62,256]{2,0,1:T(8,128)}, u32[]{:S(2)}) copy-start(f32[16,62,256]{2,0,1:T(8,128)} %param.15) | copy-start | bytes 3047428

commit v2 on v1

--- a/solution.py
+++ b/solution.py
@@ -59,9 +59,9 @@
 W_ID = 0
 W_CAM = 1
 W_SH = 10
-W_CA = 26
-W_CB = 32
-W_CC = 38
+WORDS = 32
+
+LOG2_E = math.log2(math.e)
 
 SMEM = pltpu.SMEM
 VMEM = pltpu.VMEM
@@ -144,13 +144,7 @@
     ]
     size = jnp.sqrt(normal[0] * normal[0] + normal[1] * normal[1] + normal[2] * normal[2])
     basis = harmonics(normal[0] / size, normal[1] / size, normal[2] / size)
-    pairs = [(0, 0), (0, 1), (0, 2), (1, 1), (1, 2), (2, 2)]
-
-    def product(p, q):
-        return [p[i] * q[i] if i == j else p[i] * q[j] + p[j] * q[i] for i, j in pairs]
-
     words = [jnp.full((1, ASK), -1.0, jnp.float32)] + cam + basis
-    words = words + product(a, a) + product(a, b) + product(b, b)
     lane = lax.broadcasted_iota(jnp.int32, (1, ASK), 1)
     row = jnp.zeros((1, ASK), jnp.float32)
     for i, word in enumerate(words):
@@ -168,6 +162,19 @@
             block = list_ref[0, 0, i]
             local = jnp.full((1, ASK), block % BLK_DEV, jnp.int32).astype(jnp.float32)
             out_ref[block // BLK_DEV] = jnp.where(lane == 0, local, row)
+
+
+PAIRS = [(0, 0), (0, 1), (0, 2), (1, 1), (1, 2), (2, 2)]
+
+
+def products(word):
+    a = [word(W_CAM + i) for i in range(3)]
+    b = [word(W_CAM + 3 + i) for i in range(3)]
+
+    def product(p, q):
+        return [p[i] * q[i] if i == j else p[i] * q[j] + p[j] * q[i] for i, j in PAIRS]
+
+    return product(a, a), product(a, b), product(b, b)
 
 
 def component(ref, c):
@@ -209,24 +216,27 @@
     shape_ref[6] = opacity
 
 
-def listed_slots(ask_ref, order_ref):
+def listed_slots(word_ref, order_ref):
     def look(s, found):
         order_ref[found] = s
-        return found + jnp.where(ask_ref[s, 0, W_ID] >= 0.0, 1, 0)
+        return found + jnp.where(word_ref[W_ID, s] >= 0.0, 1, 0)
 
     return lax.fori_loop(0, DEVICES, look, 0, unroll=8)
 
 
-def records_kernel(ask_ref, g_ref, shape_ref, out_ref, order_ref, count_ref):
-    count = listed_slots(ask_ref, order_ref)
-    count_ref[0] = count
+def records_kernel(ask_ref, g_ref, shape_ref, out_ref, turned_ref, word_ref, order_ref, sem):
+    turned_ref[...] = ask_ref[...].reshape(DEVICES, ASK).T[0:WORDS]
+    copy = pltpu.make_async_copy(turned_ref, word_ref, sem)
+    copy.start()
+    copy.wait()
+    count = listed_slots(word_ref, order_ref)
 
     def slot(n, carry):
         s = order_ref[n]
-        k = ask_ref[s, 0, W_ID].astype(jnp.int32)
+        k = word_ref[W_ID, s].astype(jnp.int32)
 
         def word(i):
-            return ask_ref[s, 0, i]
+            return word_ref[i, s]
 
         def comp(i):
             return g_ref[i, pl.ds(k, 1), :]
@@ -245,10 +255,10 @@
                 + word(W_CAM + 6 + p),
             )
         shapes = [shape_ref[i, pl.ds(k, 1), :] for i in range(6)]
-        for p, (at, extra) in enumerate(((W_CA, 0.3), (W_CB, 0.0), (W_CC, 0.3))):
-            total = word(at) * shapes[0]
+        for p, (factor, extra) in enumerate(zip(products(word), (0.3, 0.0, 0.3))):
+            total = factor[0] * shapes[0]
             for i in range(1, 6):
-                total = total + word(at + i) * shapes[i]
+                total = total + factor[i] * shapes[i]
             put(2 + p, total + extra)
         put(5, shape_ref[6, pl.ds(k, 1), :])
         basis = [word(W_SH + q) for q in range(16)]
@@ -265,20 +275,22 @@
 def pixel_rows(row_base):
     px = lax.broadcasted_iota(jnp.int32, (ROWS, COLS), 1).astype(jnp.float32) + 0.5
     py = lax.broadcasted_iota(jnp.int32, (ROWS, COLS), 0).astype(jnp.float32) + 0.5
-    return px, py + row_base.astype(jnp.float32)
+    py = py + row_base.astype(jnp.float32)
+    return px[0:8], (py[0:8], py[8:16])
 
 
 def row_of(ref, p, i):
-    return jnp.broadcast_to(ref[p, pl.ds(i, 1), :], (ROWS, COLS))
+    return jnp.broadcast_to(ref[p, pl.ds(i, 1), :], (8, COLS))
 
 
 def alpha_of(table, i, px, py):
     dx = px - row_of(table, 0, i)
-    dy = py - row_of(table, 1, i)
-    power = row_of(table, 2, i) * dx * dx + dy * (
-        row_of(table, 3, i) * dx + row_of(table, 4, i) * dy
-    )
-    return row_of(table, 5, i) * jnp.exp(power)
+    slope = row_of(table, 3, i) * dx
+    level = row_of(table, 2, i) * dx * dx
+    bend, peak, middle = row_of(table, 4, i), row_of(table, 5, i), row_of(table, 1, i)
+    return [
+        peak * jnp.exp2(level + dy * (slope + bend * dy)) for dy in (py[0] - middle, py[1] - middle)
+    ]
 
 
 def render_kernel(
@@ -288,6 +300,7 @@
     base_ref,
     got_ref,
     pred_ref,
+    send_ref,
     compact_ref,
     table_ref,
     alpha_ref,
@@ -311,9 +324,9 @@
     forms = [
         compact_ref[0],
         compact_ref[1],
-        -0.5 * cc / det,
-        cb / det,
-        -0.5 * ca / det,
+        (-0.5 * LOG2_E) * cc / det,
+        LOG2_E * cb / det,
+        (-0.5 * LOG2_E) * ca / det,
         compact_ref[5],
         compact_ref[6],
         compact_ref[7],
@@ -325,22 +338,30 @@
     px, py = pixel_rows(base_ref[0])
 
     def blend(i, carry):
-        trans, red, green, blue = carry
-        alpha = alpha_of(table_ref, i, px, py)
-        weight = alpha * trans
-        alpha_ref[i] = alpha
-        weight_ref[i] = weight
-        return (
-            trans - weight,
-            red + weight * row_of(table_ref, 6, i),
-            green + weight * row_of(table_ref, 7, i),
-            blue + weight * row_of(table_ref, 8, i),
-        )
-
-    zero = jnp.zeros((ROWS, COLS), jnp.float32)
-    done = lax.fori_loop(0, GAUSS, blend, (zero + 1.0, zero, zero, zero), unroll=16)
+        alphas = alpha_of(table_ref, i, px, py)
+        colours = [row_of(table_ref, 6 + ch, i) for ch in range(3)]
+        after = []
+        for half, alpha in enumerate(alphas):
+            trans, *sums = carry[half]
+            weight = alpha * trans
+            rows = pl.ds(8 * half, 8)
+            alpha_ref[i, rows, :] = alpha
+            weight_ref[i, rows, :] = weight
+            after.append(
+                (trans - weight, *[a + weight * c for a, c in zip(sums, colours)])
+            )
+        return tuple(after)
+
+    zero = jnp.zeros((8, COLS), jnp.float32)
+    start = (zero + 1.0, zero, zero, zero)
+    done = lax.fori_loop(0, GAUSS, blend, (start, start), unroll=16)
+    even = base_ref[0] % (2 * ROWS) == 0
     for ch in range(3):
-        pred_ref[ch] = done[1 + ch]
+        pred = jnp.concatenate([done[0][1 + ch], done[1][1 + ch]], axis=0)
+        pred_ref[ch] = pred
+        low, top = pred[ROWS - HALO :], pred[:HALO]
+        send_ref[0, ch] = jnp.where(even, low, top)
+        send_ref[1, ch] = jnp.where(even, top, low)
 
 
 def ssim_value(mean_x, mean_y, square_x, square_y, cross_xy):
@@ -356,7 +377,8 @@
     return jnp.dot(a, b, precision=HIGHEST_MODE, preferred_element_type=jnp.float32)
 
 
-def extended(mine, before, after):
+def extended(mine, even, one, two):
+    before, after = jnp.where(even, two, one), jnp.where(even, one, two)
     rest = jnp.zeros((EXT - ROWS - 2 * HALO, COLS), jnp.float32)
     return jnp.concatenate([before, mine, after, rest], axis=0)
 
@@ -366,18 +388,22 @@
     return [exact_dot(first, wide[EXT * m : EXT * (m + 1)]) for m in range(len(maps))]
 
 
-def target_kernel(target_ref, before_ref, after_ref, first_ref, across_ref, ext_ref, maps_ref):
+def target_kernel(
+    base_ref, target_ref, one_ref, two_ref, first_ref, across_ref, ext_ref, maps_ref
+):
+    even = base_ref[0] % (2 * ROWS) == 0
     first, across = first_ref[...], across_ref[...]
     for ch in range(3):
-        y = extended(target_ref[ch], before_ref[ch], after_ref[ch])
+        y = extended(target_ref[ch], even, one_ref[ch], two_ref[ch])
         ext_ref[ch] = y
         maps_ref[ch, 0], maps_ref[ch, 1] = smoothed([y, y * y], first, across)
 
 
 def loss_gradient(
-    base, pred_ref, before_ref, after_ref, target_ref, maps_ref, first_ref, second_ref, across_ref
+    base, pred_ref, one_ref, two_ref, target_ref, maps_ref, first_ref, second_ref, across_ref
 ):
     first, second, across = first_ref[...], second_ref[...], across_ref[...]
+    even = base % (2 * ROWS) == 0
     row = lax.broadcasted_iota(jnp.int32, (32, COLS), 0)
     image_row = row + base - 5
     inside = (image_row >= 0) & (image_row < IMG_ROWS) & (row < ROWS + 10)
@@ -385,7 +411,7 @@
     slopes = []
     for ch in range(3):
         pred = pred_ref[ch]
-        x, y = extended(pred, before_ref[ch], after_ref[ch]), target_ref[ch]
+        x, y = extended(pred, even, one_ref[ch], two_ref[ch]), target_ref[ch]
         mean, square, cross = smoothed([x, x * x, x * y], first, across)
         smooth = [mean, maps_ref[ch, 0], square, maps_ref[ch, 1], cross]
         value, pullback = jax.vjp(ssim_value, *smooth)
@@ -417,8 +443,8 @@
     end_ref,
     base_ref,
     pred_ref,
-    before_ref,
-    after_ref,
+    one_ref,
+    two_ref,
     target_ref,
     maps_ref,
     first_ref,
@@ -430,6 +456,7 @@
     alpha_ref,
     weight_ref,
     out_ref,
+    power_ref,
     part_ref,
     moment_ref,
     grad_ref,
@@ -437,8 +464,8 @@
     total, slopes = loss_gradient(
         base_ref[0],
         pred_ref,
-        before_ref,
-        after_ref,
+        one_ref,
+        two_ref,
         target_ref,
         maps_ref,
         first_ref,
@@ -459,53 +486,64 @@
         return carry
 
     lax.fori_loop(0, count_ref[0, 0], clear, 0)
-    px, py = pixel_rows(base_ref[0])
-
-    def fold(value):
-        return value[0:8] + value[8:16]
+    px, unused_py = pixel_rows(base_ref[0])
+    middle = (base_ref[0] + ROWS // 2).astype(jnp.float32)
+    slopes = [[slope[0:8], slope[8:16]] for slope in slopes]
 
     def reverse(step, behind):
-        for half in range(UNROLL - 1, -1, -1):
-            chunk = GAUSS // 8 - UNROLL * (step + 1) + half
+        for part in range(UNROLL - 1, -1, -1):
+            chunk = GAUSS // 8 - UNROLL * (step + 1) + part
             for r in range(7, -1, -1):
                 i = chunk * 8 + r
-                alpha = alpha_ref[i]
-                weight = weight_ref[i]
-                seen = (
-                    row_of(table_ref, 6, i) * slopes[0]
-                    + row_of(table_ref, 7, i) * slopes[1]
-                    + row_of(table_ref, 8, i) * slopes[2]
-                )
-                ahead = seen - behind
-                behind = behind + alpha * ahead
-                d_power = weight * ahead
-                dy = py - row_of(table_ref, 1, i)
-                d_row = d_power * dy
-                part_ref[half, 0, pl.ds(8 * r, 8), :] = fold(d_power)
-                part_ref[half, 1, pl.ds(8 * r, 8), :] = fold(d_row)
-                part_ref[half, 2, pl.ds(8 * r, 8), :] = fold(d_row * dy)
+                colours = [row_of(table_ref, 6 + ch, i) for ch in range(3)]
+                weights, after = [], []
+                for half in range(2):
+                    rows = pl.ds(8 * half, 8)
+                    weight = weight_ref[i, rows, :]
+                    seen = (
+                        colours[0] * slopes[0][half]
+                        + colours[1] * slopes[1][half]
+                        + colours[2] * slopes[2][half]
+                    )
+                    ahead = seen - behind[half]
+                    after.append(behind[half] + alpha_ref[i, rows, :] * ahead)
+                    power_ref[part, pl.ds(16 * r + 8 * half, 8), :] = weight * ahead
+                    weights.append(weight)
+                behind = after
                 for ch in range(3):
-                    part_ref[half, 3 + ch, pl.ds(8 * r, 8), :] = fold(weight * slopes[ch])
-            sums = []
-            for p in range(6):
-                piece = part_ref[half, p, pl.ds(0, 8, stride=8), :]
-                for s in range(1, 8):
-                    piece = piece + part_ref[half, p, pl.ds(s, 8, stride=8), :]
-                sums.append(piece)
+                    part_ref[part, ch, pl.ds(8 * r, 8), :] = (
+                        weights[0] * slopes[ch][0] + weights[1] * slopes[ch][1]
+                    )
+            plain = level = bend = None
+            for s in range(8):
+                upper = power_ref[part, pl.ds(s, 8, stride=16), :]
+                lower = power_ref[part, pl.ds(15 - s, 8, stride=16), :]
+                offset = 7.5 - s
+                total, tilt = upper + lower, (lower - upper) * offset
+                round_ = total * (offset * offset)
+                plain = total if s == 0 else plain + total
+                level = tilt if s == 0 else level + tilt
+                bend = round_ if s == 0 else bend + round_
             here = pl.ds(pl.multiple_of(chunk * 8, 8), 8)
-            dx = px[0:8] - table_ref[0, here, :]
-            first_x = sums[0] * dx
-            moment_ref[0, here, :] = sums[0]
+            dx = px - table_ref[0, here, :]
+            rise = middle - table_ref[1, here, :]
+            first_x = plain * dx
+            first_y = level + rise * plain
+            moment_ref[0, here, :] = plain
             moment_ref[1, here, :] = first_x
             moment_ref[2, here, :] = first_x * dx
-            moment_ref[3, here, :] = sums[1]
-            moment_ref[4, here, :] = sums[1] * dx
-            moment_ref[5, here, :] = sums[2]
+            moment_ref[3, here, :] = first_y
+            moment_ref[4, here, :] = first_y * dx
+            moment_ref[5, here, :] = bend + rise * (level + first_y)
             for ch in range(3):
-                moment_ref[6 + ch, here, :] = sums[3 + ch]
-        return behind
-
-    lax.fori_loop(0, GAUSS // 8 // UNROLL, reverse, jnp.zeros((ROWS, COLS), jnp.float32))
+                piece = part_ref[part, ch, pl.ds(0, 8, stride=8), :]
+                for s in range(1, 8):
+                    piece = piece + part_ref[part, ch, pl.ds(s, 8, stride=8), :]
+                moment_ref[6 + ch, here, :] = piece
+        return tuple(behind)
+
+    nothing = jnp.zeros((8, COLS), jnp.float32)
+    lax.fori_loop(0, GAUSS // 8 // UNROLL, reverse, (nothing, nothing))
     seg = seg_ref[...].astype(jnp.bfloat16)
 
     def over_tile(value):
@@ -547,9 +585,7 @@
 
 
 def update_kernel(
-    order_ref,
-    count_ref,
-    ask_ref,
+    word_ref,
     kept_ref,
     g_ref,
     one_ref,
@@ -565,6 +601,7 @@
     new_two_ref,
     grad_ref,
     shape_ref,
+    order_ref,
     done_sem,
 ):
     rates = [float(rate) / BIAS_FIRST for rate in learning_rates()]
@@ -594,14 +631,14 @@
     loss_ref[...] = jnp.sum(losses, axis=0) * (1.0 / (DEVICES * ROWS * COLS))
     grad_ref[...] = jnp.zeros(grad_ref.shape, jnp.float32)
     shape_ref[...] = jnp.zeros(shape_ref.shape, jnp.float32)
-    count = count_ref[0]
+    count = listed_slots(word_ref, order_ref)
 
     def slot(n, carry):
         s = order_ref[n]
-        k = ask_ref[s, 0, W_ID].astype(jnp.int32)
+        k = word_ref[W_ID, s].astype(jnp.int32)
 
         def word(i):
-            return ask_ref[s, 0, i]
+            return word_ref[i, s]
 
         here = pl.ds(k, 1)
 
@@ -614,9 +651,10 @@
             d_centre = word(W_CAM + c) * d[0] + word(W_CAM + 3 + c) * d[1]
             add(c, d_centre)
             add(3 + c, time * d_centre)
+        factors = products(word)
         for i in range(6):
             shape_ref[i, here, :] = shape_ref[i, here, :] + (
-                word(W_CA + i) * d[2] + word(W_CB + i) * d[3] + word(W_CC + i) * d[4]
+                factors[0][i] * d[2] + factors[1][i] * d[3] + factors[2][i] * d[4]
             )
         shape_ref[6, here, :] = shape_ref[6, here, :] + d[5]
         for q in range(16):
@@ -682,12 +720,10 @@
     return lax.all_to_all(slots, AXES, split_axis=0, concat_axis=0, tiled=True)
 
 
-def halo(array):
-    up = [(i, i + 1) for i in range(BANDS - 1)]
-    down = [(i + 1, i) for i in range(BANDS - 1)]
-    before = lax.ppermute(array[:, ROWS - HALO :], "band", up)
-    after = lax.ppermute(array[:, :HALO], "band", down)
-    return before, after
+def swapped(sent):
+    first = [(i, i ^ 1) for i in range(BANDS)]
+    second = [(i + 1, (i ^ 1) + 1) for i in range(BANDS - 2)]
+    return (lax.ppermute(sent[0], "band", first), lax.ppermute(sent[1], "band", second))
 
 
 def per_device(
@@ -725,37 +761,42 @@
         name="shapes",
     )(flat)
     asked, shapes, kept = lax.optimization_barrier((asked, shapes, kept))
-    records, order, count = pl.pallas_call(
+    records, words = pl.pallas_call(
         records_kernel,
-        in_specs=[spec(SMEM), spec(VMEM), spec(VMEM)],
-        out_specs=[spec(VMEM), spec(SMEM), spec(SMEM)],
-        out_shape=[
-            shaped(DEVICES, 1, RECORD),
-            jax.ShapeDtypeStruct((DEVICES + 1,), jnp.int32),
-            jax.ShapeDtypeStruct((1,), jnp.int32),
+        in_specs=[spec(VMEM)] * 3,
+        out_specs=[spec(VMEM)] * 2,
+        out_shape=[shaped(DEVICES, 1, RECORD), shaped(WORDS, DEVICES)],
+        scratch_shapes=[
+            SMEM((WORDS, DEVICES), jnp.float32),
+            SMEM((DEVICES + 1,), jnp.int32),
+            pltpu.SemaphoreType.DMA,
         ],
         compiler_params=params(16),
         name="records",
     )(asked, flat, shapes)
     records, target_band = lax.optimization_barrier((records, target_band))
     received = exchanged(records)
+    even = base[0] % (2 * ROWS) == 0
+    low, top = target_band[:, ROWS - HALO :], target_band[:, :HALO]
+    target_sent = (jnp.where(even, low, top), jnp.where(even, top, low))
     target_ext, target_maps = pl.pallas_call(
         target_kernel,
-        in_specs=[spec(VMEM)] * 5,
+        in_specs=[spec(SMEM)] + [spec(VMEM)] * 5,
         out_specs=[spec(VMEM)] * 2,
         out_shape=[shaped(3, EXT, COLS), shaped(3, 2, 32, COLS)],
         compiler_params=params(16),
         name="target",
-    )(target_band, *halo(target_band), first, across)
+    )(base, target_band, *swapped(target_sent), first, across)
     received, target_ext, target_maps = lax.optimization_barrier(
         (received, target_ext, target_maps)
     )
-    pred, compact, table, alpha, weight = pl.pallas_call(
+    pred, sent, compact, table, alpha, weight = pl.pallas_call(
         render_kernel,
         in_specs=[spec(SMEM)] * 4 + [spec(VMEM)],
-        out_specs=[spec(VMEM)] * 5,
+        out_specs=[spec(VMEM)] * 6,
         out_shape=[
             shaped(3, ROWS, COLS),
+            shaped(2, 3, HALO, COLS),
             shaped(9, TILES, GAUSS),
             shaped(9, GAUSS, COLS),
             shaped(GAUSS, ROWS, COLS),
@@ -764,7 +805,7 @@
         compiler_params=params(16),
         name="render",
     )(block_list, tile_start, tile_end, base, received)
-    pred_before, pred_after = halo(pred)
+    pred_one, pred_two = swapped(sent)
     seg = (np.arange(COLS)[None, :] // TILE == np.arange(TILES)[:, None]).astype(np.float32)
     outgoing = pl.pallas_call(
         backward_kernel,
@@ -772,7 +813,8 @@
         out_specs=spec(VMEM),
         out_shape=shaped(DEVICES, 1, SLOT),
         scratch_shapes=[
-            VMEM((UNROLL, 6, 64, COLS), jnp.float32),
+            VMEM((UNROLL, 128, COLS), jnp.float32),
+            VMEM((UNROLL, 3, 64, COLS), jnp.float32),
             VMEM((9, GAUSS, COLS), jnp.float32),
             VMEM((9, TILES, GAUSS), jnp.float32),
         ],
@@ -785,8 +827,8 @@
         tile_end,
         base,
         pred,
-        pred_before,
-        pred_after,
+        pred_one,
+        pred_two,
         target_ext,
         target_maps,
         first,
@@ -801,14 +843,18 @@
     incoming = exchanged(outgoing)
     loss, *flats = pl.pallas_call(
         update_kernel,
-        in_specs=[spec(SMEM)] * 3 + [spec(VMEM)] * 5,
+        in_specs=[spec(SMEM)] + [spec(VMEM)] * 5,
         out_specs=[spec(VMEM)] + [spec(pl.ANY)] * 4,
         out_shape=[shaped(1, 128)] + [shaped(COMPS, BLK_DEV, BLOCK)] * 4,
         scratch_shapes=[VMEM((COMPS, BLK_DEV, BLOCK), jnp.float32)] * 4
-        + [VMEM((7, BLK_DEV, BLOCK), jnp.float32), pltpu.SemaphoreType.DMA((16,))],
+        + [
+            VMEM((7, BLK_DEV, BLOCK), jnp.float32),
+            SMEM((DEVICES + 1,), jnp.int32),
+            pltpu.SemaphoreType.DMA((16,)),
+        ],
         compiler_params=params(16),
         name="update",
-    )(order, count, asked, kept, flat, flat_one, flat_two, incoming)
+    )(words, kept, flat, flat_one, flat_two, incoming)
     new_params, new_one, new_two, gradient = [jnp.transpose(a, (1, 0, 2)) for a in flats]
     return (new_params, new_one, new_two, loss[0, 0], gradient)
 

time: 107 us -> 103 us (0.963)
  starting transfers between devices: 26.7 us -> 23.3 us
  Pallas kernels: 24.3 us -> 22.6 us
    ppermute x4, starting transfers between devices: 10.6 us -> 7.59 us  [the longest x2 6.26 us: swapped(): lax.ppermute(sent[0], 'band', first)]
    ppermute x4, waiting for transfers between devices: 4.29 us -> 7.14 us  [the longest x2 7.14 us: swapped(): lax.ppermute(sent[0], 'band', first)]
    all_to_all x2, waiting for transfers between devices: 19.5 us -> 17.3 us  [exchanged(): return lax.all_to_all(slots, AXES, split_axis=0, concat_axis=0, tiled=True)]
    pallas_call x3, Pallas kernels: 10.1 us -> 8.66 us  [the longest x1 4.91 us: per_device(): pl.pallas_call(update_kernel, in_specs=[spec(SMEM)] + [spec(VMEM)] * 5, o...]
where the time goes in v2:
time: 103 us; the launch traced here: 102 us
  blocking collectives  29.1 us (28%)
  waiting for transfers between devices  24.5 us (24%)
  starting transfers between devices  23.3 us (23%)
  Pallas kernels  22.6 us (22%)
  between operations  1.48 us (1%)
  local copies, waits for them, and re-layouts  1.28 us (1%)
    all_to_all x1, blocking collectives, exchanged(): return lax.all_to_all(slots, AXES, split_axis=0, concat_axis=0, tiled=True)  29.1 us
    all_to_all x2, waiting for transfers between devices, exchanged(): return lax.all_to_all(slots, AXES, split_axis=0, concat_axis=0, tiled=True)  17.3 us
    all_to_all x2, starting transfers between devices, exchanged(): return lax.all_to_all(slots, AXES, split_axis=0, concat_axis=0, tiled=True)  15.7 us
    pallas_call x1, Pallas kernels, per_device(): pl.pallas_call(backward_kernel, in_specs=[spec(SMEM)] * 5 + [spec(VMEM)]...  8.2 us
    ppermute x2, waiting for transfers between devices, swapped(): lax.ppermute(sent[0], 'band', first)  7.14 us
    ppermute x2, starting transfers between devices, swapped(): lax.ppermute(sent[0], 'band', first)  6.26 us
    pallas_call x1, Pallas kernels, per_device(): pl.pallas_call(update_kernel, in_specs=[spec(SMEM)] + [spec(VMEM)] * 5, o...  4.91 us
    pallas_call x1, Pallas kernels, per_device(): pl.pallas_call(render_kernel, in_specs=[spec(SMEM)] * 4 + [spec(VMEM)], o...  4.06 us
  transfers between devices with their start and end apart: 6, of which 4 were waited for; matrix products, arithmetic and copies ran while one was open for 0% of the time, Pallas kernels for 1%

profile of v2, /device:TPU:1, one launch (start us, length us, event | category | flops | bytes accessed | tf_op | source)
XLA Modules:
  0.0 102.2 jit_solution(8948347183434017964)
XLA Ops:
  1.3 1.6 %request.1 = f32[128,1,128]{2,1,0:T(1,128)} custom-call(s32[1,1,16]{2,1,0:T(1,128)} %list_ref.5, s32[1,1]{1,0:T(1,128)S(6)} %copy.18.count_ref, f32[1,9]{1,0:T(1,128)} %cam_ref.1), custom_call_target="tpu_custom_call" | custom-call | tf_op jit(solution)/shard_map/request/pallas_call | solution.py:746
  2.9 11.5 %all-to-all-start = ((f32[128,1,128]{2,1,0:T(1,128)}), f32[128,1,128]{2,1,0:T(1,128)S(1)}, u32[]{:S(2)}, u32[]{:S(2)}) async-start(f32[128,1,128]{2,1,0:T(1,128)} %request.1), calls=%async_computation | async-start | bytes 131072 | tf_op jit(solution)/shard_map/all_to_all | solution.py:720
  14.4 0.0 copy-start
  14.4 1.2 %copy-done = f32[16,62,256]{2,0,1:T(8,128)S(1)} copy-done((f32[16,62,256]{2,0,1:T(8,128)S(1)}, f32[16,62,256]{2,0,1:T(8,128)}, u32[]{:S(2)}) %copy-start) | copy-done | bytes 1015832
  15.7 0.0 copy-start.1
  15.7 0.1 shapes.1
  15.7 8.3 %all-to-all-done.ask_ref = f32[128,1,128]{2,1,0:T(1,128)S(1)} async-done(((f32[128,1,128]{2,1,0:T(1,128)}), f32[128,1,128]{2,1,0:T(1,128)S(1)}, u32[]{:S(2)}, u32[]{:S(2)}) %all-to-all-start) | async-done | bytes 65568 | tf_op jit(solution)/shard_map/all_to_all | solution.py:720
  24.0 0.0 copy-done.1
  24.0 3.0 %records.1 = (f32[128,1,2304]{2,1,0:T(1,128)}, f32[32,128]{1,0:T(8,128)S(1)}) custom-call(f32[128,1,128]{2,1,0:T(1,128)S(1)} %all-to-all-done.ask_ref, f32[62,16,256]{2,1,0:T(8,128)S(1)} %bitcast.16, f32[7,16,256]{2,1,0:T(8,128)S(1)} %get-tuple-element.33.shape_ref), custom_call_target="tpu_custom_call" | custom-call | tf_op jit(solution)/shard_map/records/pallas_call | solution.py:764
  27.0 0.0 copy-start.5
  27.0 0.0 copy-start.4
  27.0 0.0 copy-start.6
  27.0 0.0 copy-start.8
  27.0 0.0 copy-start.10
  27.0 0.0 copy-start.11
  27.0 4.2 %all-to-all-start.1 = ((f32[128,1,2304]{2,1,0:T(1,128)}), f32[128,1,2304]{2,1,0:T(1,128)S(1)}, u32[]{:S(2)}, u32[]{:S(2)}) async-start(f32[128,1,2304]{2,1,0:T(1,128)} %get-tuple-element.37), calls=%async_computation.1 | async-start | bytes 2359296 | tf_op jit(solution)/shard_map/all_to_all | solution.py:720
  31.2 0.0 copy-start.7
  31.2 0.0 copy-start.9
  31.3 0.0 copy-done.5
  31.3 0.7 collective-permute-start.1
  32.0 4.4 %collective-permute-start = (f32[3,10,128]{2,1,0:T(8,128)S(1)}, f32[3,10,128]{2,1,0:T(8,128)S(1)}, u32[]{:S(2)}, u32[]{:S(2)}) collective-permute-start(f32[3,10,128]{2,1,0:T(8,128)S(1)} %get-tuple-element.58), channel_id=1, source_target_pairs={{0,1},{1,0},{2,3},{3,2},{4,5},{5,4},{6,7},{7,6},{8,9},{9,8},{10,11... | collective-permute-start | bytes 46088 | tf_op jit(solution)/shard_map/ppermute | solution.py:726
  36.3 0.0 collective-permute-done.1.two_ref
  36.3 5.9 %collective-permute-done.one_ref = f32[3,10,128]{2,1,0:T(8,128)S(1)} collective-permute-done((f32[3,10,128]{2,1,0:T(8,128)S(1)}, f32[3,10,128]{2,1,0:T(8,128)S(1)}, u32[]{:S(2)}, u32[]{:S(2)}) %collective-permute-start) | collective-permute-done | bytes 15392 | tf_op jit(solution)/shard_map/ppermute | solution.py:726
  42.3 0.0 copy-done.4
  42.3 0.0 copy-done.6
  42.3 0.8 target.1
  43.1 9.1 %all-to-all-done.1.got_ref = f32[128,1,2304]{2,1,0:T(1,128)S(1)} async-done(((f32[128,1,2304]{2,1,0:T(1,128)}), f32[128,1,2304]{2,1,0:T(1,128)S(1)}, u32[]{:S(2)}, u32[]{:S(2)}) %all-to-all-start.1) | async-done | bytes 1179680 | tf_op jit(solution)/shard_map/all_to_all | solution.py:720
  52.1 0.0 copy-done.8
  52.1 0.0 copy-done.10
  52.1 0.0 copy-done.11
  52.1 4.1 %render.1 = (f32[3,16,128]{2,1,0:T(8,128)S(1)}, f32[2,3,10,128]{3,2,1,0:T(8,128)S(1)}, f32[9,8,512]{2,1,0:T(8,128)S(1)}, f32[9,512,128]{2,1,0:T(8,128)S(1)}, f32...) custom-call(s32[1,1,16]{2,1,0:T(1,128)S(1)} %copy-done.8, s32[1,1,8]{2,1,0:T(1,128)S(1)} %copy-done.10, ...), custom_call_target="tpu_custom_call" | custom-call | tf_op jit(solution)/shard_map/render/pallas_call | solution.py:793
  56.2 0.7 collective-permute-start.3
  56.9 1.9 %collective-permute-start.2 = (f32[3,10,128]{2,1,0:T(8,128)S(1)}, f32[3,10,128]{2,1,0:T(8,128)S(1)}, u32[]{:S(2)}, u32[]{:S(2)}) collective-permute-start(f32[3,10,128]{2,1,0:T(8,128)S(1)} %get-tuple-element.56), channel_id=1, source_target_pairs={{0,1},{1,0},{2,3},{3,2},{4,5},{5,4},{6,7},{7,6},{8,9},{9,8},{10,11... | collective-permute-start | bytes 46088 | tf_op jit(solution)/shard_map/ppermute | solution.py:726
  58.8 0.0 collective-permute-done.3.two_ref
  58.8 1.2 %collective-permute-done.2.one_ref = f32[3,10,128]{2,1,0:T(8,128)S(1)} collective-permute-done((f32[3,10,128]{2,1,0:T(8,128)S(1)}, f32[3,10,128]{2,1,0:T(8,128)S(1)}, u32[]{:S(2)}, u32[]{:S(2)}) %collective-permute-start.2) | collective-permute-done | bytes 15392 | tf_op jit(solution)/shard_map/ppermute | solution.py:726
  60.0 0.0 copy-done.7
  60.0 0.0 copy-done.9
  60.0 8.2 %backward.1 = f32[128,1,2432]{2,1,0:T(1,128)S(1)} custom-call(s32[1,1,16]{2,1,0:T(1,128)S(1)} %copy-done.8, s32[1,1]{1,0:T(1,128)S(6)} %copy.18.count_ref, s32[1,1,8]{2,1,0:T(1,128)S(1)} %copy-done.10, s32[1,1,8]{2,1,0:T(1,128)S(1)} %copy-done.11, s32[1]{0:T(128)} %bitcast.3.base_ref, f32[3,16,128]{2,1,0:T(8,128)S(1)} %get-tuple-element.42.pred_ref, ...), custom_call_target="tpu_custom_call" | custom-call | tf_op jit(solution)/shard_map/backward/pallas_call | solution.py:810
  68.2 0.0 copy-start.2
  68.2 0.0 copy-start.3
  68.2 29.1 %all_to_all.15.got_ref = f32[128,1,2432]{2,1,0:T(1,128)S(1)} all-to-all(f32[128,1,2432]{2,1,0:T(1,128)S(1)} %backward.1), channel_id=1, replica_groups=mesh['view'=32,'band'=4] {'view','band'}, dimensions={0} | all-to-all | bytes 2490368 | tf_op jit(solution)/shard_map/all_to_all | solution.py:720
  97.3 0.0 copy-done.2
  97.3 0.0 copy-done.3
  97.3 4.9 %update.1 = (f32[1,128]{1,0:T(1,128)}, f32[62,16,256]{2,1,0:T(8,128)}, f32[62,16,256]{2,1,0:T(8,128)}, f32[62,16,256]{2,1,0:T(8,128)}, f32[62,16,256]{2,1,0:T(8,128)}) custom-call(f32[32,128]{1,0:T(8,128)S(1)} %get-tuple-element.34.word_ref, f32[18,16,256]{2,1,0:T(8,128)S(1)} %get-tuple-element.35.kept_ref, f32[62,16,256]{2,1,0:T(8,128)S(1)} %bitcast.17, ...), custom_call_target="tpu_custom_call" | custom-call | tf_op jit(solution)/shard_map/update/pallas_call | solution.py:844
  (2 shorter events, 0.0 us)
Async XLA Ops:
  2.9 21.1 %all-to-all-start = ((f32[128,1,128]{2,1,0:T(1,128)}), f32[128,1,128]{2,1,0:T(1,128)S(1)}, u32[]{:S(2)}, u32[]{:S(2)}) async-start(f32[128,1,128]{2,1,0:T(1,128)} %request.1), calls=%async_computation | async-start | bytes 131072 | tf_op jit(solution)/shard_map/all_to_all | solution.py:720
  14.4 1.2 %copy-start = (f32[16,62,256]{2,0,1:T(8,128)S(1)}, f32[16,62,256]{2,0,1:T(8,128)}, u32[]{:S(2)}) copy-start(f32[16,62,256]{2,0,1:T(8,128)} %param.13) | copy-start | bytes 3047428
  15.7 8.3 %copy-start.1 = (f32[16,62,256]{2,0,1:T(8,128)S(1)}, f32[16,62,256]{2,0,1:T(8,128)}, u32[]{:S(2)}) copy-start(f32[16,62,256]{2,0,1:T(8,128)} %param.13) | copy-start | bytes 3047428
  27.0 4.3 %copy-start.5 = (f32[1,3,16,128]{3,2,1,0:T(8,128)S(1)}, f32[1,3,16,128]{3,2,1,0:T(8,128)}, u32[]{:S(2)}) copy-start(f32[1,3,16,128]{3,2,1,0:T(8,128)} %param.17) | copy-start | bytes 73732
  27.0 15.3 %copy-start.4 = (f32[128,128]{1,0:T(8,128)S(1)}, f32[128,128]{1,0:T(8,128)}, u32[]{:S(2)}) copy-start(f32[128,128]{1,0:T(8,128)} %constant.29.clone.across_ref) | copy-start | bytes 196612
  27.0 15.3 %copy-start.6 = (f32[32,40]{1,0:T(8,128)S(1)}, f32[32,40]{1,0:T(8,128)}, u32[]{:S(2)}) copy-start(f32[32,40]{1,0:T(8,128)} %constant.28.clone.first_ref) | copy-start | bytes 15364
  27.0 25.1 %copy-start.8 = (s32[1,1,16]{2,1,0:T(1,128)S(1)}, s32[1,1,16]{2,1,0:T(1,128)}, u32[]{:S(2)}) copy-start(s32[1,1,16]{2,1,0:T(1,128)} %list_ref.5) | copy-start | bytes 196
  27.0 25.1 %copy-start.10 = (s32[1,1,8]{2,1,0:T(1,128)S(1)}, s32[1,1,8]{2,1,0:T(1,128)}, u32[]{:S(2)}) copy-start(s32[1,1,8]{2,1,0:T(1,128)} %start_ref.3) | copy-start | bytes 100
  27.0 25.1 %copy-start.11 = (s32[1,1,8]{2,1,0:T(1,128)S(1)}, s32[1,1,8]{2,1,0:T(1,128)}, u32[]{:S(2)}) copy-start(s32[1,1,8]{2,1,0:T(1,128)} %end_ref.3) | copy-start | bytes 100
  27.0 25.1 %all-to-all-start.1 = ((f32[128,1,2304]{2,1,0:T(1,128)}), f32[128,1,2304]{2,1,0:T(1,128)S(1)}, u32[]{:S(2)}, u32[]{:S(2)}) async-start(f32[128,1,2304]{2,1,0:T(1,128)} %get-tuple-element.37), calls=%async_computation.1 | async-start | bytes 2359296 | tf_op jit(solution)/shard_map/all_to_all | solution.py:720
  31.2 28.8 %copy-start.7 = (f32[16,32]{1,0:T(8,128)S(1)}, f32[16,32]{1,0:T(8,128)}, u32[]{:S(2)}) copy-start(f32[16,32]{1,0:T(8,128)} %constant.30.clone.second_ref) | copy-start | bytes 6148
  31.2 28.8 %copy-start.9 = (f32[8,128]{1,0:T(8,128)S(1)}, f32[8,128]{1,0:T(8,128)}, u32[]{:S(2)}) copy-start(f32[8,128]{1,0:T(8,128)} %constant.31.clone.seg_ref) | copy-start | bytes 12292
  31.3 5.0 %collective-permute-start.1 = (f32[3,10,128]{2,1,0:T(8,128)S(1)}, f32[3,10,128]{2,1,0:T(8,128)S(1)}, u32[]{:S(2)}, u32[]{:S(2)}) collective-permute-start(f32[3,10,128]{2,1,0:T(8,128)S(1)} %get-tuple-element.57), channel_id=1, source_target_pairs={{1,2},{2,1},{5,6},{6,5},{9,10},{10,9},{13,14},{14,13},{17,18},{18,... | collective-permute-start | bytes 46088 | tf_op jit(solution)/shard_map/ppermute | solution.py:726
  32.0 10.3 %collective-permute-start = (f32[3,10,128]{2,1,0:T(8,128)S(1)}, f32[3,10,128]{2,1,0:T(8,128)S(1)}, u32[]{:S(2)}, u32[]{:S(2)}) collective-permute-start(f32[3,10,128]{2,1,0:T(8,128)S(1)} %get-tuple-element.58), channel_id=1, source_target_pairs={{0,1},{1,0},{2,3},{3,2},{4,5},{5,4},{6,7},{7,6},{8,9},{9,8},{10,11... | collective-permute-start | bytes 46088 | tf_op jit(solution)/shard_map/ppermute | solution.py:726
  56.2 2.6 %collective-permute-start.3 = (f32[3,10,128]{2,1,0:T(8,128)S(1)}, f32[3,10,128]{2,1,0:T(8,128)S(1)}, u32[]{:S(2)}, u32[]{:S(2)}) collective-permute-start(f32[3,10,128]{2,1,0:T(8,128)S(1)} %get-tuple-element.55), channel_id=1, source_target_pairs={{1,2},{2,1},{5,6},{6,5},{9,10},{10,9},{13,14},{14,13},{17,18},{18,... | collective-permute-start | bytes 46088 | tf_op jit(solution)/shard_map/ppermute | solution.py:726
  56.9 3.1 %collective-permute-start.2 = (f32[3,10,128]{2,1,0:T(8,128)S(1)}, f32[3,10,128]{2,1,0:T(8,128)S(1)}, u32[]{:S(2)}, u32[]{:S(2)}) collective-permute-start(f32[3,10,128]{2,1,0:T(8,128)S(1)} %get-tuple-element.56), channel_id=1, source_target_pairs={{0,1},{1,0},{2,3},{3,2},{4,5},{5,4},{6,7},{7,6},{8,9},{9,8},{10,11... | collective-permute-start | bytes 46088 | tf_op jit(solution)/shard_map/ppermute | solution.py:726
  68.2 29.1 %copy-start.2 = (f32[16,62,256]{2,0,1:T(8,128)S(1)}, f32[16,62,256]{2,0,1:T(8,128)}, u32[]{:S(2)}) copy-start(f32[16,62,256]{2,0,1:T(8,128)} %param.14) | copy-start | bytes 3047428
  68.2 29.1 %copy-start.3 = (f32[16,62,256]{2,0,1:T(8,128)S(1)}, f32[16,62,256]{2,0,1:T(8,128)}, u32[]{:S(2)}) copy-start(f32[16,62,256]{2,0,1:T(8,128)} %param.15) | copy-start | bytes 3047428

commit v3 on v2

--- a/solution.py
+++ b/solution.py
@@ -383,9 +383,12 @@
     return jnp.concatenate([before, mine, after, rest], axis=0)
 
 
-def smoothed(maps, first, across):
+def smoothed(maps, rows, across):
+    height = maps[0].shape[0]
     wide = exact_dot(jnp.concatenate(maps, axis=0), across)
-    return [exact_dot(first, wide[EXT * m : EXT * (m + 1)]) for m in range(len(maps))]
+    side = [wide[height * m : height * (m + 1)] for m in range(len(maps))]
+    done = exact_dot(rows, jnp.concatenate(side, axis=1))
+    return [done[:, COLS * m : COLS * (m + 1)] for m in range(len(maps))]
 
 
 def target_kernel(
@@ -393,10 +396,13 @@
 ):
     even = base_ref[0] % (2 * ROWS) == 0
     first, across = first_ref[...], across_ref[...]
+    maps = []
     for ch in range(3):
         y = extended(target_ref[ch], even, one_ref[ch], two_ref[ch])
         ext_ref[ch] = y
-        maps_ref[ch, 0], maps_ref[ch, 1] = smoothed([y, y * y], first, across)
+        maps = maps + [y, y * y]
+    for i, done in enumerate(smoothed(maps, first, across)):
+        maps_ref[i // 2, i % 2] = done
 
 
 def loss_gradient(
@@ -408,39 +414,41 @@
     image_row = row + base - 5
     inside = (image_row >= 0) & (image_row < IMG_ROWS) & (row < ROWS + 10)
     total = jnp.zeros((ROWS, COLS), jnp.float32)
-    slopes = []
+    maps = []
     for ch in range(3):
-        pred = pred_ref[ch]
-        x, y = extended(pred, even, one_ref[ch], two_ref[ch]), target_ref[ch]
-        mean, square, cross = smoothed([x, x * x, x * y], first, across)
+        x = extended(pred_ref[ch], even, one_ref[ch], two_ref[ch])
+        maps = maps + [x, x * x, x * target_ref[ch]]
+    maps = smoothed(maps, first, across)
+    values, adjoint = [], []
+    for ch in range(3):
+        mean, square, cross = maps[3 * ch : 3 * ch + 3]
         smooth = [mean, maps_ref[ch, 0], square, maps_ref[ch, 1], cross]
         value, pullback = jax.vjp(ssim_value, *smooth)
         parts = pullback(jnp.full_like(value, -SSIM_WEIGHT / 3.0))
-        adjoint = [jnp.where(inside, parts[m], 0.0) for m in (0, 2, 4)]
-        back = [exact_dot(second, part) for part in adjoint]
-        back = exact_dot(jnp.concatenate(back, axis=0), across)
-        target = y[HALO : HALO + ROWS]
+        values.append(value)
+        adjoint = adjoint + [jnp.where(inside, parts[m], 0.0) for m in (0, 2, 4)]
+    back = smoothed(adjoint, second, across)
+    slopes = []
+    for ch in range(3):
+        pred, target = pred_ref[ch], target_ref[ch, pl.ds(HALO, ROWS), :]
         error = pred - target
         sign = jnp.where(error > 0.0, 1.0, jnp.where(error < 0.0, -1.0, 0.0))
         slopes.append(
             ABS_WEIGHT / 3.0 * sign
-            + back[0:ROWS]
-            + 2.0 * pred * back[ROWS : 2 * ROWS]
-            + target * back[2 * ROWS : 3 * ROWS]
+            + back[3 * ch]
+            + 2.0 * pred * back[3 * ch + 1]
+            + target * back[3 * ch + 2]
         )
         total = total + (
             ABS_WEIGHT / 3.0 * jnp.abs(error)
-            + SSIM_WEIGHT / 3.0 * (1.0 - value[5 : 5 + ROWS])
+            + SSIM_WEIGHT / 3.0 * (1.0 - values[ch][5 : 5 + ROWS])
         )
     total = jnp.sum(jnp.sum(total, axis=1, keepdims=True), axis=0, keepdims=True)
     return total, slopes
 
 
 def backward_kernel(
-    list_ref,
-    count_ref,
-    start_ref,
-    end_ref,
+    lists_in,
     base_ref,
     pred_ref,
     one_ref,
@@ -460,9 +468,13 @@
     part_ref,
     moment_ref,
     grad_ref,
+    lists_ref,
+    lists_sem,
 ):
+    copy = pltpu.make_async_copy(lists_in, lists_ref, lists_sem)
+    copy.start()
     total, slopes = loss_gradient(
-        base_ref[0],
+        base_ref[0:1],
         pred_ref,
         one_ref,
         two_ref,
@@ -482,12 +494,13 @@
     lax.fori_loop(0, DEVICES, tell, 0, unroll=8)
 
     def clear(i, carry):
-        out_ref[list_ref[0, 0, i] // BLK_DEV, :, pl.ds(0, RECORD)] = empty
+        out_ref[lists_ref[0, i] // BLK_DEV, :, pl.ds(0, RECORD)] = empty
         return carry
 
-    lax.fori_loop(0, count_ref[0, 0], clear, 0)
-    px, unused_py = pixel_rows(base_ref[0])
-    middle = (base_ref[0] + ROWS // 2).astype(jnp.float32)
+    copy.wait()
+    lax.fori_loop(0, lists_ref[0, 32], clear, 0)
+    px = lax.broadcasted_iota(jnp.int32, (8, COLS), 1).astype(jnp.float32) + 0.5
+    middle = (base_ref[...] + ROWS // 2).astype(jnp.float32)
     slopes = [[slope[0:8], slope[8:16]] for slope in slopes]
 
     def reverse(step, behind):
@@ -570,12 +583,12 @@
     for ch in range(3):
         grad_ref[6 + ch] = m[6 + ch]
     for t in range(TILES):
-        first = start_ref[0, 0, t]
+        first = lists_ref[0, 16 + t]
         for j in range(TILE_MOST):
 
-            @pl.when(first + j < end_ref[0, 0, t])
+            @pl.when(first + j < lists_ref[0, 24 + t])
             def _(t=t, j=j, first=first):
-                owner = list_ref[0, 0, first + j] // BLK_DEV
+                owner = lists_ref[0, first + j] // BLK_DEV
                 for p in range(9):
                     lanes = pl.ds(p * BLOCK, BLOCK)
                     out_ref[owner, :, lanes] = (
@@ -585,7 +598,7 @@
 
 
 def update_kernel(
-    word_ref,
+    turned_ref,
     kept_ref,
     g_ref,
     one_ref,
@@ -601,9 +614,13 @@
     new_two_ref,
     grad_ref,
     shape_ref,
+    word_ref,
     order_ref,
+    word_sem,
     done_sem,
 ):
+    words = pltpu.make_async_copy(turned_ref, word_ref, word_sem)
+    words.start()
     rates = [float(rate) / BIAS_FIRST for rate in learning_rates()]
     copies = []
 
@@ -631,6 +648,7 @@
     loss_ref[...] = jnp.sum(losses, axis=0) * (1.0 / (DEVICES * ROWS * COLS))
     grad_ref[...] = jnp.zeros(grad_ref.shape, jnp.float32)
     shape_ref[...] = jnp.zeros(shape_ref.shape, jnp.float32)
+    words.wait()
     count = listed_slots(word_ref, order_ref)
 
     def slot(n, carry):
@@ -743,6 +761,11 @@
     ]
     first, second, across = tap_matrices()
     base = (lax.axis_index("band") * ROWS).astype(jnp.int32).reshape(1)
+    base_rows = jnp.broadcast_to(base.reshape(1, 1), (8, COLS))
+    lists = jnp.concatenate(
+        [block_list[0, 0], tile_start[0, 0], tile_end[0, 0], block_count[0]]
+        + [jnp.zeros((95,), jnp.int32)]
+    ).reshape(1, 128)
     request = pl.pallas_call(
         request_kernel,
         in_specs=[spec(SMEM)] * 3,
@@ -774,7 +797,9 @@
         compiler_params=params(16),
         name="records",
     )(asked, flat, shapes)
-    records, target_band = lax.optimization_barrier((records, target_band))
+    records, target_band, lists, base_rows = lax.optimization_barrier(
+        (records, target_band, lists, base_rows)
+    )
     received = exchanged(records)
     even = base[0] % (2 * ROWS) == 0
     low, top = target_band[:, ROWS - HALO :], target_band[:, :HALO]
@@ -809,7 +834,7 @@
     seg = (np.arange(COLS)[None, :] // TILE == np.arange(TILES)[:, None]).astype(np.float32)
     outgoing = pl.pallas_call(
         backward_kernel,
-        in_specs=[spec(SMEM)] * 5 + [spec(VMEM)] * 13,
+        in_specs=[spec(VMEM)] * 15,
         out_specs=spec(VMEM),
         out_shape=shaped(DEVICES, 1, SLOT),
         scratch_shapes=[
@@ -817,15 +842,14 @@
             VMEM((UNROLL, 3, 64, COLS), jnp.float32),
             VMEM((9, GAUSS, COLS), jnp.float32),
             VMEM((9, TILES, GAUSS), jnp.float32),
+            SMEM((1, 128), jnp.int32),
+            pltpu.SemaphoreType.DMA,
         ],
         compiler_params=params(16),
         name="backward",
     )(
-        block_list,
-        block_count,
-        tile_start,
-        tile_end,
-        base,
+        lists,
+        base_rows,
         pred,
         pred_one,
         pred_two,
@@ -843,13 +867,15 @@
     incoming = exchanged(outgoing)
     loss, *flats = pl.pallas_call(
         update_kernel,
-        in_specs=[spec(SMEM)] + [spec(VMEM)] * 5,
+        in_specs=[spec(VMEM)] * 6,
         out_specs=[spec(VMEM)] + [spec(pl.ANY)] * 4,
         out_shape=[shaped(1, 128)] + [shaped(COMPS, BLK_DEV, BLOCK)] * 4,
         scratch_shapes=[VMEM((COMPS, BLK_DEV, BLOCK), jnp.float32)] * 4
         + [
             VMEM((7, BLK_DEV, BLOCK), jnp.float32),
+            SMEM((WORDS, DEVICES), jnp.float32),
             SMEM((DEVICES + 1,), jnp.int32),
+            pltpu.SemaphoreType.DMA,
             pltpu.SemaphoreType.DMA((16,)),
         ],
         compiler_params=params(16),

time: 103 us -> 102 us (level)
  Pallas kernels: 22.6 us -> 21.5 us
    pallas_call x2, Pallas kernels: 13.1 us -> 12 us  [the longest x1 7.04 us: per_device(): pl.pallas_call(backward_kernel, in_specs=[spec(VMEM)] * 15, out_specs=spe...]
  transfers between devices with their start and end apart: 6 -> 6, of which waited for: 4 -> 4; matrix products, arithmetic and copies ran while one was open for 0% -> 1% of each run, Pallas kernels for 1% -> 1%
where the time goes in v3:
time: 102 us
  blocking collectives  29.1 us (29%)
  waiting for transfers between devices  23.8 us (23%)
  starting transfers between devices  23.4 us (23%)
  Pallas kernels  21.5 us (21%)
  local copies, waits for them, and re-layouts  2.12 us (2%)
  between operations  1.5 us (1%)
    all_to_all x1, blocking collectives, exchanged(): return lax.all_to_all(slots, AXES, split_axis=0, concat_axis=0, tiled=True)  29.1 us
    all_to_all x2, waiting for transfers between devices, exchanged(): return lax.all_to_all(slots, AXES, split_axis=0, concat_axis=0, tiled=True)  16.7 us
    all_to_all x2, starting transfers between devices, exchanged(): return lax.all_to_all(slots, AXES, split_axis=0, concat_axis=0, tiled=True)  15.9 us
    ppermute x2, waiting for transfers between devices, swapped(): lax.ppermute(sent[0], 'band', first)  7.14 us
    pallas_call x1, Pallas kernels, per_device(): pl.pallas_call(backward_kernel, in_specs=[spec(VMEM)] * 15, out_specs=spe...  7.04 us
    ppermute x2, starting transfers between devices, swapped(): lax.ppermute(sent[0], 'band', first)  6.17 us
    pallas_call x1, Pallas kernels, per_device(): pl.pallas_call(update_kernel, in_specs=[spec(VMEM)] * 6, out_specs=[spec(...  5 us
    pallas_call x1, Pallas kernels, per_device(): pl.pallas_call(render_kernel, in_specs=[spec(SMEM)] * 4 + [spec(VMEM)], o...  4.06 us
  transfers between devices with their start and end apart: 6, of which 4 were waited for; matrix products, arithmetic and copies ran while one was open for 1% of the time, Pallas kernels for 1%

profile of v3, /device:TPU:1, one launch (start us, length us, event | category | flops | bytes accessed | tf_op | source)
XLA Modules:
  0.0 101.5 jit_solution(6950608901559447682)
XLA Ops:
  1.3 1.6 %request.1 = f32[128,1,128]{2,1,0:T(1,128)} custom-call(s32[1,1,16]{2,1,0:T(1,128)} %list_ref.3, s32[1,1]{1,0:T(1,128)} %copy.18.count_ref, f32[1,9]{1,0:T(1,128)} %cam_ref.1), custom_call_target="tpu_custom_call" | custom-call | tf_op jit(solution)/shard_map/request/pallas_call | solution.py:769
  2.9 11.5 %all-to-all-start = ((f32[128,1,128]{2,1,0:T(1,128)}), f32[128,1,128]{2,1,0:T(1,128)S(1)}, u32[]{:S(2)}, u32[]{:S(2)}) async-start(f32[128,1,128]{2,1,0:T(1,128)} %request.1), calls=%async_computation | async-start | bytes 131072 | tf_op jit(solution)/shard_map/all_to_all | solution.py:738
  14.4 0.0 copy-start
  14.4 1.2 %copy-done = f32[16,62,256]{2,0,1:T(8,128)S(1)} copy-done((f32[16,62,256]{2,0,1:T(8,128)S(1)}, f32[16,62,256]{2,0,1:T(8,128)}, u32[]{:S(2)}) %copy-start) | copy-done | bytes 1015832
  15.6 0.0 copy-start.1
  15.6 0.1 shapes.1
  15.7 0.8 concatenate.3
  16.6 7.4 %all-to-all-done.ask_ref = f32[128,1,128]{2,1,0:T(1,128)S(1)} async-done(((f32[128,1,128]{2,1,0:T(1,128)}), f32[128,1,128]{2,1,0:T(1,128)S(1)}, u32[]{:S(2)}, u32[]{:S(2)}) %all-to-all-start) | async-done | bytes 65568 | tf_op jit(solution)/shard_map/all_to_all | solution.py:738
  24.0 0.0 copy-done.1
  24.0 3.2 %records.1 = (f32[128,1,2304]{2,1,0:T(1,128)}, f32[32,128]{1,0:T(8,128)S(1)}) custom-call(f32[128,1,128]{2,1,0:T(1,128)S(1)} %all-to-all-done.ask_ref, f32[62,16,256]{2,1,0:T(8,128)S(1)} %bitcast.22, f32[7,16,256]{2,1,0:T(8,128)S(1)} %get-tuple-element.35.shape_ref), custom_call_target="tpu_custom_call" | custom-call | tf_op jit(solution)/shard_map/records/pallas_call | solution.py:787
  27.2 0.0 copy-start.5
  27.2 0.0 copy-start.4
  27.2 0.0 copy-start.6
  27.2 0.0 copy-start.8
  27.2 0.0 copy-start.10
  27.2 0.0 copy-start.11
  27.2 4.4 %all-to-all-start.1 = ((f32[128,1,2304]{2,1,0:T(1,128)}), f32[128,1,2304]{2,1,0:T(1,128)S(1)}, u32[]{:S(2)}, u32[]{:S(2)}) async-start(f32[128,1,2304]{2,1,0:T(1,128)} %get-tuple-element.41), calls=%async_computation.1 | async-start | bytes 2359296 | tf_op jit(solution)/shard_map/all_to_all | solution.py:738
  31.7 0.0 copy-start.7
  31.7 0.0 copy-start.9
  31.7 0.0 copy-done.5
  31.7 0.7 collective-permute-start.1
  32.4 4.3 %collective-permute-start = (f32[3,10,128]{2,1,0:T(8,128)S(1)}, f32[3,10,128]{2,1,0:T(8,128)S(1)}, u32[]{:S(2)}, u32[]{:S(2)}) collective-permute-start(f32[3,10,128]{2,1,0:T(8,128)S(1)} %get-tuple-element.62), channel_id=1, source_target_pairs={{0,1},{1,0},{2,3},{3,2},{4,5},{5,4},{6,7},{7,6},{8,9},{9,8},{10,11... | collective-permute-start | bytes 46088 | tf_op jit(solution)/shard_map/ppermute | solution.py:744
  36.7 0.0 collective-permute-done.1.two_ref
  36.7 5.9 %collective-permute-done.one_ref = f32[3,10,128]{2,1,0:T(8,128)S(1)} collective-permute-done((f32[3,10,128]{2,1,0:T(8,128)S(1)}, f32[3,10,128]{2,1,0:T(8,128)S(1)}, u32[]{:S(2)}, u32[]{:S(2)}) %collective-permute-start) | collective-permute-done | bytes 15392 | tf_op jit(solution)/shard_map/ppermute | solution.py:744
  42.6 0.0 copy-done.4
  42.6 0.0 copy-done.6
  42.6 0.6 target.1
  43.2 9.3 %all-to-all-done.1.got_ref = f32[128,1,2304]{2,1,0:T(1,128)S(1)} async-done(((f32[128,1,2304]{2,1,0:T(1,128)}), f32[128,1,2304]{2,1,0:T(1,128)S(1)}, u32[]{:S(2)}, u32[]{:S(2)}) %all-to-all-start.1) | async-done | bytes 1179680 | tf_op jit(solution)/shard_map/all_to_all | solution.py:738
  52.5 0.0 copy-done.8
  52.5 0.0 copy-done.10
  52.5 0.0 copy-done.11
  52.5 4.1 %render.1 = (f32[3,16,128]{2,1,0:T(8,128)S(1)}, f32[2,3,10,128]{3,2,1,0:T(8,128)S(1)}, f32[9,8,512]{2,1,0:T(8,128)S(1)}, f32[9,512,128]{2,1,0:T(8,128)S(1)}, f32...) custom-call(s32[1,1,16]{2,1,0:T(1,128)S(1)} %copy-done.8, s32[1,1,8]{2,1,0:T(1,128)S(1)} %copy-done.10, ...), custom_call_target="tpu_custom_call" | custom-call | tf_op jit(solution)/shard_map/render/pallas_call | solution.py:818
  56.6 0.7 collective-permute-start.3
  57.2 1.9 %collective-permute-start.2 = (f32[3,10,128]{2,1,0:T(8,128)S(1)}, f32[3,10,128]{2,1,0:T(8,128)S(1)}, u32[]{:S(2)}, u32[]{:S(2)}) collective-permute-start(f32[3,10,128]{2,1,0:T(8,128)S(1)} %get-tuple-element.60), channel_id=1, source_target_pairs={{0,1},{1,0},{2,3},{3,2},{4,5},{5,4},{6,7},{7,6},{8,9},{9,8},{10,11... | collective-permute-start | bytes 46088 | tf_op jit(solution)/shard_map/ppermute | solution.py:744
  59.1 0.0 collective-permute-done.3.two_ref
  59.1 1.2 %collective-permute-done.2.one_ref = f32[3,10,128]{2,1,0:T(8,128)S(1)} collective-permute-done((f32[3,10,128]{2,1,0:T(8,128)S(1)}, f32[3,10,128]{2,1,0:T(8,128)S(1)}, u32[]{:S(2)}, u32[]{:S(2)}) %collective-permute-start.2) | collective-permute-done | bytes 15392 | tf_op jit(solution)/shard_map/ppermute | solution.py:744
  60.3 0.0 copy-done.7
  60.3 0.0 copy-done.9
  60.3 7.0 %backward.1 = f32[128,1,2432]{2,1,0:T(1,128)S(1)} custom-call(s32[1,128]{1,0:T(1,128)S(1)} %bitcast.31, s32[8,128]{1,0:T(8,128)S(1)} %broadcast_in_dim.9.base_ref, f32[3,16,128]{2,1,0:T(8,128)S(1)} %get-tuple-element.46.pred_ref, f32[3,10,128]{2,1,0:T(8,128)S(1)} %collective-permute-done.2.one_ref, f32[3,10,128]{2,1,0:T(8,128)S(1)} %collective-permute-done.3.two_ref, ...), custom_call_target="tpu_custom_call" | custom-call | tf_op jit(solution)/shard_map/backward/pallas_call | solution.py:835
  67.4 0.0 copy-start.2
  67.4 0.0 copy-start.3
  67.4 29.1 %all_to_all.15.got_ref = f32[128,1,2432]{2,1,0:T(1,128)S(1)} all-to-all(f32[128,1,2432]{2,1,0:T(1,128)S(1)} %backward.1), channel_id=1, replica_groups=mesh['view'=32,'band'=4] {'view','band'}, dimensions={0} | all-to-all | bytes 2490368 | tf_op jit(solution)/shard_map/all_to_all | solution.py:738
  96.5 0.0 copy-done.2
  96.5 0.0 copy-done.3
  96.5 5.0 %update.1 = (f32[1,128]{1,0:T(1,128)}, f32[62,16,256]{2,1,0:T(8,128)}, f32[62,16,256]{2,1,0:T(8,128)}, f32[62,16,256]{2,1,0:T(8,128)}, f32[62,16,256]{2,1,0:T(8,128)}) custom-call(f32[32,128]{1,0:T(8,128)S(1)} %get-tuple-element.36.turned_ref, f32[18,16,256]{2,1,0:T(8,128)S(1)} %get-tuple-element.37.kept_ref, f32[62,16,256]{2,1,0:T(8,128)S(1)} %bitcast.23, ...), custom_call_target="tpu_custom_call" | custom-call | tf_op jit(solution)/shard_map/update/pallas_call | solution.py:868
  (4 shorter events, 0.0 us)
Async XLA Ops:
  2.9 21.1 %all-to-all-start = ((f32[128,1,128]{2,1,0:T(1,128)}), f32[128,1,128]{2,1,0:T(1,128)S(1)}, u32[]{:S(2)}, u32[]{:S(2)}) async-start(f32[128,1,128]{2,1,0:T(1,128)} %request.1), calls=%async_computation | async-start | bytes 131072 | tf_op jit(solution)/shard_map/all_to_all | solution.py:738
  14.4 1.2 %copy-start = (f32[16,62,256]{2,0,1:T(8,128)S(1)}, f32[16,62,256]{2,0,1:T(8,128)}, u32[]{:S(2)}) copy-start(f32[16,62,256]{2,0,1:T(8,128)} %param.13) | copy-start | bytes 3047428
  15.6 8.3 %copy-start.1 = (f32[16,62,256]{2,0,1:T(8,128)S(1)}, f32[16,62,256]{2,0,1:T(8,128)}, u32[]{:S(2)}) copy-start(f32[16,62,256]{2,0,1:T(8,128)} %param.13) | copy-start | bytes 3047428
  27.2 4.5 %copy-start.5 = (f32[1,3,16,128]{3,2,1,0:T(8,128)S(1)}, f32[1,3,16,128]{3,2,1,0:T(8,128)}, u32[]{:S(2)}) copy-start(f32[1,3,16,128]{3,2,1,0:T(8,128)} %param.17) | copy-start | bytes 73732
  27.2 15.4 %copy-start.4 = (f32[128,128]{1,0:T(8,128)S(1)}, f32[128,128]{1,0:T(8,128)}, u32[]{:S(2)}) copy-start(f32[128,128]{1,0:T(8,128)} %constant.30.clone.across_ref) | copy-start | bytes 196612
  27.2 15.4 %copy-start.6 = (f32[32,40]{1,0:T(8,128)S(1)}, f32[32,40]{1,0:T(8,128)}, u32[]{:S(2)}) copy-start(f32[32,40]{1,0:T(8,128)} %constant.29.clone.first_ref) | copy-start | bytes 15364
  27.2 25.3 %copy-start.8 = (s32[1,1,16]{2,1,0:T(1,128)S(1)}, s32[1,1,16]{2,1,0:T(1,128)}, u32[]{:S(2)}) copy-start(s32[1,1,16]{2,1,0:T(1,128)} %list_ref.3) | copy-start | bytes 196
  27.2 25.3 %copy-start.10 = (s32[1,1,8]{2,1,0:T(1,128)S(1)}, s32[1,1,8]{2,1,0:T(1,128)}, u32[]{:S(2)}) copy-start(s32[1,1,8]{2,1,0:T(1,128)} %start_ref.1) | copy-start | bytes 100
  27.2 25.2 %copy-start.11 = (s32[1,1,8]{2,1,0:T(1,128)S(1)}, s32[1,1,8]{2,1,0:T(1,128)}, u32[]{:S(2)}) copy-start(s32[1,1,8]{2,1,0:T(1,128)} %end_ref.1) | copy-start | bytes 100
  27.2 25.2 %all-to-all-start.1 = ((f32[128,1,2304]{2,1,0:T(1,128)}), f32[128,1,2304]{2,1,0:T(1,128)S(1)}, u32[]{:S(2)}, u32[]{:S(2)}) async-start(f32[128,1,2304]{2,1,0:T(1,128)} %get-tuple-element.41), calls=%async_computation.1 | async-start | bytes 2359296 | tf_op jit(solution)/shard_map/all_to_all | solution.py:738
  31.7 28.7 %copy-start.7 = (f32[16,32]{1,0:T(8,128)S(1)}, f32[16,32]{1,0:T(8,128)}, u32[]{:S(2)}) copy-start(f32[16,32]{1,0:T(8,128)} %constant.31.clone.second_ref) | copy-start | bytes 6148
  31.7 28.7 %copy-start.9 = (f32[8,128]{1,0:T(8,128)S(1)}, f32[8,128]{1,0:T(8,128)}, u32[]{:S(2)}) copy-start(f32[8,128]{1,0:T(8,128)} %constant.32.clone.seg_ref) | copy-start | bytes 12292
  31.7 5.0 %collective-permute-start.1 = (f32[3,10,128]{2,1,0:T(8,128)S(1)}, f32[3,10,128]{2,1,0:T(8,128)S(1)}, u32[]{:S(2)}, u32[]{:S(2)}) collective-permute-start(f32[3,10,128]{2,1,0:T(8,128)S(1)} %get-tuple-element.61), channel_id=1, source_target_pairs={{1,2},{2,1},{5,6},{6,5},{9,10},{10,9},{13,14},{14,13},{17,18},{18,... | collective-permute-start | bytes 46088 | tf_op jit(solution)/shard_map/ppermute | solution.py:744
  32.4 10.2 %collective-permute-start = (f32[3,10,128]{2,1,0:T(8,128)S(1)}, f32[3,10,128]{2,1,0:T(8,128)S(1)}, u32[]{:S(2)}, u32[]{:S(2)}) collective-permute-start(f32[3,10,128]{2,1,0:T(8,128)S(1)} %get-tuple-element.62), channel_id=1, source_target_pairs={{0,1},{1,0},{2,3},{3,2},{4,5},{5,4},{6,7},{7,6},{8,9},{9,8},{10,11... | collective-permute-start | bytes 46088 | tf_op jit(solution)/shard_map/ppermute | solution.py:744
  56.6 2.6 %collective-permute-start.3 = (f32[3,10,128]{2,1,0:T(8,128)S(1)}, f32[3,10,128]{2,1,0:T(8,128)S(1)}, u32[]{:S(2)}, u32[]{:S(2)}) collective-permute-start(f32[3,10,128]{2,1,0:T(8,128)S(1)} %get-tuple-element.59), channel_id=1, source_target_pairs={{1,2},{2,1},{5,6},{6,5},{9,10},{10,9},{13,14},{14,13},{17,18},{18,... | collective-permute-start | bytes 46088 | tf_op jit(solution)/shard_map/ppermute | solution.py:744
  57.2 3.1 %collective-permute-start.2 = (f32[3,10,128]{2,1,0:T(8,128)S(1)}, f32[3,10,128]{2,1,0:T(8,128)S(1)}, u32[]{:S(2)}, u32[]{:S(2)}) collective-permute-start(f32[3,10,128]{2,1,0:T(8,128)S(1)} %get-tuple-element.60), channel_id=1, source_target_pairs={{0,1},{1,0},{2,3},{3,2},{4,5},{5,4},{6,7},{7,6},{8,9},{9,8},{10,11... | collective-permute-start | bytes 46088 | tf_op jit(solution)/shard_map/ppermute | solution.py:744
  67.4 29.1 %copy-start.2 = (f32[16,62,256]{2,0,1:T(8,128)S(1)}, f32[16,62,256]{2,0,1:T(8,128)}, u32[]{:S(2)}) copy-start(f32[16,62,256]{2,0,1:T(8,128)} %param.14) | copy-start | bytes 3047428
  67.4 29.1 %copy-start.3 = (f32[16,62,256]{2,0,1:T(8,128)S(1)}, f32[16,62,256]{2,0,1:T(8,128)}, u32[]{:S(2)}) copy-start(f32[16,62,256]{2,0,1:T(8,128)} %param.15) | copy-start | bytes 3047428

commit v4 on v3

--- a/solution.py
+++ b/solution.py
@@ -21,11 +21,12 @@
 TILE_MOST = 2
 GAUSS = TILE_MOST * BLOCK
 HALO = 10
-EXT = 40
+EXT = 48
+WIDE = 32
 RECORD = 9 * BLOCK
 SLOT = RECORD + 128
 ASK = 128
-UNROLL = 4
+UNROLL = 8
 KEPT = 18
 IMG_ROWS = BANDS * ROWS
 AXES = ("view", "band")
@@ -81,22 +82,14 @@
     return [raw_tap / tap_total for raw_tap in raw_taps]
 
 
-def tap_matrices():
+def across_matrix():
     taps = kernel_taps()
-    first = np.zeros((32, EXT), np.float32)
-    for r in range(ROWS + 10):
-        for o in range(11):
-            first[r, r + o] = taps[o]
-    second = np.zeros((ROWS, 32), np.float32)
-    for r in range(ROWS):
-        for o in range(11):
-            second[r, r + o] = taps[o]
     across = np.zeros((COLS, COLS), np.float32)
     for c in range(COLS):
         for o in range(11):
             if 0 <= c + o - 5 < COLS:
                 across[c + o - 5, c] = taps[o]
-    return first, second, across
+    return across
 
 
 def learning_rates():
@@ -221,7 +214,7 @@
         order_ref[found] = s
         return found + jnp.where(word_ref[W_ID, s] >= 0.0, 1, 0)
 
-    return lax.fori_loop(0, DEVICES, look, 0, unroll=8)
+    return lax.fori_loop(0, DEVICES, look, 0, unroll=32)
 
 
 def records_kernel(ask_ref, g_ref, shape_ref, out_ref, turned_ref, word_ref, order_ref, sem):
@@ -354,7 +347,7 @@
 
     zero = jnp.zeros((8, COLS), jnp.float32)
     start = (zero + 1.0, zero, zero, zero)
-    done = lax.fori_loop(0, GAUSS, blend, (start, start), unroll=16)
+    done = lax.fori_loop(0, GAUSS, blend, (start, start), unroll=32)
     even = base_ref[0] % (2 * ROWS) == 0
     for ch in range(3):
         pred = jnp.concatenate([done[0][1 + ch], done[1][1 + ch]], axis=0)
@@ -383,34 +376,45 @@
     return jnp.concatenate([before, mine, after, rest], axis=0)
 
 
-def smoothed(maps, rows, across):
+def smoothed(maps, rows_out, across, held_ref):
+    taps = kernel_taps()
     height = maps[0].shape[0]
-    wide = exact_dot(jnp.concatenate(maps, axis=0), across)
-    side = [wide[height * m : height * (m + 1)] for m in range(len(maps))]
-    done = exact_dot(rows, jnp.concatenate(side, axis=1))
-    return [done[:, COLS * m : COLS * (m + 1)] for m in range(len(maps))]
+    for m, value in enumerate(maps):
+        held_ref[pl.ds(height * m, height), :] = value
+    done = []
+    for m in range(len(maps)):
+
+        def shifted(o, m=m):
+            return held_ref[pl.ds(height * m + o, rows_out), :]
+
+        total = taps[5] * shifted(5)
+        for o in range(5):
+            total = total + taps[o] * (shifted(o) + shifted(10 - o))
+        done.append(total)
+    wide = exact_dot(jnp.concatenate(done, axis=0), across)
+    return [wide[rows_out * m : rows_out * (m + 1)] for m in range(len(maps))]
 
 
 def target_kernel(
-    base_ref, target_ref, one_ref, two_ref, first_ref, across_ref, ext_ref, maps_ref
+    base_ref, target_ref, one_ref, two_ref, across_ref, ext_ref, maps_ref, held_ref
 ):
     even = base_ref[0] % (2 * ROWS) == 0
-    first, across = first_ref[...], across_ref[...]
+    across = across_ref[...]
     maps = []
     for ch in range(3):
         y = extended(target_ref[ch], even, one_ref[ch], two_ref[ch])
         ext_ref[ch] = y
         maps = maps + [y, y * y]
-    for i, done in enumerate(smoothed(maps, first, across)):
+    for i, done in enumerate(smoothed(maps, WIDE, across, held_ref)):
         maps_ref[i // 2, i % 2] = done
 
 
 def loss_gradient(
-    base, pred_ref, one_ref, two_ref, target_ref, maps_ref, first_ref, second_ref, across_ref
+    base, pred_ref, one_ref, two_ref, target_ref, maps_ref, across_ref, held_ref
 ):
-    first, second, across = first_ref[...], second_ref[...], across_ref[...]
+    across = across_ref[...]
     even = base % (2 * ROWS) == 0
-    row = lax.broadcasted_iota(jnp.int32, (32, COLS), 0)
+    row = lax.broadcasted_iota(jnp.int32, (WIDE, COLS), 0)
     image_row = row + base - 5
     inside = (image_row >= 0) & (image_row < IMG_ROWS) & (row < ROWS + 10)
     total = jnp.zeros((ROWS, COLS), jnp.float32)
@@ -418,7 +422,7 @@
     for ch in range(3):
         x = extended(pred_ref[ch], even, one_ref[ch], two_ref[ch])
         maps = maps + [x, x * x, x * target_ref[ch]]
-    maps = smoothed(maps, first, across)
+    maps = smoothed(maps, WIDE, across, held_ref)
     values, adjoint = [], []
     for ch in range(3):
         mean, square, cross = maps[3 * ch : 3 * ch + 3]
@@ -427,7 +431,7 @@
         parts = pullback(jnp.full_like(value, -SSIM_WEIGHT / 3.0))
         values.append(value)
         adjoint = adjoint + [jnp.where(inside, parts[m], 0.0) for m in (0, 2, 4)]
-    back = smoothed(adjoint, second, across)
+    back = smoothed(adjoint, ROWS, across, held_ref)
     slopes = []
     for ch in range(3):
         pred, target = pred_ref[ch], target_ref[ch, pl.ds(HALO, ROWS), :]
@@ -455,8 +459,6 @@
     two_ref,
     target_ref,
     maps_ref,
-    first_ref,
-    second_ref,
     across_ref,
     seg_ref,
     compact_ref,
@@ -468,6 +470,7 @@
     part_ref,
     moment_ref,
     grad_ref,
+    held_ref,
     lists_ref,
     lists_sem,
 ):
@@ -480,9 +483,8 @@
         two_ref,
         target_ref,
         maps_ref,
-        first_ref,
-        second_ref,
         across_ref,
+        held_ref,
     )
     loss_row = jnp.broadcast_to(total, (1, 128))
     empty = jnp.zeros((1, RECORD), jnp.float32)
@@ -759,7 +761,7 @@
         jnp.transpose(a, (1, 0, 2))
         for a in (gaussians, first_moment, second_moment)
     ]
-    first, second, across = tap_matrices()
+    across = across_matrix()
     base = (lax.axis_index("band") * ROWS).astype(jnp.int32).reshape(1)
     base_rows = jnp.broadcast_to(base.reshape(1, 1), (8, COLS))
     lists = jnp.concatenate(
@@ -806,12 +808,13 @@
     target_sent = (jnp.where(even, low, top), jnp.where(even, top, low))
     target_ext, target_maps = pl.pallas_call(
         target_kernel,
-        in_specs=[spec(SMEM)] + [spec(VMEM)] * 5,
+        in_specs=[spec(SMEM)] + [spec(VMEM)] * 4,
         out_specs=[spec(VMEM)] * 2,
-        out_shape=[shaped(3, EXT, COLS), shaped(3, 2, 32, COLS)],
+        out_shape=[shaped(3, EXT, COLS), shaped(3, 2, WIDE, COLS)],
+        scratch_shapes=[VMEM((6 * EXT, COLS), jnp.float32)],
         compiler_params=params(16),
         name="target",
-    )(base, target_band, *swapped(target_sent), first, across)
+    )(base, target_band, *swapped(target_sent), across)
     received, target_ext, target_maps = lax.optimization_barrier(
         (received, target_ext, target_maps)
     )
@@ -834,7 +837,7 @@
     seg = (np.arange(COLS)[None, :] // TILE == np.arange(TILES)[:, None]).astype(np.float32)
     outgoing = pl.pallas_call(
         backward_kernel,
-        in_specs=[spec(VMEM)] * 15,
+        in_specs=[spec(VMEM)] * 13,
         out_specs=spec(VMEM),
         out_shape=shaped(DEVICES, 1, SLOT),
         scratch_shapes=[
@@ -842,6 +845,7 @@
             VMEM((UNROLL, 3, 64, COLS), jnp.float32),
             VMEM((9, GAUSS, COLS), jnp.float32),
             VMEM((9, TILES, GAUSS), jnp.float32),
+            VMEM((9 * EXT, COLS), jnp.float32),
             SMEM((1, 128), jnp.int32),
             pltpu.SemaphoreType.DMA,
         ],
@@ -855,8 +859,6 @@
         pred_two,
         target_ext,
         target_maps,
-        first,
-        second,
         across,
         seg,
         compact,

time: 102 us -> 100 us (0.980)
  Pallas kernels: 21.5 us -> 19.2 us
    pallas_call x2, Pallas kernels: 7.61 us -> 6.36 us  [the longest x1 6.09 us: per_device(): pl.pallas_call(backward_kernel, in_specs=[spec(VMEM)] * 13, out_specs=spe...]
  transfers between devices with their start and end apart: 6 -> 6, of which waited for: 4 -> 4; matrix products, arithmetic and copies ran while one was open for 1% -> 1% of each run, Pallas kernels for 1% -> 0%
where the time goes in v4:
time: 100 us; the launch traced here: 99.5 us
  blocking collectives  29.1 us (29%)
  waiting for transfers between devices  24.1 us (24%)
  starting transfers between devices  23.5 us (24%)
  Pallas kernels  19.2 us (19%)
  local copies, waits for them, and re-layouts  2.11 us (2%)
  between operations  1.49 us (1%)
    all_to_all x1, blocking collectives, exchanged(): return lax.all_to_all(slots, AXES, split_axis=0, concat_axis=0, tiled=True)  29.1 us
    all_to_all x2, waiting for transfers between devices, exchanged(): return lax.all_to_all(slots, AXES, split_axis=0, concat_axis=0, tiled=True)  17 us
    all_to_all x2, starting transfers between devices, exchanged(): return lax.all_to_all(slots, AXES, split_axis=0, concat_axis=0, tiled=True)  16 us
    ppermute x2, waiting for transfers between devices, swapped(): lax.ppermute(sent[0], 'band', first)  7.15 us
    ppermute x2, starting transfers between devices, swapped(): lax.ppermute(sent[0], 'band', first)  6.18 us
    pallas_call x1, Pallas kernels, per_device(): pl.pallas_call(backward_kernel, in_specs=[spec(VMEM)] * 13, out_specs=spe...  6.09 us
    pallas_call x1, Pallas kernels, per_device(): pl.pallas_call(update_kernel, in_specs=[spec(VMEM)] * 6, out_specs=[spec(...  4.52 us
    pallas_call x1, Pallas kernels, per_device(): pl.pallas_call(render_kernel, in_specs=[spec(SMEM)] * 4 + [spec(VMEM)], o...  3.83 us
  transfers between devices with their start and end apart: 6, of which 4 were waited for; matrix products, arithmetic and copies ran while one was open for 1% of the time, Pallas kernels for 0%

profile of v4, /device:TPU:1, one launch (start us, length us, event | category | flops | bytes accessed | tf_op | source)
XLA Modules:
  0.0 99.5 jit_solution(10897518535874924268)
XLA Ops:
  1.3 1.6 %request.1 = f32[128,1,128]{2,1,0:T(1,128)} custom-call(s32[1,1,16]{2,1,0:T(1,128)} %list_ref.3, s32[1,1]{1,0:T(1,128)} %copy.16.count_ref, f32[1,9]{1,0:T(1,128)} %cam_ref.1), custom_call_target="tpu_custom_call" | custom-call | tf_op jit(solution)/shard_map/request/pallas_call | solution.py:771
  2.9 11.5 %all-to-all-start = ((f32[128,1,128]{2,1,0:T(1,128)}), f32[128,1,128]{2,1,0:T(1,128)S(1)}, u32[]{:S(2)}, u32[]{:S(2)}) async-start(f32[128,1,128]{2,1,0:T(1,128)} %request.1), calls=%async_computation | async-start | bytes 131072 | tf_op jit(solution)/shard_map/all_to_all | solution.py:740
  14.4 0.0 copy-start
  14.5 1.2 %copy-done = f32[16,62,256]{2,0,1:T(8,128)S(1)} copy-done((f32[16,62,256]{2,0,1:T(8,128)S(1)}, f32[16,62,256]{2,0,1:T(8,128)}, u32[]{:S(2)}) %copy-start) | copy-done | bytes 1015832
  15.7 0.0 copy-start.1
  15.7 0.1 shapes.1
  15.8 0.8 concatenate.3
  16.6 7.4 %all-to-all-done.ask_ref = f32[128,1,128]{2,1,0:T(1,128)S(1)} async-done(((f32[128,1,128]{2,1,0:T(1,128)}), f32[128,1,128]{2,1,0:T(1,128)S(1)}, u32[]{:S(2)}, u32[]{:S(2)}) %all-to-all-start) | async-done | bytes 65568 | tf_op jit(solution)/shard_map/all_to_all | solution.py:740
  24.0 0.0 copy-done.1
  24.0 2.7 %records.1 = (f32[128,1,2304]{2,1,0:T(1,128)}, f32[32,128]{1,0:T(8,128)S(1)}) custom-call(f32[128,1,128]{2,1,0:T(1,128)S(1)} %all-to-all-done.ask_ref, f32[62,16,256]{2,1,0:T(8,128)S(1)} %bitcast.22, f32[7,16,256]{2,1,0:T(8,128)S(1)} %get-tuple-element.35.shape_ref), custom_call_target="tpu_custom_call" | custom-call | tf_op jit(solution)/shard_map/records/pallas_call | solution.py:789
  26.8 0.0 copy-start.5
  26.8 0.0 copy-start.4
  26.8 0.0 copy-start.6
  26.8 0.0 copy-start.8
  26.8 0.0 copy-start.9
  26.8 4.5 %all-to-all-start.1 = ((f32[128,1,2304]{2,1,0:T(1,128)}), f32[128,1,2304]{2,1,0:T(1,128)S(1)}, u32[]{:S(2)}, u32[]{:S(2)}) async-start(f32[128,1,2304]{2,1,0:T(1,128)} %get-tuple-element.41), calls=%async_computation.1 | async-start | bytes 2359296 | tf_op jit(solution)/shard_map/all_to_all | solution.py:740
  31.3 0.0 copy-start.7
  31.3 0.0 copy-done.5
  31.4 0.7 collective-permute-start.1
  32.0 4.3 %collective-permute-start = (f32[3,10,128]{2,1,0:T(8,128)S(1)}, f32[3,10,128]{2,1,0:T(8,128)S(1)}, u32[]{:S(2)}, u32[]{:S(2)}) collective-permute-start(f32[3,10,128]{2,1,0:T(8,128)S(1)} %get-tuple-element.62), channel_id=1, source_target_pairs={{0,1},{1,0},{2,3},{3,2},{4,5},{5,4},{6,7},{7,6},{8,9},{9,8},{10,11... | collective-permute-start | bytes 46088 | tf_op jit(solution)/shard_map/ppermute | solution.py:746
  36.3 0.0 collective-permute-done.1.two_ref
  36.3 5.9 %collective-permute-done.one_ref = f32[3,10,128]{2,1,0:T(8,128)S(1)} collective-permute-done((f32[3,10,128]{2,1,0:T(8,128)S(1)}, f32[3,10,128]{2,1,0:T(8,128)S(1)}, u32[]{:S(2)}, u32[]{:S(2)}) %collective-permute-start) | collective-permute-done | bytes 15392 | tf_op jit(solution)/shard_map/ppermute | solution.py:746
  42.3 0.0 copy-done.4
  42.3 0.3 target.1
  42.5 9.6 %all-to-all-done.1.got_ref = f32[128,1,2304]{2,1,0:T(1,128)S(1)} async-done(((f32[128,1,2304]{2,1,0:T(1,128)}), f32[128,1,2304]{2,1,0:T(1,128)S(1)}, u32[]{:S(2)}, u32[]{:S(2)}) %all-to-all-start.1) | async-done | bytes 1179680 | tf_op jit(solution)/shard_map/all_to_all | solution.py:740
  52.1 0.0 copy-done.6
  52.1 0.0 copy-done.8
  52.1 0.0 copy-done.9
  52.1 3.8 %render.1 = (f32[3,16,128]{2,1,0:T(8,128)S(1)}, f32[2,3,10,128]{3,2,1,0:T(8,128)S(1)}, f32[9,8,512]{2,1,0:T(8,128)S(1)}, f32[9,512,128]{2,1,0:T(8,128)S(1)}, f32...) custom-call(s32[1,1,16]{2,1,0:T(1,128)S(1)} %copy-done.6, s32[1,1,8]{2,1,0:T(1,128)S(1)} %copy-done.8, ...), custom_call_target="tpu_custom_call" | custom-call | tf_op jit(solution)/shard_map/render/pallas_call | solution.py:821
  56.0 0.7 collective-permute-start.3
  56.6 1.9 %collective-permute-start.2 = (f32[3,10,128]{2,1,0:T(8,128)S(1)}, f32[3,10,128]{2,1,0:T(8,128)S(1)}, u32[]{:S(2)}, u32[]{:S(2)}) collective-permute-start(f32[3,10,128]{2,1,0:T(8,128)S(1)} %get-tuple-element.60), channel_id=1, source_target_pairs={{0,1},{1,0},{2,3},{3,2},{4,5},{5,4},{6,7},{7,6},{8,9},{9,8},{10,11... | collective-permute-start | bytes 46088 | tf_op jit(solution)/shard_map/ppermute | solution.py:746
  58.5 0.0 collective-permute-done.3.two_ref
  58.5 1.2 %collective-permute-done.2.one_ref = f32[3,10,128]{2,1,0:T(8,128)S(1)} collective-permute-done((f32[3,10,128]{2,1,0:T(8,128)S(1)}, f32[3,10,128]{2,1,0:T(8,128)S(1)}, u32[]{:S(2)}, u32[]{:S(2)}) %collective-permute-start.2) | collective-permute-done | bytes 15392 | tf_op jit(solution)/shard_map/ppermute | solution.py:746
  59.7 0.0 copy-done.7
  59.8 6.1 %backward.1 = f32[128,1,2432]{2,1,0:T(1,128)S(1)} custom-call(s32[1,128]{1,0:T(1,128)S(1)} %bitcast.31, s32[8,128]{1,0:T(8,128)S(1)} %broadcast_in_dim.9.base_ref, f32[3,16,128]{2,1,0:T(8,128)S(1)} %get-tuple-element.46.pred_ref, f32[3,10,128]{2,1,0:T(8,128)S(1)} %collective-permute-done.2.one_ref, f32[3,10,128]{2,1,0:T(8,128)S(1)} %collective-permute-done.3.two_ref, ...), custom_call_target="tpu_custom_call" | custom-call | tf_op jit(solution)/shard_map/backward/pallas_call | solution.py:838
  65.8 0.0 copy-start.2
  65.9 0.0 copy-start.3
  65.9 29.1 %all_to_all.15.got_ref = f32[128,1,2432]{2,1,0:T(1,128)S(1)} all-to-all(f32[128,1,2432]{2,1,0:T(1,128)S(1)} %backward.1), channel_id=1, replica_groups=mesh['view'=32,'band'=4] {'view','band'}, dimensions={0} | all-to-all | bytes 2490368 | tf_op jit(solution)/shard_map/all_to_all | solution.py:740
  95.0 0.0 copy-done.2
  95.0 0.0 copy-done.3
  95.0 4.5 %update.1 = (f32[1,128]{1,0:T(1,128)}, f32[62,16,256]{2,1,0:T(8,128)}, f32[62,16,256]{2,1,0:T(8,128)}, f32[62,16,256]{2,1,0:T(8,128)}, f32[62,16,256]{2,1,0:T(8,128)}) custom-call(f32[32,128]{1,0:T(8,128)S(1)} %get-tuple-element.36.turned_ref, f32[18,16,256]{2,1,0:T(8,128)S(1)} %get-tuple-element.37.kept_ref, f32[62,16,256]{2,1,0:T(8,128)S(1)} %bitcast.23, ...), custom_call_target="tpu_custom_call" | custom-call | tf_op jit(solution)/shard_map/update/pallas_call | solution.py:870
  (4 shorter events, 0.0 us)
Async XLA Ops:
  2.9 21.1 %all-to-all-start = ((f32[128,1,128]{2,1,0:T(1,128)}), f32[128,1,128]{2,1,0:T(1,128)S(1)}, u32[]{:S(2)}, u32[]{:S(2)}) async-start(f32[128,1,128]{2,1,0:T(1,128)} %request.1), calls=%async_computation | async-start | bytes 131072 | tf_op jit(solution)/shard_map/all_to_all | solution.py:740
  14.4 1.2 %copy-start = (f32[16,62,256]{2,0,1:T(8,128)S(1)}, f32[16,62,256]{2,0,1:T(8,128)}, u32[]{:S(2)}) copy-start(f32[16,62,256]{2,0,1:T(8,128)} %param.11) | copy-start | bytes 3047428
  15.7 8.3 %copy-start.1 = (f32[16,62,256]{2,0,1:T(8,128)S(1)}, f32[16,62,256]{2,0,1:T(8,128)}, u32[]{:S(2)}) copy-start(f32[16,62,256]{2,0,1:T(8,128)} %param.11) | copy-start | bytes 3047428
  26.8 4.6 %copy-start.5 = (f32[1,3,16,128]{3,2,1,0:T(8,128)S(1)}, f32[1,3,16,128]{3,2,1,0:T(8,128)}, u32[]{:S(2)}) copy-start(f32[1,3,16,128]{3,2,1,0:T(8,128)} %param.15) | copy-start | bytes 73732
  26.8 15.5 %copy-start.4 = (f32[128,128]{1,0:T(8,128)S(1)}, f32[128,128]{1,0:T(8,128)}, u32[]{:S(2)}) copy-start(f32[128,128]{1,0:T(8,128)} %constant.25.clone.across_ref) | copy-start | bytes 196612
  26.8 25.3 %copy-start.6 = (s32[1,1,16]{2,1,0:T(1,128)S(1)}, s32[1,1,16]{2,1,0:T(1,128)}, u32[]{:S(2)}) copy-start(s32[1,1,16]{2,1,0:T(1,128)} %list_ref.3) | copy-start | bytes 196
  26.8 25.3 %copy-start.8 = (s32[1,1,8]{2,1,0:T(1,128)S(1)}, s32[1,1,8]{2,1,0:T(1,128)}, u32[]{:S(2)}) copy-start(s32[1,1,8]{2,1,0:T(1,128)} %start_ref.1) | copy-start | bytes 100
  26.8 25.3 %copy-start.9 = (s32[1,1,8]{2,1,0:T(1,128)S(1)}, s32[1,1,8]{2,1,0:T(1,128)}, u32[]{:S(2)}) copy-start(s32[1,1,8]{2,1,0:T(1,128)} %end_ref.1) | copy-start | bytes 100
  26.8 25.3 %all-to-all-start.1 = ((f32[128,1,2304]{2,1,0:T(1,128)}), f32[128,1,2304]{2,1,0:T(1,128)S(1)}, u32[]{:S(2)}, u32[]{:S(2)}) async-start(f32[128,1,2304]{2,1,0:T(1,128)} %get-tuple-element.41), calls=%async_computation.1 | async-start | bytes 2359296 | tf_op jit(solution)/shard_map/all_to_all | solution.py:740
  31.3 28.4 %copy-start.7 = (f32[8,128]{1,0:T(8,128)S(1)}, f32[8,128]{1,0:T(8,128)}, u32[]{:S(2)}) copy-start(f32[8,128]{1,0:T(8,128)} %constant.26.clone.seg_ref) | copy-start | bytes 12292
  31.4 5.0 %collective-permute-start.1 = (f32[3,10,128]{2,1,0:T(8,128)S(1)}, f32[3,10,128]{2,1,0:T(8,128)S(1)}, u32[]{:S(2)}, u32[]{:S(2)}) collective-permute-start(f32[3,10,128]{2,1,0:T(8,128)S(1)} %get-tuple-element.61), channel_id=1, source_target_pairs={{1,2},{2,1},{5,6},{6,5},{9,10},{10,9},{13,14},{14,13},{17,18},{18,... | collective-permute-start | bytes 46088 | tf_op jit(solution)/shard_map/ppermute | solution.py:746
  32.0 10.2 %collective-permute-start = (f32[3,10,128]{2,1,0:T(8,128)S(1)}, f32[3,10,128]{2,1,0:T(8,128)S(1)}, u32[]{:S(2)}, u32[]{:S(2)}) collective-permute-start(f32[3,10,128]{2,1,0:T(8,128)S(1)} %get-tuple-element.62), channel_id=1, source_target_pairs={{0,1},{1,0},{2,3},{3,2},{4,5},{5,4},{6,7},{7,6},{8,9},{9,8},{10,11... | collective-permute-start | bytes 46088 | tf_op jit(solution)/shard_map/ppermute | solution.py:746
  56.0 2.6 %collective-permute-start.3 = (f32[3,10,128]{2,1,0:T(8,128)S(1)}, f32[3,10,128]{2,1,0:T(8,128)S(1)}, u32[]{:S(2)}, u32[]{:S(2)}) collective-permute-start(f32[3,10,128]{2,1,0:T(8,128)S(1)} %get-tuple-element.59), channel_id=1, source_target_pairs={{1,2},{2,1},{5,6},{6,5},{9,10},{10,9},{13,14},{14,13},{17,18},{18,... | collective-permute-start | bytes 46088 | tf_op jit(solution)/shard_map/ppermute | solution.py:746
  56.6 3.1 %collective-permute-start.2 = (f32[3,10,128]{2,1,0:T(8,128)S(1)}, f32[3,10,128]{2,1,0:T(8,128)S(1)}, u32[]{:S(2)}, u32[]{:S(2)}) collective-permute-start(f32[3,10,128]{2,1,0:T(8,128)S(1)} %get-tuple-element.60), channel_id=1, source_target_pairs={{0,1},{1,0},{2,3},{3,2},{4,5},{5,4},{6,7},{7,6},{8,9},{9,8},{10,11... | collective-permute-start | bytes 46088 | tf_op jit(solution)/shard_map/ppermute | solution.py:746
  65.8 29.1 %copy-start.2 = (f32[16,62,256]{2,0,1:T(8,128)S(1)}, f32[16,62,256]{2,0,1:T(8,128)}, u32[]{:S(2)}) copy-start(f32[16,62,256]{2,0,1:T(8,128)} %param.12) | copy-start | bytes 3047428
  65.9 29.1 %copy-start.3 = (f32[16,62,256]{2,0,1:T(8,128)S(1)}, f32[16,62,256]{2,0,1:T(8,128)}, u32[]{:S(2)}) copy-start(f32[16,62,256]{2,0,1:T(8,128)} %param.13) | copy-start | bytes 3047428

commit v5 on v4

--- a/solution.py
+++ b/solution.py
@@ -292,6 +292,7 @@
     end_ref,
     base_ref,
     got_ref,
+    target_ref,
     pred_ref,
     send_ref,
     compact_ref,
@@ -352,9 +353,10 @@
     for ch in range(3):
         pred = jnp.concatenate([done[0][1 + ch], done[1][1 + ch]], axis=0)
         pred_ref[ch] = pred
-        low, top = pred[ROWS - HALO :], pred[:HALO]
-        send_ref[0, ch] = jnp.where(even, low, top)
-        send_ref[1, ch] = jnp.where(even, top, low)
+        for at, rows in ((ch, pred), (3 + ch, target_ref[ch])):
+            low, top = rows[ROWS - HALO :], rows[:HALO]
+            send_ref[0, at] = jnp.where(even, low, top)
+            send_ref[1, at] = jnp.where(even, top, low)
 
 
 def ssim_value(mean_x, mean_y, square_x, square_y, cross_xy):
@@ -395,22 +397,8 @@
     return [wide[rows_out * m : rows_out * (m + 1)] for m in range(len(maps))]
 
 
-def target_kernel(
-    base_ref, target_ref, one_ref, two_ref, across_ref, ext_ref, maps_ref, held_ref
-):
-    even = base_ref[0] % (2 * ROWS) == 0
-    across = across_ref[...]
-    maps = []
-    for ch in range(3):
-        y = extended(target_ref[ch], even, one_ref[ch], two_ref[ch])
-        ext_ref[ch] = y
-        maps = maps + [y, y * y]
-    for i, done in enumerate(smoothed(maps, WIDE, across, held_ref)):
-        maps_ref[i // 2, i % 2] = done
-
-
 def loss_gradient(
-    base, pred_ref, one_ref, two_ref, target_ref, maps_ref, across_ref, held_ref
+    base, pred_ref, one_ref, two_ref, target_ref, across_ref, held_ref
 ):
     across = across_ref[...]
     even = base % (2 * ROWS) == 0
@@ -421,20 +409,19 @@
     maps = []
     for ch in range(3):
         x = extended(pred_ref[ch], even, one_ref[ch], two_ref[ch])
-        maps = maps + [x, x * x, x * target_ref[ch]]
+        y = extended(target_ref[ch], even, one_ref[3 + ch], two_ref[3 + ch])
+        maps = maps + [x, y, x * x, y * y, x * y]
     maps = smoothed(maps, WIDE, across, held_ref)
     values, adjoint = [], []
     for ch in range(3):
-        mean, square, cross = maps[3 * ch : 3 * ch + 3]
-        smooth = [mean, maps_ref[ch, 0], square, maps_ref[ch, 1], cross]
-        value, pullback = jax.vjp(ssim_value, *smooth)
+        value, pullback = jax.vjp(ssim_value, *maps[5 * ch : 5 * ch + 5])
         parts = pullback(jnp.full_like(value, -SSIM_WEIGHT / 3.0))
         values.append(value)
         adjoint = adjoint + [jnp.where(inside, parts[m], 0.0) for m in (0, 2, 4)]
     back = smoothed(adjoint, ROWS, across, held_ref)
     slopes = []
     for ch in range(3):
-        pred, target = pred_ref[ch], target_ref[ch, pl.ds(HALO, ROWS), :]
+        pred, target = pred_ref[ch], target_ref[ch]
         error = pred - target
         sign = jnp.where(error > 0.0, 1.0, jnp.where(error < 0.0, -1.0, 0.0))
         slopes.append(
@@ -458,7 +445,6 @@
     one_ref,
     two_ref,
     target_ref,
-    maps_ref,
     across_ref,
     seg_ref,
     compact_ref,
@@ -482,7 +468,6 @@
         one_ref,
         two_ref,
         target_ref,
-        maps_ref,
         across_ref,
         held_ref,
     )
@@ -799,32 +784,15 @@
         compiler_params=params(16),
         name="records",
     )(asked, flat, shapes)
-    records, target_band, lists, base_rows = lax.optimization_barrier(
-        (records, target_band, lists, base_rows)
-    )
+    records, lists, base_rows = lax.optimization_barrier((records, lists, base_rows))
     received = exchanged(records)
-    even = base[0] % (2 * ROWS) == 0
-    low, top = target_band[:, ROWS - HALO :], target_band[:, :HALO]
-    target_sent = (jnp.where(even, low, top), jnp.where(even, top, low))
-    target_ext, target_maps = pl.pallas_call(
-        target_kernel,
-        in_specs=[spec(SMEM)] + [spec(VMEM)] * 4,
-        out_specs=[spec(VMEM)] * 2,
-        out_shape=[shaped(3, EXT, COLS), shaped(3, 2, WIDE, COLS)],
-        scratch_shapes=[VMEM((6 * EXT, COLS), jnp.float32)],
-        compiler_params=params(16),
-        name="target",
-    )(base, target_band, *swapped(target_sent), across)
-    received, target_ext, target_maps = lax.optimization_barrier(
-        (received, target_ext, target_maps)
-    )
     pred, sent, compact, table, alpha, weight = pl.pallas_call(
         render_kernel,
-        in_specs=[spec(SMEM)] * 4 + [spec(VMEM)],
+        in_specs=[spec(SMEM)] * 4 + [spec(VMEM)] * 2,
         out_specs=[spec(VMEM)] * 6,
         out_shape=[
             shaped(3, ROWS, COLS),
-            shaped(2, 3, HALO, COLS),
+            shaped(2, 6, HALO, COLS),
             shaped(9, TILES, GAUSS),
             shaped(9, GAUSS, COLS),
             shaped(GAUSS, ROWS, COLS),
@@ -832,12 +800,12 @@
         ],
         compiler_params=params(16),
         name="render",
-    )(block_list, tile_start, tile_end, base, received)
+    )(block_list, tile_start, tile_end, base, received, target_band)
     pred_one, pred_two = swapped(sent)
     seg = (np.arange(COLS)[None, :] // TILE == np.arange(TILES)[:, None]).astype(np.float32)
     outgoing = pl.pallas_call(
         backward_kernel,
-        in_specs=[spec(VMEM)] * 13,
+        in_specs=[spec(VMEM)] * 12,
         out_specs=spec(VMEM),
         out_shape=shaped(DEVICES, 1, SLOT),
         scratch_shapes=[
@@ -845,7 +813,7 @@
             VMEM((UNROLL, 3, 64, COLS), jnp.float32),
             VMEM((9, GAUSS, COLS), jnp.float32),
             VMEM((9, TILES, GAUSS), jnp.float32),
-            VMEM((9 * EXT, COLS), jnp.float32),
+            VMEM((15 * EXT, COLS), jnp.float32),
             SMEM((1, 128), jnp.int32),
             pltpu.SemaphoreType.DMA,
         ],
@@ -857,8 +825,7 @@
         pred,
         pred_one,
         pred_two,
-        target_ext,
-        target_maps,
+        target_band,
         across,
         seg,
         compact,

time: 100 us -> 99.4 us (level)
  blocking collectives: 29.1 us -> 53.8 us
  waiting for transfers between devices: 24.1 us -> 8.89 us
  starting transfers between devices: 23.5 us -> 14.1 us
    all_to_all x1 -> x2, blocking collectives: 29.1 us -> 53.8 us  [exchanged(): return lax.all_to_all(slots, AXES, split_axis=0, concat_axis=0, tiled=True)]
    all_to_all x2 -> x1, waiting for transfers between devices: 17 us -> 7.41 us  [exchanged(): return lax.all_to_all(slots, AXES, split_axis=0, concat_axis=0, tiled=True)]
    ppermute x2 -> x1, waiting for transfers between devices: 7.15 us -> 1.48 us  [swapped(): lax.ppermute(sent[0], 'band', first)]
    all_to_all x2 -> x1, starting transfers between devices: 16 us -> 11.5 us  [exchanged(): return lax.all_to_all(slots, AXES, split_axis=0, concat_axis=0, tiled=True)]
    ppermute x2 -> x1, starting transfers between devices: 6.18 us -> 1.89 us  [swapped(): lax.ppermute(sent[0], 'band', first)]
    pallas_call x3 -> x2, Pallas kernels: 10.2 us -> 10.3 us  [the longest x1 6.48 us: per_device(): pl.pallas_call(backward_kernel, in_specs=[spec(VMEM)] * 12, out_specs=spe...]
  transfers between devices with their start and end apart: 6 -> 3, of which waited for: 4 -> 2; matrix products, arithmetic and copies ran while one was open for 1% -> 1% of each run, Pallas kernels for 0% -> 0%
where the time goes in v5:
time: 99.4 us; the launch traced here: 98.9 us
  blocking collectives  53.8 us (54%)
  Pallas kernels  18.6 us (19%)
  starting transfers between devices  14.1 us (14%)
  waiting for transfers between devices  8.89 us (9%)
  local copies, waits for them, and re-layouts  2.11 us (2%)
  between operations  1.43 us (1%)
    all_to_all x2, blocking collectives, exchanged(): return lax.all_to_all(slots, AXES, split_axis=0, concat_axis=0, tiled=True)  53.8 us
    all_to_all x1, starting transfers between devices, exchanged(): return lax.all_to_all(slots, AXES, split_axis=0, concat_axis=0, tiled=True)  11.5 us
    all_to_all x1, waiting for transfers between devices, exchanged(): return lax.all_to_all(slots, AXES, split_axis=0, concat_axis=0, tiled=True)  7.41 us
    pallas_call x1, Pallas kernels, per_device(): pl.pallas_call(backward_kernel, in_specs=[spec(VMEM)] * 12, out_specs=spe...  6.48 us
    pallas_call x1, Pallas kernels, per_device(): pl.pallas_call(update_kernel, in_specs=[spec(VMEM)] * 6, out_specs=[spec(...  4.69 us
    pallas_call x1, Pallas kernels, per_device(): pl.pallas_call(render_kernel, in_specs=[spec(SMEM)] * 4 + [spec(VMEM)] *...  3.84 us
  transfers between devices with their start and end apart: 3, of which 2 were waited for; matrix products, arithmetic and copies ran while one was open for 1% of the time, Pallas kernels for 0%

profile of v5, /device:TPU:1, one launch (start us, length us, event | category | flops | bytes accessed | tf_op | source)
XLA Modules:
  0.0 98.9 jit_solution(6123813158276274197)
XLA Ops:
  1.3 1.7 %request.1 = f32[128,1,128]{2,1,0:T(1,128)} custom-call(s32[1,1,16]{2,1,0:T(1,128)} %list_ref.3, s32[1,1]{1,0:T(1,128)} %copy.16.count_ref, f32[1,9]{1,0:T(1,128)} %cam_ref.1), custom_call_target="tpu_custom_call" | custom-call | tf_op jit(solution)/shard_map/request/pallas_call | solution.py:756
  2.9 11.5 %all-to-all-start = ((f32[128,1,128]{2,1,0:T(1,128)}), f32[128,1,128]{2,1,0:T(1,128)S(1)}, u32[]{:S(2)}, u32[]{:S(2)}) async-start(f32[128,1,128]{2,1,0:T(1,128)} %request.1), calls=%async_computation | async-start | bytes 131072 | tf_op jit(solution)/shard_map/all_to_all | solution.py:725
  14.4 0.0 copy-start
  14.5 1.2 %copy-done = f32[16,62,256]{2,0,1:T(8,128)S(1)} copy-done((f32[16,62,256]{2,0,1:T(8,128)S(1)}, f32[16,62,256]{2,0,1:T(8,128)}, u32[]{:S(2)}) %copy-start) | copy-done | bytes 1015832
  15.7 0.0 copy-start.1
  15.7 0.1 shapes.1
  15.8 0.8 concatenate.3
  16.6 7.4 %all-to-all-done.ask_ref = f32[128,1,128]{2,1,0:T(1,128)S(1)} async-done(((f32[128,1,128]{2,1,0:T(1,128)}), f32[128,1,128]{2,1,0:T(1,128)S(1)}, u32[]{:S(2)}, u32[]{:S(2)}) %all-to-all-start) | async-done | bytes 65568 | tf_op jit(solution)/shard_map/all_to_all | solution.py:725
  24.0 0.0 copy-done.1
  24.0 1.9 %records.1 = (f32[128,1,2304]{2,1,0:T(1,128)S(1)}, f32[32,128]{1,0:T(8,128)S(1)}) custom-call(f32[128,1,128]{2,1,0:T(1,128)S(1)} %all-to-all-done.ask_ref, f32[62,16,256]{2,1,0:T(8,128)S(1)} %bitcast.22, f32[7,16,256]{2,1,0:T(8,128)S(1)} %get-tuple-element.29.shape_ref), custom_call_target="tpu_custom_call" | custom-call | tf_op jit(solution)/shard_map/records/pallas_call | solution.py:774
  25.9 0.0 copy-start.4
  25.9 0.0 copy-start.6
  25.9 0.0 copy-start.8
  25.9 0.0 copy-start.9
  25.9 24.8 %all_to_all.15.got_ref = f32[128,1,2304]{2,1,0:T(1,128)S(1)} all-to-all(f32[128,1,2304]{2,1,0:T(1,128)S(1)} %get-tuple-element.35), channel_id=1, replica_groups=mesh['view'=32,'band'=4] {'view','band'}, dimensions={0} | all-to-all | bytes 2359296 | tf_op jit(solution)/shard_map/all_to_all | solution.py:725
  50.7 0.0 copy-start.5
  50.7 0.0 copy-start.7
  50.7 0.0 copy-done.4
  50.7 0.0 copy-done.6
  50.7 0.0 copy-done.8
  50.7 0.0 copy-done.9
  50.8 3.8 %render.1 = (f32[3,16,128]{2,1,0:T(8,128)S(1)}, f32[2,6,10,128]{3,2,1,0:T(8,128)S(1)}, f32[9,8,512]{2,1,0:T(8,128)S(1)}, f32[9,512,128]{2,1,0:T(8,128)S(1)}, f32...) custom-call(s32[1,1,16]{2,1,0:T(1,128)S(1)} %copy-done.6, s32[1,1,8]{2,1,0:T(1,128)S(1)} %copy-done.8, ...), custom_call_target="tpu_custom_call" | custom-call | tf_op jit(solution)/shard_map/render/pallas_call | solution.py:789
  54.6 0.7 collective-permute-start.1
  55.3 1.9 %collective-permute-start = (f32[6,10,128]{2,1,0:T(8,128)S(1)}, f32[6,10,128]{2,1,0:T(8,128)S(1)}, u32[]{:S(2)}, u32[]{:S(2)}) collective-permute-start(f32[6,10,128]{2,1,0:T(8,128)S(1)} %get-tuple-element.48), channel_id=1, source_target_pairs={{0,1},{1,0},{2,3},{3,2},{4,5},{5,4},{6,7},{7,6},{8,9},{9,8},{10,11... | collective-permute-start | bytes 92168 | tf_op jit(solution)/shard_map/ppermute | solution.py:731
  57.2 0.0 collective-permute-done.1.two_ref
  57.2 1.5 %collective-permute-done.one_ref = f32[6,10,128]{2,1,0:T(8,128)S(1)} collective-permute-done((f32[6,10,128]{2,1,0:T(8,128)S(1)}, f32[6,10,128]{2,1,0:T(8,128)S(1)}, u32[]{:S(2)}, u32[]{:S(2)}) %collective-permute-start) | collective-permute-done | bytes 30752 | tf_op jit(solution)/shard_map/ppermute | solution.py:731
  58.7 0.0 copy-done.5
  58.7 0.0 copy-done.7
  58.7 6.5 %backward.1 = f32[128,1,2432]{2,1,0:T(1,128)S(1)} custom-call(s32[1,128]{1,0:T(1,128)S(1)} %bitcast.31, s32[8,128]{1,0:T(8,128)S(1)} %broadcast_in_dim.9.base_ref, f32[3,16,128]{2,1,0:T(8,128)S(1)} %get-tuple-element.36.pred_ref, f32[6,10,128]{2,1,0:T(8,128)S(1)} %collective-permute-done.one_ref, f32[6,10,128]{2,1,0:T(8,128)S(1)} %collective-permute-done.1.two_ref, ...), custom_call_target="tpu_custom_call" | custom-call | tf_op jit(solution)/shard_map/backward/pallas_call | solution.py:806
  65.2 0.0 copy-start.2
  65.2 0.0 copy-start.3
  65.2 29.0 %all_to_all.16.got_ref = f32[128,1,2432]{2,1,0:T(1,128)S(1)} all-to-all(f32[128,1,2432]{2,1,0:T(1,128)S(1)} %backward.1), channel_id=1, replica_groups=mesh['view'=32,'band'=4] {'view','band'}, dimensions={0} | all-to-all | bytes 2490368 | tf_op jit(solution)/shard_map/all_to_all | solution.py:725
  94.2 0.0 copy-done.2
  94.2 0.0 copy-done.3
  94.2 4.7 %update.1 = (f32[1,128]{1,0:T(1,128)}, f32[62,16,256]{2,1,0:T(8,128)}, f32[62,16,256]{2,1,0:T(8,128)}, f32[62,16,256]{2,1,0:T(8,128)}, f32[62,16,256]{2,1,0:T(8,128)}) custom-call(f32[32,128]{1,0:T(8,128)S(1)} %get-tuple-element.30.turned_ref, f32[18,16,256]{2,1,0:T(8,128)S(1)} %get-tuple-element.31.kept_ref, f32[62,16,256]{2,1,0:T(8,128)S(1)} %bitcast.23, ...), custom_call_target="tpu_custom_call" | custom-call | tf_op jit(solution)/shard_map/update/pallas_call | solution.py:837
  (3 shorter events, 0.0 us)
Async XLA Ops:
  2.9 21.1 %all-to-all-start = ((f32[128,1,128]{2,1,0:T(1,128)}), f32[128,1,128]{2,1,0:T(1,128)S(1)}, u32[]{:S(2)}, u32[]{:S(2)}) async-start(f32[128,1,128]{2,1,0:T(1,128)} %request.1), calls=%async_computation | async-start | bytes 131072 | tf_op jit(solution)/shard_map/all_to_all | solution.py:725
  14.4 1.2 %copy-start = (f32[16,62,256]{2,0,1:T(8,128)S(1)}, f32[16,62,256]{2,0,1:T(8,128)}, u32[]{:S(2)}) copy-start(f32[16,62,256]{2,0,1:T(8,128)} %param.11) | copy-start | bytes 3047428
  15.7 8.3 %copy-start.1 = (f32[16,62,256]{2,0,1:T(8,128)S(1)}, f32[16,62,256]{2,0,1:T(8,128)}, u32[]{:S(2)}) copy-start(f32[16,62,256]{2,0,1:T(8,128)} %param.11) | copy-start | bytes 3047428
  25.9 24.8 %copy-start.4 = (f32[1,3,16,128]{3,2,1,0:T(8,128)S(1)}, f32[1,3,16,128]{3,2,1,0:T(8,128)}, u32[]{:S(2)}) copy-start(f32[1,3,16,128]{3,2,1,0:T(8,128)} %param.15) | copy-start | bytes 73732
  25.9 24.8 %copy-start.6 = (s32[1,1,16]{2,1,0:T(1,128)S(1)}, s32[1,1,16]{2,1,0:T(1,128)}, u32[]{:S(2)}) copy-start(s32[1,1,16]{2,1,0:T(1,128)} %list_ref.3) | copy-start | bytes 196
  25.9 24.8 %copy-start.8 = (s32[1,1,8]{2,1,0:T(1,128)S(1)}, s32[1,1,8]{2,1,0:T(1,128)}, u32[]{:S(2)}) copy-start(s32[1,1,8]{2,1,0:T(1,128)} %start_ref.1) | copy-start | bytes 100
  25.9 24.8 %copy-start.9 = (s32[1,1,8]{2,1,0:T(1,128)S(1)}, s32[1,1,8]{2,1,0:T(1,128)}, u32[]{:S(2)}) copy-start(s32[1,1,8]{2,1,0:T(1,128)} %end_ref.1) | copy-start | bytes 100
  50.7 7.9 %copy-start.5 = (f32[128,128]{1,0:T(8,128)S(1)}, f32[128,128]{1,0:T(8,128)}, u32[]{:S(2)}) copy-start(f32[128,128]{1,0:T(8,128)} %constant.12.clone.across_ref) | copy-start | bytes 196612
  50.7 7.9 %copy-start.7 = (f32[8,128]{1,0:T(8,128)S(1)}, f32[8,128]{1,0:T(8,128)}, u32[]{:S(2)}) copy-start(f32[8,128]{1,0:T(8,128)} %constant.13.clone.seg_ref) | copy-start | bytes 12292
  54.6 2.6 %collective-permute-start.1 = (f32[6,10,128]{2,1,0:T(8,128)S(1)}, f32[6,10,128]{2,1,0:T(8,128)S(1)}, u32[]{:S(2)}, u32[]{:S(2)}) collective-permute-start(f32[6,10,128]{2,1,0:T(8,128)S(1)} %get-tuple-element.47), channel_id=1, source_target_pairs={{1,2},{2,1},{5,6},{6,5},{9,10},{10,9},{13,14},{14,13},{17,18},{18,... | collective-permute-start | bytes 92168 | tf_op jit(solution)/shard_map/ppermute | solution.py:731
  55.3 3.4 %collective-permute-start = (f32[6,10,128]{2,1,0:T(8,128)S(1)}, f32[6,10,128]{2,1,0:T(8,128)S(1)}, u32[]{:S(2)}, u32[]{:S(2)}) collective-permute-start(f32[6,10,128]{2,1,0:T(8,128)S(1)} %get-tuple-element.48), channel_id=1, source_target_pairs={{0,1},{1,0},{2,3},{3,2},{4,5},{5,4},{6,7},{7,6},{8,9},{9,8},{10,11... | collective-permute-start | bytes 92168 | tf_op jit(solution)/shard_map/ppermute | solution.py:731
  65.2 29.0 %copy-start.2 = (f32[16,62,256]{2,0,1:T(8,128)S(1)}, f32[16,62,256]{2,0,1:T(8,128)}, u32[]{:S(2)}) copy-start(f32[16,62,256]{2,0,1:T(8,128)} %param.12) | copy-start | bytes 3047428
  65.2 29.0 %copy-start.3 = (f32[16,62,256]{2,0,1:T(8,128)S(1)}, f32[16,62,256]{2,0,1:T(8,128)}, u32[]{:S(2)}) copy-start(f32[16,62,256]{2,0,1:T(8,128)} %param.13) | copy-start | bytes 3047428

commit v6 on v5

--- a/solution.py
+++ b/solution.py
@@ -209,6 +209,16 @@
     shape_ref[6] = opacity
 
 
+def each_listed(slot, count):
+    def pair(n, carry):
+        slot(2 * n, 0)
+        slot(2 * n + 1, 0)
+        return carry
+
+    lax.fori_loop(0, count // 2, pair, 0)
+    lax.fori_loop(2 * (count // 2), count, slot, 0)
+
+
 def listed_slots(word_ref, order_ref):
     def look(s, found):
         order_ref[found] = s
@@ -262,7 +272,7 @@
             put(6 + ch, colour + 0.5)
         return carry
 
-    lax.fori_loop(0, count, slot, 0)
+    each_listed(slot, count)
 
 
 def pixel_rows(row_base):
@@ -294,7 +304,8 @@
     got_ref,
     target_ref,
     pred_ref,
-    send_ref,
+    send_one_ref,
+    send_two_ref,
     compact_ref,
     table_ref,
     alpha_ref,
@@ -355,8 +366,8 @@
         pred_ref[ch] = pred
         for at, rows in ((ch, pred), (3 + ch, target_ref[ch])):
             low, top = rows[ROWS - HALO :], rows[:HALO]
-            send_ref[0, at] = jnp.where(even, low, top)
-            send_ref[1, at] = jnp.where(even, top, low)
+            send_one_ref[at] = jnp.where(even, low, top)
+            send_two_ref[at] = jnp.where(even, top, low)
 
 
 def ssim_value(mean_x, mean_y, square_x, square_y, cross_xy):
@@ -551,12 +562,20 @@
             seg, value, (((1,), (1,)), ((), ())), preferred_element_type=jnp.float32
         )
 
+    wide_seg = jnp.concatenate([seg, seg], axis=1)
     m = []
     for p in range(9):
         value = moment_ref[p]
         large = value.astype(jnp.bfloat16)
         small = (value - large.astype(jnp.float32)).astype(jnp.bfloat16)
-        m.append(over_tile(large) + over_tile(small))
+        m.append(
+            lax.dot_general(
+                wide_seg,
+                jnp.concatenate([large, small], axis=1),
+                (((1,), (1,)), ((), ())),
+                preferred_element_type=jnp.float32,
+            )
+        )
     ca, cb, cc = compact_ref[2], compact_ref[3], compact_ref[4]
     inverse = 1.0 / (ca * cc - cb * cb)
     d_inverse = -0.5 * cc * m[2] + cb * m[4] - 0.5 * ca * m[5]
@@ -668,7 +687,7 @@
                 add(14 + 3 * q + ch, basis * d[6 + ch])
         return carry
 
-    lax.fori_loop(0, count, slot, 0)
+    each_listed(slot, count)
     for low, high in ((14, 30), (30, 46), (46, COMPS)):
         finish(low, high)
     squares = [kept_ref[c] for c in range(3)]
@@ -725,10 +744,10 @@
     return lax.all_to_all(slots, AXES, split_axis=0, concat_axis=0, tiled=True)
 
 
-def swapped(sent):
+def swapped(one, two):
     first = [(i, i ^ 1) for i in range(BANDS)]
     second = [(i + 1, (i ^ 1) + 1) for i in range(BANDS - 2)]
-    return (lax.ppermute(sent[0], "band", first), lax.ppermute(sent[1], "band", second))
+    return (lax.ppermute(one, "band", first), lax.ppermute(two, "band", second))
 
 
 def per_device(
@@ -786,13 +805,14 @@
     )(asked, flat, shapes)
     records, lists, base_rows = lax.optimization_barrier((records, lists, base_rows))
     received = exchanged(records)
-    pred, sent, compact, table, alpha, weight = pl.pallas_call(
+    pred, sent_one, sent_two, compact, table, alpha, weight = pl.pallas_call(
         render_kernel,
         in_specs=[spec(SMEM)] * 4 + [spec(VMEM)] * 2,
-        out_specs=[spec(VMEM)] * 6,
+        out_specs=[spec(VMEM)] * 7,
         out_shape=[
             shaped(3, ROWS, COLS),
-            shaped(2, 6, HALO, COLS),
+            shaped(6, HALO, COLS),
+            shaped(6, HALO, COLS),
             shaped(9, TILES, GAUSS),
             shaped(9, GAUSS, COLS),
             shaped(GAUSS, ROWS, COLS),
@@ -801,7 +821,7 @@
         compiler_params=params(16),
         name="render",
     )(block_list, tile_start, tile_end, base, received, target_band)
-    pred_one, pred_two = swapped(sent)
+    pred_one, pred_two = swapped(sent_one, sent_two)
     seg = (np.arange(COLS)[None, :] // TILE == np.arange(TILES)[:, None]).astype(np.float32)
     outgoing = pl.pallas_call(
         backward_kernel,

time: 99.4 us -> 98.7 us (level)
  starting transfers between devices: 14.1 us -> 12.8 us
    ppermute x2, starting transfers between devices: 2.55 us -> 1.28 us  [swapped(): return (lax.ppermute(one, 'band', first), lax.ppermute(two, 'band', second))]
where the time goes in v6:
time: 98.7 us; the launch traced here: 98.2 us
  blocking collectives  54.2 us (55%)
  Pallas kernels  18.6 us (19%)
  starting transfers between devices  12.8 us (13%)
  waiting for transfers between devices  9.14 us (9%)
  local copies, waits for them, and re-layouts  2.11 us (2%)
  between operations  1.43 us (1%)
    all_to_all x2, blocking collectives, exchanged(): return lax.all_to_all(slots, AXES, split_axis=0, concat_axis=0, tiled=True)  54.2 us
    all_to_all x1, starting transfers between devices, exchanged(): return lax.all_to_all(slots, AXES, split_axis=0, concat_axis=0, tiled=True)  11.5 us
    all_to_all x1, waiting for transfers between devices, exchanged(): return lax.all_to_all(slots, AXES, split_axis=0, concat_axis=0, tiled=True)  7.41 us
    pallas_call x1, Pallas kernels, per_device(): pl.pallas_call(backward_kernel, in_specs=[spec(VMEM)] * 12, out_specs=spe...  6.46 us
    pallas_call x1, Pallas kernels, per_device(): pl.pallas_call(update_kernel, in_specs=[spec(VMEM)] * 6, out_specs=[spec(...  4.69 us
    pallas_call x1, Pallas kernels, per_device(): pl.pallas_call(render_kernel, in_specs=[spec(SMEM)] * 4 + [spec(VMEM)] *...  3.84 us
  transfers between devices with their start and end apart: 3, of which 2 were waited for; matrix products, arithmetic and copies ran while one was open for 1% of the time, Pallas kernels for 0%

profile of v6, /device:TPU:1, one launch (start us, length us, event | category | flops | bytes accessed | tf_op | source)
XLA Modules:
  0.0 98.2 jit_solution(13037864183583320324)
XLA Ops:
  1.3 1.7 %request.1 = f32[128,1,128]{2,1,0:T(1,128)} custom-call(s32[1,1,16]{2,1,0:T(1,128)} %list_ref.3, s32[1,1]{1,0:T(1,128)} %copy.16.count_ref, f32[1,9]{1,0:T(1,128)} %cam_ref.1), custom_call_target="tpu_custom_call" | custom-call | tf_op jit(solution)/shard_map/request/pallas_call | solution.py:775
  2.9 11.5 %all-to-all-start = ((f32[128,1,128]{2,1,0:T(1,128)}), f32[128,1,128]{2,1,0:T(1,128)S(1)}, u32[]{:S(2)}, u32[]{:S(2)}) async-start(f32[128,1,128]{2,1,0:T(1,128)} %request.1), calls=%async_computation | async-start | bytes 131072 | tf_op jit(solution)/shard_map/all_to_all | solution.py:744
  14.4 0.0 copy-start
  14.4 1.2 %copy-done = f32[16,62,256]{2,0,1:T(8,128)S(1)} copy-done((f32[16,62,256]{2,0,1:T(8,128)S(1)}, f32[16,62,256]{2,0,1:T(8,128)}, u32[]{:S(2)}) %copy-start) | copy-done | bytes 1015832
  15.7 0.0 copy-start.1
  15.7 0.1 shapes.1
  15.7 0.8 concatenate.3
  16.6 7.4 %all-to-all-done.ask_ref = f32[128,1,128]{2,1,0:T(1,128)S(1)} async-done(((f32[128,1,128]{2,1,0:T(1,128)}), f32[128,1,128]{2,1,0:T(1,128)S(1)}, u32[]{:S(2)}, u32[]{:S(2)}) %all-to-all-start) | async-done | bytes 65568 | tf_op jit(solution)/shard_map/all_to_all | solution.py:744
  24.0 0.0 copy-done.1
  24.0 1.8 %records.1 = (f32[128,1,2304]{2,1,0:T(1,128)S(1)}, f32[32,128]{1,0:T(8,128)S(1)}) custom-call(f32[128,1,128]{2,1,0:T(1,128)S(1)} %all-to-all-done.ask_ref, f32[62,16,256]{2,1,0:T(8,128)S(1)} %bitcast.18, f32[7,16,256]{2,1,0:T(8,128)S(1)} %get-tuple-element.30.shape_ref), custom_call_target="tpu_custom_call" | custom-call | tf_op jit(solution)/shard_map/records/pallas_call | solution.py:793
  25.8 0.0 copy-start.4
  25.9 0.0 copy-start.6
  25.9 0.0 copy-start.8
  25.9 0.0 copy-start.9
  25.9 0.0 copy-start.5
  25.9 0.0 copy-start.7
  25.9 24.8 %all_to_all.15.got_ref = f32[128,1,2304]{2,1,0:T(1,128)S(1)} all-to-all(f32[128,1,2304]{2,1,0:T(1,128)S(1)} %get-tuple-element.36), channel_id=1, replica_groups=mesh['view'=32,'band'=4] {'view','band'}, dimensions={0} | all-to-all | bytes 2359296 | tf_op jit(solution)/shard_map/all_to_all | solution.py:744
  50.8 0.0 copy-done.4
  50.8 0.0 copy-done.6
  50.8 0.0 copy-done.8
  50.8 0.0 copy-done.9
  50.8 3.8 %render.1 = (f32[3,16,128]{2,1,0:T(8,128)S(1)}, f32[6,10,128]{2,1,0:T(8,128)S(1)}, f32[6,10,128]{2,1,0:T(8,128)S(1)}, f32[9,8,512]{2,1,0:T(8,128)S(1)}, f32[9,51...) custom-call(s32[1,1,16]{2,1,0:T(1,128)S(1)} %copy-done.6, s32[1,1,8]{2,1,0:T(1,128)S(1)} %copy-done.8, ...), custom_call_target="tpu_custom_call" | custom-call | tf_op jit(solution)/shard_map/render/pallas_call | solution.py:808
  54.6 0.6 collective-permute-start
  55.3 0.7 collective-permute-start.1
  55.9 1.7 %collective-permute-done.one_ref = f32[6,10,128]{2,1,0:T(8,128)S(1)} collective-permute-done((f32[6,10,128]{2,1,0:T(8,128)S(1)}, f32[6,10,128]{2,1,0:T(8,128)S(1)}, u32[]{:S(2)}, u32[]{:S(2)}) %collective-permute-start) | collective-permute-done | bytes 30752 | tf_op jit(solution)/shard_map/ppermute | solution.py:750
  57.7 0.0 collective-permute-done.1.two_ref
  57.7 0.0 copy-done.5
  57.7 0.0 copy-done.7
  57.7 6.5 %backward.1 = f32[128,1,2432]{2,1,0:T(1,128)S(1)} custom-call(s32[1,128]{1,0:T(1,128)S(1)} %bitcast.27, s32[8,128]{1,0:T(8,128)S(1)} %broadcast_in_dim.9.base_ref, f32[3,16,128]{2,1,0:T(8,128)S(1)} %get-tuple-element.37.pred_ref, f32[6,10,128]{2,1,0:T(8,128)S(1)} %collective-permute-done.one_ref, f32[6,10,128]{2,1,0:T(8,128)S(1)} %collective-permute-done.1.two_ref, ...), custom_call_target="tpu_custom_call" | custom-call | tf_op jit(solution)/shard_map/backward/pallas_call | solution.py:826
  64.1 0.0 copy-start.2
  64.2 0.0 copy-start.3
  64.2 29.3 %all_to_all.16.got_ref = f32[128,1,2432]{2,1,0:T(1,128)S(1)} all-to-all(f32[128,1,2432]{2,1,0:T(1,128)S(1)} %backward.1), channel_id=1, replica_groups=mesh['view'=32,'band'=4] {'view','band'}, dimensions={0} | all-to-all | bytes 2490368 | tf_op jit(solution)/shard_map/all_to_all | solution.py:744
  93.5 0.0 copy-done.2
  93.5 0.0 copy-done.3
  93.5 4.7 %update.1 = (f32[1,128]{1,0:T(1,128)}, f32[62,16,256]{2,1,0:T(8,128)}, f32[62,16,256]{2,1,0:T(8,128)}, f32[62,16,256]{2,1,0:T(8,128)}, f32[62,16,256]{2,1,0:T(8,128)}) custom-call(f32[32,128]{1,0:T(8,128)S(1)} %get-tuple-element.31.turned_ref, f32[18,16,256]{2,1,0:T(8,128)S(1)} %get-tuple-element.32.kept_ref, f32[62,16,256]{2,1,0:T(8,128)S(1)} %bitcast.19, ...), custom_call_target="tpu_custom_call" | custom-call | tf_op jit(solution)/shard_map/update/pallas_call | solution.py:857
  (2 shorter events, 0.0 us)
Async XLA Ops:
  2.9 21.0 %all-to-all-start = ((f32[128,1,128]{2,1,0:T(1,128)}), f32[128,1,128]{2,1,0:T(1,128)S(1)}, u32[]{:S(2)}, u32[]{:S(2)}) async-start(f32[128,1,128]{2,1,0:T(1,128)} %request.1), calls=%async_computation | async-start | bytes 131072 | tf_op jit(solution)/shard_map/all_to_all | solution.py:744
  14.4 1.2 %copy-start = (f32[16,62,256]{2,0,1:T(8,128)S(1)}, f32[16,62,256]{2,0,1:T(8,128)}, u32[]{:S(2)}) copy-start(f32[16,62,256]{2,0,1:T(8,128)} %param.11) | copy-start | bytes 3047428
  15.7 8.3 %copy-start.1 = (f32[16,62,256]{2,0,1:T(8,128)S(1)}, f32[16,62,256]{2,0,1:T(8,128)}, u32[]{:S(2)}) copy-start(f32[16,62,256]{2,0,1:T(8,128)} %param.11) | copy-start | bytes 3047428
  25.8 24.9 %copy-start.4 = (f32[1,3,16,128]{3,2,1,0:T(8,128)S(1)}, f32[1,3,16,128]{3,2,1,0:T(8,128)}, u32[]{:S(2)}) copy-start(f32[1,3,16,128]{3,2,1,0:T(8,128)} %param.15) | copy-start | bytes 73732
  25.9 24.9 %copy-start.6 = (s32[1,1,16]{2,1,0:T(1,128)S(1)}, s32[1,1,16]{2,1,0:T(1,128)}, u32[]{:S(2)}) copy-start(s32[1,1,16]{2,1,0:T(1,128)} %list_ref.3) | copy-start | bytes 196
  25.9 24.9 %copy-start.8 = (s32[1,1,8]{2,1,0:T(1,128)S(1)}, s32[1,1,8]{2,1,0:T(1,128)}, u32[]{:S(2)}) copy-start(s32[1,1,8]{2,1,0:T(1,128)} %start_ref.1) | copy-start | bytes 100
  25.9 24.9 %copy-start.9 = (s32[1,1,8]{2,1,0:T(1,128)S(1)}, s32[1,1,8]{2,1,0:T(1,128)}, u32[]{:S(2)}) copy-start(s32[1,1,8]{2,1,0:T(1,128)} %end_ref.1) | copy-start | bytes 100
  25.9 31.8 %copy-start.5 = (f32[128,128]{1,0:T(8,128)S(1)}, f32[128,128]{1,0:T(8,128)}, u32[]{:S(2)}) copy-start(f32[128,128]{1,0:T(8,128)} %constant.12.clone.across_ref) | copy-start | bytes 196612
  25.9 31.7 %copy-start.7 = (f32[8,128]{1,0:T(8,128)S(1)}, f32[8,128]{1,0:T(8,128)}, u32[]{:S(2)}) copy-start(f32[8,128]{1,0:T(8,128)} %constant.13.clone.seg_ref) | copy-start | bytes 12292
  54.6 3.0 %collective-permute-start = (f32[6,10,128]{2,1,0:T(8,128)S(1)}, f32[6,10,128]{2,1,0:T(8,128)S(1)}, u32[]{:S(2)}, u32[]{:S(2)}) collective-permute-start(f32[6,10,128]{2,1,0:T(8,128)S(1)} %get-tuple-element.38), channel_id=1, source_target_pairs={{0,1},{1,0},{2,3},{3,2},{4,5},{5,4},{6,7},{7,6},{8,9},{9,8},{10,11... | collective-permute-start | bytes 92168 | tf_op jit(solution)/shard_map/ppermute | solution.py:750
  55.3 2.4 %collective-permute-start.1 = (f32[6,10,128]{2,1,0:T(8,128)S(1)}, f32[6,10,128]{2,1,0:T(8,128)S(1)}, u32[]{:S(2)}, u32[]{:S(2)}) collective-permute-start(f32[6,10,128]{2,1,0:T(8,128)S(1)} %get-tuple-element.39), channel_id=1, source_target_pairs={{1,2},{2,1},{5,6},{6,5},{9,10},{10,9},{13,14},{14,13},{17,18},{18,... | collective-permute-start | bytes 92168 | tf_op jit(solution)/shard_map/ppermute | solution.py:750
  64.1 29.4 %copy-start.2 = (f32[16,62,256]{2,0,1:T(8,128)S(1)}, f32[16,62,256]{2,0,1:T(8,128)}, u32[]{:S(2)}) copy-start(f32[16,62,256]{2,0,1:T(8,128)} %param.12) | copy-start | bytes 3047428
  64.2 29.4 %copy-start.3 = (f32[16,62,256]{2,0,1:T(8,128)S(1)}, f32[16,62,256]{2,0,1:T(8,128)}, u32[]{:S(2)}) copy-start(f32[16,62,256]{2,0,1:T(8,128)} %param.13) | copy-start | bytes 3047428

commit v7 on v6

--- a/solution.py
+++ b/solution.py
@@ -688,7 +688,7 @@
         return carry
 
     each_listed(slot, count)
-    for low, high in ((14, 30), (30, 46), (46, COMPS)):
+    for low, high in ((14, 18), (18, 26), (26, 44), (44, COMPS)):
         finish(low, high)
     squares = [kept_ref[c] for c in range(3)]
     rot = [[kept_ref[3 + 3 * i + c] for c in range(3)] for i in range(3)]
@@ -865,7 +865,7 @@
             SMEM((WORDS, DEVICES), jnp.float32),
             SMEM((DEVICES + 1,), jnp.int32),
             pltpu.SemaphoreType.DMA,
-            pltpu.SemaphoreType.DMA((16,)),
+            pltpu.SemaphoreType.DMA((20,)),
         ],
         compiler_params=params(16),
         name="update",

time: 98.7 us -> 98.5 us (level)
  no operation moved by 1% of the time
where the time goes in v7:
time: 98.5 us; the launch traced here: 98 us
  blocking collectives  54.2 us (55%)
  Pallas kernels  18.3 us (19%)
  starting transfers between devices  12.8 us (13%)
  waiting for transfers between devices  9.14 us (9%)
  local copies, waits for them, and re-layouts  2.11 us (2%)
  between operations  1.43 us (1%)
    all_to_all x2, blocking collectives, exchanged(): return lax.all_to_all(slots, AXES, split_axis=0, concat_axis=0, tiled=True)  54.2 us
    all_to_all x1, starting transfers between devices, exchanged(): return lax.all_to_all(slots, AXES, split_axis=0, concat_axis=0, tiled=True)  11.5 us
    all_to_all x1, waiting for transfers between devices, exchanged(): return lax.all_to_all(slots, AXES, split_axis=0, concat_axis=0, tiled=True)  7.41 us
    pallas_call x1, Pallas kernels, per_device(): pl.pallas_call(backward_kernel, in_specs=[spec(VMEM)] * 12, out_specs=spe...  6.45 us
    pallas_call x1, Pallas kernels, per_device(): pl.pallas_call(update_kernel, in_specs=[spec(VMEM)] * 6, out_specs=[spec(...  4.52 us
    pallas_call x1, Pallas kernels, per_device(): pl.pallas_call(render_kernel, in_specs=[spec(SMEM)] * 4 + [spec(VMEM)] *...  3.84 us
  transfers between devices with their start and end apart: 3, of which 2 were waited for; matrix products, arithmetic and copies ran while one was open for 1% of the time, Pallas kernels for 0%

profile of v7, /device:TPU:1, one launch (start us, length us, event | category | flops | bytes accessed | tf_op | source)
XLA Modules:
  0.0 98.0 jit_solution(2167160545918286059)
XLA Ops:
  1.3 1.7 %request.1 = f32[128,1,128]{2,1,0:T(1,128)} custom-call(s32[1,1,16]{2,1,0:T(1,128)} %list_ref.3, s32[1,1]{1,0:T(1,128)} %copy.16.count_ref, f32[1,9]{1,0:T(1,128)} %cam_ref.1), custom_call_target="tpu_custom_call" | custom-call | tf_op jit(solution)/shard_map/request/pallas_call | solution.py:775
  2.9 11.5 %all-to-all-start = ((f32[128,1,128]{2,1,0:T(1,128)}), f32[128,1,128]{2,1,0:T(1,128)S(1)}, u32[]{:S(2)}, u32[]{:S(2)}) async-start(f32[128,1,128]{2,1,0:T(1,128)} %request.1), calls=%async_computation | async-start | bytes 131072 | tf_op jit(solution)/shard_map/all_to_all | solution.py:744
  14.4 0.0 copy-start
  14.5 1.2 %copy-done = f32[16,62,256]{2,0,1:T(8,128)S(1)} copy-done((f32[16,62,256]{2,0,1:T(8,128)S(1)}, f32[16,62,256]{2,0,1:T(8,128)}, u32[]{:S(2)}) %copy-start) | copy-done | bytes 1015832
  15.7 0.0 copy-start.1
  15.7 0.1 shapes.1
  15.7 0.8 concatenate.3
  16.6 7.4 %all-to-all-done.ask_ref = f32[128,1,128]{2,1,0:T(1,128)S(1)} async-done(((f32[128,1,128]{2,1,0:T(1,128)}), f32[128,1,128]{2,1,0:T(1,128)S(1)}, u32[]{:S(2)}, u32[]{:S(2)}) %all-to-all-start) | async-done | bytes 65568 | tf_op jit(solution)/shard_map/all_to_all | solution.py:744
  24.0 0.0 copy-done.1
  24.0 1.8 %records.1 = (f32[128,1,2304]{2,1,0:T(1,128)S(1)}, f32[32,128]{1,0:T(8,128)S(1)}) custom-call(f32[128,1,128]{2,1,0:T(1,128)S(1)} %all-to-all-done.ask_ref, f32[62,16,256]{2,1,0:T(8,128)S(1)} %bitcast.18, f32[7,16,256]{2,1,0:T(8,128)S(1)} %get-tuple-element.30.shape_ref), custom_call_target="tpu_custom_call" | custom-call | tf_op jit(solution)/shard_map/records/pallas_call | solution.py:793
  25.8 0.0 copy-start.4
  25.8 0.0 copy-start.6
  25.8 0.0 copy-start.8
  25.8 0.0 copy-start.9
  25.8 0.0 copy-start.5
  25.8 0.0 copy-start.7
  25.9 24.9 %all_to_all.15.got_ref = f32[128,1,2304]{2,1,0:T(1,128)S(1)} all-to-all(f32[128,1,2304]{2,1,0:T(1,128)S(1)} %get-tuple-element.36), channel_id=1, replica_groups=mesh['view'=32,'band'=4] {'view','band'}, dimensions={0} | all-to-all | bytes 2359296 | tf_op jit(solution)/shard_map/all_to_all | solution.py:744
  50.8 0.0 copy-done.4
  50.8 0.0 copy-done.6
  50.8 0.0 copy-done.8
  50.8 0.0 copy-done.9
  50.8 3.8 %render.1 = (f32[3,16,128]{2,1,0:T(8,128)S(1)}, f32[6,10,128]{2,1,0:T(8,128)S(1)}, f32[6,10,128]{2,1,0:T(8,128)S(1)}, f32[9,8,512]{2,1,0:T(8,128)S(1)}, f32[9,51...) custom-call(s32[1,1,16]{2,1,0:T(1,128)S(1)} %copy-done.6, s32[1,1,8]{2,1,0:T(1,128)S(1)} %copy-done.8, ...), custom_call_target="tpu_custom_call" | custom-call | tf_op jit(solution)/shard_map/render/pallas_call | solution.py:808
  54.7 0.6 collective-permute-start
  55.3 0.7 collective-permute-start.1
  55.9 1.7 %collective-permute-done.one_ref = f32[6,10,128]{2,1,0:T(8,128)S(1)} collective-permute-done((f32[6,10,128]{2,1,0:T(8,128)S(1)}, f32[6,10,128]{2,1,0:T(8,128)S(1)}, u32[]{:S(2)}, u32[]{:S(2)}) %collective-permute-start) | collective-permute-done | bytes 30752 | tf_op jit(solution)/shard_map/ppermute | solution.py:750
  57.7 0.0 collective-permute-done.1.two_ref
  57.7 0.0 copy-done.5
  57.7 0.0 copy-done.7
  57.7 6.4 %backward.1 = f32[128,1,2432]{2,1,0:T(1,128)S(1)} custom-call(s32[1,128]{1,0:T(1,128)S(1)} %bitcast.27, s32[8,128]{1,0:T(8,128)S(1)} %broadcast_in_dim.9.base_ref, f32[3,16,128]{2,1,0:T(8,128)S(1)} %get-tuple-element.37.pred_ref, f32[6,10,128]{2,1,0:T(8,128)S(1)} %collective-permute-done.one_ref, f32[6,10,128]{2,1,0:T(8,128)S(1)} %collective-permute-done.1.two_ref, ...), custom_call_target="tpu_custom_call" | custom-call | tf_op jit(solution)/shard_map/backward/pallas_call | solution.py:826
  64.1 0.0 copy-start.2
  64.1 0.0 copy-start.3
  64.2 29.3 %all_to_all.16.got_ref = f32[128,1,2432]{2,1,0:T(1,128)S(1)} all-to-all(f32[128,1,2432]{2,1,0:T(1,128)S(1)} %backward.1), channel_id=1, replica_groups=mesh['view'=32,'band'=4] {'view','band'}, dimensions={0} | all-to-all | bytes 2490368 | tf_op jit(solution)/shard_map/all_to_all | solution.py:744
  93.5 0.0 copy-done.2
  93.5 0.0 copy-done.3
  93.5 4.5 %update.1 = (f32[1,128]{1,0:T(1,128)}, f32[62,16,256]{2,1,0:T(8,128)}, f32[62,16,256]{2,1,0:T(8,128)}, f32[62,16,256]{2,1,0:T(8,128)}, f32[62,16,256]{2,1,0:T(8,128)}) custom-call(f32[32,128]{1,0:T(8,128)S(1)} %get-tuple-element.31.turned_ref, f32[18,16,256]{2,1,0:T(8,128)S(1)} %get-tuple-element.32.kept_ref, f32[62,16,256]{2,1,0:T(8,128)S(1)} %bitcast.19, ...), custom_call_target="tpu_custom_call" | custom-call | tf_op jit(solution)/shard_map/update/pallas_call | solution.py:857
  (2 shorter events, 0.0 us)
Async XLA Ops:
  2.9 21.1 %all-to-all-start = ((f32[128,1,128]{2,1,0:T(1,128)}), f32[128,1,128]{2,1,0:T(1,128)S(1)}, u32[]{:S(2)}, u32[]{:S(2)}) async-start(f32[128,1,128]{2,1,0:T(1,128)} %request.1), calls=%async_computation | async-start | bytes 131072 | tf_op jit(solution)/shard_map/all_to_all | solution.py:744
  14.4 1.2 %copy-start = (f32[16,62,256]{2,0,1:T(8,128)S(1)}, f32[16,62,256]{2,0,1:T(8,128)}, u32[]{:S(2)}) copy-start(f32[16,62,256]{2,0,1:T(8,128)} %param.11) | copy-start | bytes 3047428
  15.7 8.3 %copy-start.1 = (f32[16,62,256]{2,0,1:T(8,128)S(1)}, f32[16,62,256]{2,0,1:T(8,128)}, u32[]{:S(2)}) copy-start(f32[16,62,256]{2,0,1:T(8,128)} %param.11) | copy-start | bytes 3047428
  25.8 25.0 %copy-start.4 = (f32[1,3,16,128]{3,2,1,0:T(8,128)S(1)}, f32[1,3,16,128]{3,2,1,0:T(8,128)}, u32[]{:S(2)}) copy-start(f32[1,3,16,128]{3,2,1,0:T(8,128)} %param.15) | copy-start | bytes 73732
  25.8 25.0 %copy-start.6 = (s32[1,1,16]{2,1,0:T(1,128)S(1)}, s32[1,1,16]{2,1,0:T(1,128)}, u32[]{:S(2)}) copy-start(s32[1,1,16]{2,1,0:T(1,128)} %list_ref.3) | copy-start | bytes 196
  25.8 25.0 %copy-start.8 = (s32[1,1,8]{2,1,0:T(1,128)S(1)}, s32[1,1,8]{2,1,0:T(1,128)}, u32[]{:S(2)}) copy-start(s32[1,1,8]{2,1,0:T(1,128)} %start_ref.1) | copy-start | bytes 100
  25.8 25.0 %copy-start.9 = (s32[1,1,8]{2,1,0:T(1,128)S(1)}, s32[1,1,8]{2,1,0:T(1,128)}, u32[]{:S(2)}) copy-start(s32[1,1,8]{2,1,0:T(1,128)} %end_ref.1) | copy-start | bytes 100
  25.8 31.8 %copy-start.5 = (f32[128,128]{1,0:T(8,128)S(1)}, f32[128,128]{1,0:T(8,128)}, u32[]{:S(2)}) copy-start(f32[128,128]{1,0:T(8,128)} %constant.12.clone.across_ref) | copy-start | bytes 196612
  25.8 31.8 %copy-start.7 = (f32[8,128]{1,0:T(8,128)S(1)}, f32[8,128]{1,0:T(8,128)}, u32[]{:S(2)}) copy-start(f32[8,128]{1,0:T(8,128)} %constant.13.clone.seg_ref) | copy-start | bytes 12292
  54.7 3.0 %collective-permute-start = (f32[6,10,128]{2,1,0:T(8,128)S(1)}, f32[6,10,128]{2,1,0:T(8,128)S(1)}, u32[]{:S(2)}, u32[]{:S(2)}) collective-permute-start(f32[6,10,128]{2,1,0:T(8,128)S(1)} %get-tuple-element.38), channel_id=1, source_target_pairs={{0,1},{1,0},{2,3},{3,2},{4,5},{5,4},{6,7},{7,6},{8,9},{9,8},{10,11... | collective-permute-start | bytes 92168 | tf_op jit(solution)/shard_map/ppermute | solution.py:750
  55.3 2.4 %collective-permute-start.1 = (f32[6,10,128]{2,1,0:T(8,128)S(1)}, f32[6,10,128]{2,1,0:T(8,128)S(1)}, u32[]{:S(2)}, u32[]{:S(2)}) collective-permute-start(f32[6,10,128]{2,1,0:T(8,128)S(1)} %get-tuple-element.39), channel_id=1, source_target_pairs={{1,2},{2,1},{5,6},{6,5},{9,10},{10,9},{13,14},{14,13},{17,18},{18,... | collective-permute-start | bytes 92168 | tf_op jit(solution)/shard_map/ppermute | solution.py:750
  64.1 29.3 %copy-start.2 = (f32[16,62,256]{2,0,1:T(8,128)S(1)}, f32[16,62,256]{2,0,1:T(8,128)}, u32[]{:S(2)}) copy-start(f32[16,62,256]{2,0,1:T(8,128)} %param.12) | copy-start | bytes 3047428
  64.1 29.3 %copy-start.3 = (f32[16,62,256]{2,0,1:T(8,128)S(1)}, f32[16,62,256]{2,0,1:T(8,128)}, u32[]{:S(2)}) copy-start(f32[16,62,256]{2,0,1:T(8,128)} %param.13) | copy-start | bytes 3047428
